TPU v7x, 32 devices: a whole 2x2x4 slice. The times are simulated.
32 devices in a mesh: ctx: 4 (over x, core), shard: 8 (over z, y).
Axes of the slice: x: 2, y: 2, z: 4, core: 2. Of those that a mesh axis runs over, the one named last changes fastest.
Arguments:
- tokens: bfloat16 [8, 1024, 2048], P('shard', 'ctx'), may hold values from -6 to 6
- target: bfloat16 [8, 1024, 2048], P('shard', 'ctx'), may hold values from -6 to 6
- routes: int32 [8, 1024, 6], P('shard', 'ctx'), may hold values from 0 to 15, all different within a row; in each aligned block of 256 rows (0 to 255, 256 to 511, ..., all dimensions but the last counted through in order) at most 128 rows name the same one
- attn_gain: bfloat16 [2048], P('shard'), may hold values from 0.5 to 1.5
- w_query: bfloat16 [2048, 3072], P('shard'), may hold values from -0.125 to 0.125
- w_latent_in: bfloat16 [2048, 576], P('shard'), may hold values from -0.125 to 0.125
- latent_gain: bfloat16 [512], P('shard'), may hold values from 0.5 to 1.5
- w_latent_out: bfloat16 [512, 4096], P('shard'), may hold values from -0.25 to 0.25
- w_attn_out: bfloat16 [2048, 2048], P('shard'), may hold values from -2 to 2
- ffn_gain: bfloat16 [2048], P('shard'), may hold values from 0.5 to 1.5
- w_router: bfloat16 [2048, 16], P('shard'), may hold values from -0.0625 to 0.0625
- shared_gate: bfloat16 [2048, 2816], P('shard'), may hold values from -0.125 to 0.125
- shared_up: bfloat16 [2048, 2816], P('shard'), may hold values from -0.125 to 0.125
- shared_down: bfloat16 [2816, 2048], P('shard'), may hold values from -0.109375 to 0.109375
- expert_gate: bfloat16 [32, 2048, 704], P(('ctx', 'shard')), may hold values from -0.125 to 0.125
- expert_up: bfloat16 [32, 2048, 704], P(('ctx', 'shard')), may hold values from -0.125 to 0.125
- expert_down: bfloat16 [32, 704, 2048], P(('ctx', 'shard')), may hold values from -1.25 to 1.25
Outputs:
- layer_out: bfloat16 [8, 1024, 2048], P('shard', 'ctx')
- loss: float32 [], replicated
- token_grad: float32 [8, 1024, 2048], P('shard', 'ctx')
- attn_gain_grad: float32 [2048], P(('ctx', 'shard'))
- query_grad: float32 [2048, 3072], P(('ctx', 'shard'))
- latent_in_grad: float32 [2048, 576], P(('ctx', 'shard'))
- latent_gain_grad: float32 [512], P(('ctx', 'shard'))
- latent_out_grad: float32 [512, 4096], P(('ctx', 'shard'))
- attn_out_grad: float32 [2048, 2048], P(('ctx', 'shard'))
- ffn_gain_grad: float32 [2048], P(('ctx', 'shard'))
- router_grad: float32 [2048, 16], P(('ctx', 'shard'))
- shared_gate_grad: float32 [2048, 2816], P(('ctx', 'shard'))
- shared_up_grad: float32 [2048, 2816], P(('ctx', 'shard'))
- shared_down_grad: float32 [2816, 2048], P(('ctx', 'shard'))
- expert_gate_grad: float32 [32, 2048, 704], P(('ctx', 'shard'))
- expert_up_grad: float32 [32, 2048, 704], P(('ctx', 'shard'))
- expert_down_grad: float32 [32, 704, 2048], P(('ctx', 'shard'))
Inputs may be any that keep to these rules, and one draw needn't show every extreme that they name: `routes`: each token names 6 different experts; among the 256 tokens of one device no expert is named more than 128 times, a bound that some block reaches.
All inputs are finite; a program needn't handle non-finite values.
Results may differ from a plain program's by a relative error of at most 0.014.
Values may be sent and summed in bfloat16 or wider, within the bound.
No kernel may reach another device: no remote copies, remote signals or barrier semaphores. Data moves between devices by JAX's collectives and lax.ppermute only.
A program may use at most 448 MiB of HBM per device.

v0:
```python
import jax
import jax.numpy as jnp
from jax import lax
from jax.sharding import PartitionSpec as P

H = 16
DN = 128
DR = 64
DV = 128
LAT = 512
TOP = 6
BLOCK = 256


epsilon = 1e-06
base_freq = 10000.0
highest = lax.Precision.HIGHEST


def tables(position, width):
    half = width // 2
    freqs = base_freq ** (-jnp.arange(half, dtype=jnp.float32) / half)
    angle = position.astype(jnp.float32)[:, None] * freqs[None, :]
    return (jnp.cos(angle), jnp.sin(angle))


def rotate(values, cosine, sine):
    half = values.shape[-1] // 2
    first = values[..., :half]
    second = values[..., half:]
    return jnp.concatenate([first * cosine - second * sine, second * cosine + first * sine], -1)


def rotate_back(grads, cosine, sine):
    half = grads.shape[-1] // 2
    first = grads[..., :half]
    second = grads[..., half:]
    return jnp.concatenate([first * cosine + second * sine, second * cosine - first * sine], -1)


def inverse_root(values):
    return lax.rsqrt(jnp.mean(values * values, axis=-1, keepdims=True) + epsilon)


def norm_back(values, factor, gain, grads):
    scaled = grads * gain
    d_values = factor * scaled - values * factor**3 * jnp.mean(
        values * scaled, axis=-1, keepdims=True
    )
    return (d_values, jnp.sum(grads * values * factor, axis=0))


def silu_parts(values):
    sigma = jax.nn.sigmoid(values)
    return (values * sigma, sigma * (1.0 + values * (1.0 - sigma)))


def on_device(
    tokens,
    target,
    routes,
    attn_gain,
    w_query,
    w_latent_in,
    latent_gain,
    w_latent_out,
    w_attn_out,
    ffn_gain,
    w_router,
    shared_gate,
    shared_up,
    shared_down,
    expert_gate,
    expert_up,
    expert_down,
):
    rows = tokens.shape[1]
    width = tokens.shape[2]
    ctx_count = lax.axis_size("ctx")
    shard_count = lax.axis_size("shard")
    experts = ctx_count * shard_count // 2
    capacity = max(2, (rows * TOP * 4 + experts * 3 - 1) // (experts * 3))
    seq_len = rows * ctx_count
    scale = (DN + DR) ** (-0.5)
    (
        gain_attn,
        query_proj,
        latent_down,
        gain_latent,
        latent_up,
        out_proj,
        gain_ffn,
        router_proj,
        gate_proj,
        up_proj,
        down_proj,
    ) = (
        lax.all_gather(attn_gain, "shard", axis=0, tiled=True),
        lax.all_gather(w_query, "shard", axis=0, tiled=True),
        lax.all_gather(w_latent_in, "shard", axis=0, tiled=True),
        lax.all_gather(latent_gain, "shard", axis=0, tiled=True),
        lax.all_gather(w_latent_out, "shard", axis=0, tiled=True),
        lax.all_gather(w_attn_out, "shard", axis=0, tiled=True),
        lax.all_gather(ffn_gain, "shard", axis=0, tiled=True),
        lax.all_gather(w_router, "shard", axis=0, tiled=True),
        lax.all_gather(shared_gate, "shard", axis=0, tiled=True),
        lax.all_gather(shared_up, "shard", axis=0, tiled=True),
        lax.all_gather(shared_down, "shard", axis=0, tiled=True),
    )
    source = tokens[0].astype(jnp.float32)
    place = lax.axis_index("ctx") * rows + jnp.arange(rows)
    cosine, sine = tables(place, DR)
    factor_attn = inverse_root(source)
    attn_in = (source * factor_attn * gain_attn).astype(jnp.bfloat16)
    query_raw = jnp.dot(attn_in, query_proj, preferred_element_type=jnp.float32).reshape(
        rows, H, DN + DR
    )
    query = jnp.concatenate(
        [query_raw[..., :DN], rotate(query_raw[..., DN:], cosine[:, None, :], sine[:, None, :])], -1
    ).astype(jnp.bfloat16)
    latent_raw = jnp.dot(attn_in, latent_down, preferred_element_type=jnp.float32)
    latent_part = latent_raw[:, :LAT]
    factor_latent = inverse_root(latent_part)
    latent = (latent_part * factor_latent * gain_latent).astype(jnp.bfloat16)
    key_rope = rotate(latent_raw[:, LAT:], cosine, sine).astype(jnp.bfloat16)
    pairs_own = jnp.dot(latent, latent_up, preferred_element_type=jnp.float32).astype(jnp.bfloat16)
    pairs_all, rope_all = (
        lax.all_gather(pairs_own, "ctx", axis=0, tiled=True),
        lax.all_gather(key_rope, "ctx", axis=0, tiled=True),
    )
    pairs_all = pairs_all.reshape(seq_len, H, DN + DV)
    keys_all = pairs_all[..., :DN]
    values_all = pairs_all[..., DN:]
    scores = (
        jnp.einsum("qhd,khd->hqk", query[..., :DN], keys_all, preferred_element_type=jnp.float32)
        + jnp.einsum("qhd,kd->hqk", query[..., DN:], rope_all, preferred_element_type=jnp.float32)
    ) * scale
    key_place = jnp.arange(seq_len)
    visible = key_place[None, :] // BLOCK <= place[:, None] // BLOCK
    scores = jnp.where(visible[None], scores, -1e30)
    top_score = jnp.max(scores, axis=-1, keepdims=True)
    weights = jnp.exp(scores - top_score)
    probs = weights / jnp.sum(weights, axis=-1, keepdims=True)
    probs_low = probs.astype(jnp.bfloat16)
    heads_out = jnp.einsum(
        "hqk,khd->qhd", probs_low, values_all, preferred_element_type=jnp.float32
    )
    heads_low = heads_out.reshape(rows, H * DV).astype(jnp.bfloat16)
    middle = source + jnp.dot(heads_low, out_proj, preferred_element_type=jnp.float32)
    factor_ffn = inverse_root(middle)
    ffn_in = (middle * factor_ffn * gain_ffn).astype(jnp.bfloat16)
    logits = jnp.dot(ffn_in, router_proj, preferred_element_type=jnp.float32)
    router = jax.nn.softmax(logits, axis=-1)
    choose = routes[0]
    chosen = choose[:, :, None] == jnp.arange(experts, dtype=jnp.int32)[None, None, :]
    gates = jnp.sum(jnp.where(chosen, router[:, None, :], 0.0), axis=-1)
    shared_gate_val = jnp.dot(ffn_in, gate_proj, preferred_element_type=jnp.float32)
    shared_up_val = jnp.dot(ffn_in, up_proj, preferred_element_type=jnp.float32)
    shared_act, shared_slope = silu_parts(shared_gate_val)
    shared_hidden = (shared_act * shared_up_val).astype(jnp.bfloat16)
    shared_branch = jnp.dot(shared_hidden, down_proj, preferred_element_type=jnp.float32)
    hot = chosen.astype(jnp.int32).reshape(rows * TOP, experts)
    slots = jnp.sum(
        (jnp.cumsum(hot, axis=0, dtype=jnp.int32) - hot) * hot, axis=-1, dtype=jnp.int32
    ).reshape(rows, TOP)
    spread_rows = jnp.broadcast_to(ffn_in[:, None, :], (rows, TOP, width))
    outgoing = (
        jnp.zeros((experts, capacity, width), jnp.bfloat16).at[choose, slots].set(spread_rows)
    )
    outgoing = jnp.stack([outgoing, outgoing], 1).reshape(2 * experts, capacity, width)
    gate_half = expert_gate[0]
    up_half = expert_up[0]
    down_half = expert_down[0]
    arrived = lax.all_to_all(outgoing, ("ctx", "shard"), split_axis=0, concat_axis=0, tiled=True)
    gate_val = jnp.einsum("snd,df->snf", arrived, gate_half, preferred_element_type=jnp.float32)
    up_val = jnp.einsum("snd,df->snf", arrived, up_half, preferred_element_type=jnp.float32)
    hidden = (gate_val * jax.nn.sigmoid(gate_val) * up_val).astype(jnp.bfloat16)
    partial_out = jnp.einsum("snf,fd->snd", hidden, down_half, preferred_element_type=jnp.float32)
    returned = lax.all_to_all(
        partial_out.astype(jnp.bfloat16), ("ctx", "shard"), split_axis=0, concat_axis=0, tiled=True
    ).astype(partial_out.dtype)
    returned, arrived_rows, gate_vals, up_vals, hidden_rows = (
        returned,
        arrived,
        gate_val,
        up_val,
        hidden,
    )
    combined = jnp.sum(returned.reshape(experts, 2, capacity, width), axis=1)
    routed_rows = combined[choose, slots]
    routed = jnp.sum(gates[:, :, None] * routed_rows, axis=1)
    final = middle + shared_branch + routed
    error = final - target[0].astype(jnp.float32)
    loss = lax.psum(jnp.sum(error * error), ("ctx", "shard")) / (
        rows * ctx_count * shard_count * width
    )
    (
        gain_attn,
        query_proj,
        latent_down,
        gain_latent,
        latent_up,
        out_proj,
        gain_ffn,
        router_proj,
        gate_proj,
        up_proj,
        down_proj,
    ) = (
        lax.all_gather(attn_gain, "shard", axis=0, tiled=True),
        lax.all_gather(w_query, "shard", axis=0, tiled=True),
        lax.all_gather(w_latent_in, "shard", axis=0, tiled=True),
        lax.all_gather(latent_gain, "shard", axis=0, tiled=True),
        lax.all_gather(w_latent_out, "shard", axis=0, tiled=True),
        lax.all_gather(w_attn_out, "shard", axis=0, tiled=True),
        lax.all_gather(ffn_gain, "shard", axis=0, tiled=True),
        lax.all_gather(w_router, "shard", axis=0, tiled=True),
        lax.all_gather(shared_gate, "shard", axis=0, tiled=True),
        lax.all_gather(shared_up, "shard", axis=0, tiled=True),
        lax.all_gather(shared_down, "shard", axis=0, tiled=True),
    )
    d_gates = jnp.sum(routed_rows * error[:, None, :], axis=-1)
    d_routed = (gates[:, :, None] * error[:, None, :]).astype(jnp.bfloat16)
    incoming = jnp.zeros((experts, capacity, width), jnp.bfloat16).at[choose, slots].set(d_routed)
    incoming = jnp.stack([incoming, incoming], 1).reshape(2 * experts, capacity, width)
    d_arrived = lax.all_to_all(incoming, ("ctx", "shard"), split_axis=0, concat_axis=0, tiled=True)
    d_hidden = jnp.einsum("snd,fd->snf", d_arrived, down_half, preferred_element_type=jnp.float32)
    d_down_half = jnp.einsum(
        "snf,snd->fd", hidden_rows, d_arrived, preferred_element_type=jnp.float32
    )
    expert_act, expert_slope = silu_parts(gate_vals)
    d_gate_val = (d_hidden * up_vals * expert_slope).astype(jnp.bfloat16)
    d_up_val = (d_hidden * expert_act).astype(jnp.bfloat16)
    d_gate_half = jnp.einsum(
        "snd,snf->df", arrived_rows, d_gate_val, preferred_element_type=jnp.float32
    )
    d_up_half = jnp.einsum(
        "snd,snf->df", arrived_rows, d_up_val, preferred_element_type=jnp.float32
    )
    d_rows = jnp.einsum(
        "snf,df->snd", d_gate_val, gate_half, preferred_element_type=jnp.float32
    ) + jnp.einsum("snf,df->snd", d_up_val, up_half, preferred_element_type=jnp.float32)
    d_back = lax.all_to_all(
        d_rows.astype(jnp.bfloat16), ("ctx", "shard"), split_axis=0, concat_axis=0, tiled=True
    ).astype(d_rows.dtype)
    d_combined = jnp.sum(d_back.reshape(experts, 2, capacity, width), axis=1)
    d_ffn = jnp.sum(d_combined[choose, slots], axis=1)
    d_router = jnp.sum(jnp.where(chosen, d_gates[:, :, None], 0.0), axis=1)
    d_logits = (router * (d_router - jnp.sum(router * d_router, axis=-1, keepdims=True))).astype(
        jnp.bfloat16
    )
    d_shared_out = error.astype(jnp.bfloat16)
    d_down_proj = jnp.einsum(
        "tf,td->fd", shared_hidden, d_shared_out, preferred_element_type=jnp.float32
    )
    d_shared_hidden = jnp.einsum(
        "td,fd->tf", d_shared_out, down_proj, preferred_element_type=jnp.float32
    )
    d_shared_gate = (d_shared_hidden * shared_up_val * shared_slope).astype(jnp.bfloat16)
    d_shared_up = (d_shared_hidden * shared_act).astype(jnp.bfloat16)
    d_gate_proj = jnp.einsum("td,tf->df", ffn_in, d_shared_gate, preferred_element_type=jnp.float32)
    d_up_proj = jnp.einsum("td,tf->df", ffn_in, d_shared_up, preferred_element_type=jnp.float32)
    d_router_proj = jnp.einsum("td,te->de", ffn_in, d_logits, preferred_element_type=jnp.float32)
    d_ffn = (
        d_ffn
        + jnp.einsum("tf,df->td", d_shared_gate, gate_proj, preferred_element_type=jnp.float32)
        + jnp.einsum("tf,df->td", d_shared_up, up_proj, preferred_element_type=jnp.float32)
        + jnp.einsum("te,de->td", d_logits, router_proj, preferred_element_type=jnp.float32)
    )
    d_middle_norm, d_gain_ffn = norm_back(middle, factor_ffn, gain_ffn, d_ffn)
    d_middle = error + d_middle_norm
    d_branch = d_middle.astype(jnp.bfloat16)
    d_out_proj = jnp.einsum("tk,td->kd", heads_low, d_branch, preferred_element_type=jnp.float32)
    d_heads = jnp.einsum("td,kd->tk", d_branch, out_proj, preferred_element_type=jnp.float32)
    d_heads = d_heads.astype(jnp.bfloat16).reshape(rows, H, DV)
    d_values = jnp.einsum("hqk,qhd->khd", probs_low, d_heads, preferred_element_type=jnp.float32)
    d_probs = jnp.einsum("qhd,khd->hqk", d_heads, values_all, preferred_element_type=jnp.float32)
    d_scores = (probs * (d_probs - jnp.sum(probs * d_probs, axis=-1, keepdims=True))).astype(
        jnp.bfloat16
    )
    d_query_plain = (
        jnp.einsum("hqk,khd->qhd", d_scores, keys_all, preferred_element_type=jnp.float32) * scale
    )
    d_query_rope = (
        jnp.einsum("hqk,kd->qhd", d_scores, rope_all, preferred_element_type=jnp.float32) * scale
    )
    d_keys = (
        jnp.einsum("hqk,qhd->khd", d_scores, query[..., :DN], preferred_element_type=jnp.float32)
        * scale
    )
    d_key_rope = (
        jnp.einsum("hqk,qhd->kd", d_scores, query[..., DN:], preferred_element_type=jnp.float32)
        * scale
    )
    d_pairs_term = jnp.concatenate([d_keys, d_values], -1).reshape(seq_len, H * (DN + DV))
    up_wide = latent_up.astype(jnp.float32)
    d_pairs, d_rope = (
        lax.psum_scatter(
            d_pairs_term.astype(jnp.bfloat16), "ctx", scatter_dimension=0, tiled=True
        ).astype(jnp.float32),
        lax.psum_scatter(
            d_key_rope.astype(jnp.bfloat16), "ctx", scatter_dimension=0, tiled=True
        ).astype(jnp.float32),
    )
    d_latent_up = jnp.dot(
        latent.astype(jnp.float32).T, d_pairs, precision=highest, preferred_element_type=jnp.float32
    )
    d_latent = jnp.dot(d_pairs, up_wide.T, precision=highest, preferred_element_type=jnp.float32)
    d_latent_part, d_gain_latent = norm_back(latent_part, factor_latent, gain_latent, d_latent)
    d_latent_raw = jnp.concatenate([d_latent_part, rotate_back(d_rope, cosine, sine)], -1).astype(
        jnp.bfloat16
    )
    d_query_raw = (
        jnp.concatenate(
            [d_query_plain, rotate_back(d_query_rope, cosine[:, None, :], sine[:, None, :])], -1
        )
        .reshape(rows, H * (DN + DR))
        .astype(jnp.bfloat16)
    )
    d_query_proj = jnp.einsum("td,tk->dk", attn_in, d_query_raw, preferred_element_type=jnp.float32)
    d_latent_down = jnp.einsum(
        "td,tk->dk", attn_in, d_latent_raw, preferred_element_type=jnp.float32
    )
    d_attn_in = jnp.einsum(
        "tk,dk->td", d_query_raw, query_proj, preferred_element_type=jnp.float32
    ) + jnp.einsum("tk,dk->td", d_latent_raw, latent_down, preferred_element_type=jnp.float32)
    d_source_norm, d_gain_attn = norm_back(source, factor_attn, gain_attn, d_attn_in)
    token_grad = d_middle + d_source_norm
    (
        g_attn,
        g_query,
        g_latent_in,
        g_latent,
        g_latent_out,
        g_attn_out,
        g_ffn,
        g_router,
        g_gate,
        g_up,
        g_down,
    ) = (
        lax.psum_scatter(d_gain_attn, ("ctx", "shard"), scatter_dimension=0, tiled=True),
        lax.psum_scatter(d_query_proj, ("ctx", "shard"), scatter_dimension=0, tiled=True),
        lax.psum_scatter(d_latent_down, ("ctx", "shard"), scatter_dimension=0, tiled=True),
        lax.psum_scatter(d_gain_latent, ("ctx", "shard"), scatter_dimension=0, tiled=True),
        lax.psum_scatter(d_latent_up, ("ctx", "shard"), scatter_dimension=0, tiled=True),
        lax.psum_scatter(d_out_proj, ("ctx", "shard"), scatter_dimension=0, tiled=True),
        lax.psum_scatter(d_gain_ffn, ("ctx", "shard"), scatter_dimension=0, tiled=True),
        lax.psum_scatter(d_router_proj, ("ctx", "shard"), scatter_dimension=0, tiled=True),
        lax.psum_scatter(d_gate_proj, ("ctx", "shard"), scatter_dimension=0, tiled=True),
        lax.psum_scatter(d_up_proj, ("ctx", "shard"), scatter_dimension=0, tiled=True),
        lax.psum_scatter(d_down_proj, ("ctx", "shard"), scatter_dimension=0, tiled=True),
    )
    return (
        final.astype(jnp.bfloat16)[None],
        loss,
        token_grad[None],
        g_attn,
        g_query,
        g_latent_in,
        g_latent,
        g_latent_out,
        g_attn_out,
        g_ffn,
        g_router,
        g_gate,
        g_up,
        g_down,
        d_gate_half[None],
        d_up_half[None],
        d_down_half[None],
    )


def solution(mesh):
    in_specs = (
        P("shard", "ctx", None),
        P("shard", "ctx", None),
        P("shard", "ctx", None),
        P("shard"),
        P("shard", None),
        P("shard", None),
        P("shard"),
        P("shard", None),
        P("shard", None),
        P("shard"),
        P("shard", None),
        P("shard", None),
        P("shard", None),
        P("shard", None),
        P(("ctx", "shard"), None, None),
        P(("ctx", "shard"), None, None),
        P(("ctx", "shard"), None, None),
    )
    out_specs = (
        P("shard", "ctx", None),
        P(),
        P("shard", "ctx", None),
        P(("ctx", "shard")),
        P(("ctx", "shard"), None),
        P(("ctx", "shard"), None),
        P(("ctx", "shard")),
        P(("ctx", "shard"), None),
        P(("ctx", "shard"), None),
        P(("ctx", "shard")),
        P(("ctx", "shard"), None),
        P(("ctx", "shard"), None),
        P(("ctx", "shard"), None),
        P(("ctx", "shard"), None),
        P(("ctx", "shard"), None, None),
        P(("ctx", "shard"), None, None),
        P(("ctx", "shard"), None, None),
    )
    return jax.shard_map(
        on_device, mesh=mesh, in_specs=in_specs, out_specs=out_specs, check_vma=False
    )
```

profile of v0, /device:TPU:0, one launch (start us, length us, event | category | flops | bytes accessed | tf_op | source)
XLA Modules:
  0.0 5562.9 jit_solution(16051728437984108256)
XLA Ops:
  12.2 23.4 all-reduce
  70.2 70.1 %all-gather.13.cloned.1.call-done = bf16[512,4096]{1,0:T(8,128)(2,1)} async-done(((bf16[64,4096]{1,0:T(8,128)(2,1)}), bf16[512,4096]{1,0:T(8,128)(2,1)}) %all-gather.13.cloned.1.call-update) | async-done | bytes 4194320 | tf_op jit(solution)/shard_map/all_gather | solution.py:102
  149.4 17.8 all-gather.1
  226.5 154.7 %all-gather.17.cloned.1.call-done = bf16[2048,3072]{1,0:T(8,128)(2,1)} async-done(((bf16[256,3072]{1,0:T(8,128)(2,1)}), bf16[2048,3072]{1,0:T(8,128)(2,1)}) %all-gather.17.cloned.1.call-update) | async-done | bytes 12582928 | tf_op jit(solution)/shard_map/all_gather | solution.py:99
  381.2 16.5 copy.119
  413.2 18.5 fusion.2
  431.7 18.2 fusion.108
  449.9 16.6 fusion.50
  466.6 39.8 all-gather.19.cloned.1.call-done
  567.2 626.3 %all-to-all-done = bf16[32,128,2048]{2,1,0:T(8,128)(2,1)} async-done(((bf16[32,128,2048]{2,1,0:T(8,128)(2,1)}), bf16[32,128,2048]{2,1,0:T(8,128)(2,1)}, u32[]{:S(2)}, u32[]{:S(2)}) %all-to-all-start) | async-done | bytes 16777248 | tf_op jit(solution)/shard_map/all_to_all | solution.py:174
  1209.7 21.1 multiply_convert_fusion.4
  1255.9 522.9 %all_gather.62 = bf16[2048,16]{0,1:T(8,128)(2,1)S(1)} all-gather(bf16[256,16]{0,1:T(8,128)(2,1)S(1)} %copy-done.70), channel_id=1, replica_groups=mesh['ctx'=4,'shard'=8] {'shard'}, dimensions={0}, use_global_device_ids=true | all-gather | bytes 73728 | tf_op jit(solution)/shard_map/all_gather | solution.py:105
  1815.8 38.9 gather_fusion
  1932.5 367.0 %all_to_all.20 = bf16[32,128,2048]{2,1,0:T(8,128)(2,1)S(1)} all-to-all(bf16[32,128,2048]{2,1,0:T(8,128)(2,1)S(1)} %bitcast.219), channel_id=1, replica_groups=mesh['ctx'=4,'shard'=8] {'ctx','shard'}, dimensions={0} | all-to-all | bytes 33554432 | tf_op jit(solution)/shard_map/all_to_all | solution.py:226
  2299.6 25.6 multiply_convert_fusion.2
  2325.1 22.2 fusion.22
  2347.3 23.7 add_convert_fusion
  2386.7 363.3 %all-to-all-done.3 = bf16[32,128,2048]{2,1,0:T(8,128)(2,1)} async-done(((bf16[32,128,2048]{2,1,0:T(8,128)(2,1)}), bf16[32,128,2048]{2,1,0:T(8,128)(2,1)}, u32[]{:S(2)}, u32[]{:S(2)}) %all-to-all-start.3) | async-done | bytes 16777248 | tf_op jit(solution)/shard_map/all_to_all | solution.py:243
  2764.6 38.7 gather_fusion.1
  2850.9 20.0 convert_bitcast_fusion
  2956.3 41.8 reduce-scatter.13.cloned.1.call-done
  3047.4 88.1 %reduce-scatter.31.cloned.1.call-done = f32[64,16]{1,0:T(8,128)} async-done(((f32[2048,16]{1,0:T(8,128)}), f32[64,16]{1,0:T(8,128)}) %reduce-scatter.31.cloned.1.call-update) | async-done | bytes 4112
  3136.9 18.0 convolution_bitcast_fusion.2
  3154.9 17.8 convolution_bitcast_fusion
  3198.2 46.0 all-reduce.4
  3251.0 373.1 %reduce-scatter.29.cloned.1.call-done = f32[88,2048]{1,0:T(8,128)} async-done(((f32[2816,2048]{1,0:T(8,128)}), f32[88,2048]{1,0:T(8,128)}) %reduce-scatter.29.cloned.1.call-update) | async-done | bytes 720912 | tf_op jit(solution)/shard_map/reduce_scatter | solution.py:352
  3624.1 491.1 %reduce-scatter.27.cloned.1.call-done = f32[64,2816]{1,0:T(8,128)} async-done(((f32[2048,2816]{1,0:T(8,128)}), f32[64,2816]{1,0:T(8,128)}) %reduce-scatter.27.cloned.1.call-update) | async-done | bytes 720912 | tf_op jit(solution)/shard_map/reduce_scatter | solution.py:351
  4115.1 490.9 %reduce-scatter.25.cloned.1.call-done = f32[64,2816]{1,0:T(8,128)} async-done(((f32[2048,2816]{1,0:T(8,128)}), f32[64,2816]{1,0:T(8,128)}) %reduce-scatter.25.cloned.1.call-update) | async-done | bytes 720912 | tf_op jit(solution)/shard_map/reduce_scatter | solution.py:350
  4606.0 150.3 %reduce-scatter.19.cloned.1.call-done = f32[64,576]{1,0:T(8,128)} async-done(((f32[2048,576]{1,0:T(8,128)}), f32[64,576]{1,0:T(8,128)}) %reduce-scatter.19.cloned.1.call-update) | async-done | bytes 147472 | tf_op jit(solution)/shard_map/reduce_scatter | solution.py:344
  4756.4 185.1 %reduce-scatter.21.cloned.1.call-done = f32[16,4096]{1,0:T(8,128)} async-done(((f32[512,4096]{1,0:T(8,128)}), f32[16,4096]{1,0:T(8,128)}) %reduce-scatter.21.cloned.1.call-update) | async-done | bytes 262160 | tf_op jit(solution)/shard_map/reduce_scatter | solution.py:346
  4941.5 360.6 %reduce-scatter.23.cloned.1.call-done = f32[64,2048]{1,0:T(8,128)} async-done(((f32[2048,2048]{1,0:T(8,128)}), f32[64,2048]{1,0:T(8,128)}) %reduce-scatter.23.cloned.1.call-update) | async-done | bytes 524304 | tf_op jit(solution)/shard_map/reduce_scatter | solution.py:347
  5302.1 252.6 %reduce-scatter.17.cloned.1.call-done = f32[64,3072]{1,0:T(8,128)} async-done(((f32[2048,3072]{1,0:T(8,128)}), f32[64,3072]{1,0:T(8,128)}) %reduce-scatter.17.cloned.1.call-update) | async-done | bytes 786448 | tf_op jit(solution)/shard_map/reduce_scatter | solution.py:343
  (341 shorter events, 584.0 us)
Async XLA Ops:
  7.2 1226.2 %copy-start = (bf16[1,704,2048]{2,1,0:T(8,128)(2,1)S(1)}, bf16[1,704,2048]{2,1,0:T(8,128)(2,1)}, u32[]{:S(2)}) copy-start(bf16[1,704,2048]{2,1,0:T(8,128)(2,1)} %param.33) | copy-start | bytes 8650756
  7.2 59.4 %all-gather.11.cloned.1.call-start = ((), (), s32[]{:S(2)}) async-start(), calls=%async_computation.14 | async-start | bytes 2654208 | tf_op jit(solution)/shard_map/all_gather | solution.py:100
  7.9 132.4 %all-gather.13.cloned.1.call-start = ((), (), s32[]{:S(2)}) async-start(), calls=%async_computation.15 | async-start | bytes 4718592 | tf_op jit(solution)/shard_map/all_gather | solution.py:102
  8.7 194.0 %all-gather.15.cloned.1.call-start = ((), (), s32[]{:S(2)}) async-start(), calls=%async_computation.16 | async-start | bytes 10485760 | tf_op jit(solution)/shard_map/all_gather | solution.py:128
  52.0 345.8 %copy-start.39 = (f32[8,1,256]{2,1,0:T(1,128)}, f32[8,1,256]{2,1,0:T(1,128)S(1)}, u32[]{:S(2)}) copy-start(f32[8,1,256]{2,1,0:T(1,128)S(1)} %convert_element_type.192) | copy-start | bytes 24580
  69.5 118.6 %copy-start.18 = (f32[256,576]{0,1:T(8,128)}, f32[256,576]{0,1:T(8,128)S(1)}, u32[]{:S(2)}) copy-start(f32[256,576]{0,1:T(8,128)S(1)} %fusion.72) | copy-start | bytes 1769476
  145.3 235.9 %all-gather.17.cloned.1.call-start = ((), (), s32[]{:S(2)}) async-start(), calls=%async_computation.17 | async-start | bytes 14155776 | tf_op jit(solution)/shard_map/all_gather | solution.py:99
  145.9 360.5 %all-gather.19.cloned.1.call-start = ((), (), s32[]{:S(2)}) async-start(), calls=%async_computation.18 | async-start | bytes 9437184 | tf_op jit(solution)/shard_map/all_gather | solution.py:103
  167.3 346.1 %copy-start.48 = (f32[8,1,256]{2,1,0:T(1,128)}, f32[8,1,256]{2,1,0:T(1,128)S(1)}, u32[]{:S(2)}) copy-start(f32[8,1,256]{2,1,0:T(1,128)S(1)} %convert_element_type.193) | copy-start | bytes 24580
  188.3 216.6 %copy-start.44 = (f32[256,32]{0,1:T(8,128)}, f32[256,32]{0,1:T(8,128)S(1)}, u32[]{:S(2)}) copy-start(f32[256,32]{0,1:T(8,128)S(1)} %get-tuple-element.49) | copy-start | bytes 98308
  188.3 216.6 %copy-start.46 = (f32[256,32]{0,1:T(8,128)}, f32[256,32]{0,1:T(8,128)S(1)}, u32[]{:S(2)}) copy-start(f32[256,32]{0,1:T(8,128)S(1)} %get-tuple-element.50) | copy-start | bytes 98308
  194.5 210.5 %copy-start.34 = (bf16[1024,64]{0,1:T(8,128)(2,1)}, bf16[1024,64]{0,1:T(8,128)(2,1)S(1)}, u32[]{:S(2)}) copy-start(bf16[1024,64]{0,1:T(8,128)(2,1)S(1)} %all_gather.56) | copy-start | bytes 393220
  562.0 631.5 %all-to-all-start = ((bf16[32,128,2048]{2,1,0:T(8,128)(2,1)}), bf16[32,128,2048]{2,1,0:T(8,128)(2,1)}, u32[]{:S(2)}, u32[]{:S(2)}) async-start(bf16[32,128,2048]{2,1,0:T(8,128)(2,1)} %bitcast.218), calls=%async_computation | async-start | bytes 33554432 | tf_op jit(solution)/shard_map/all_to_all | solution.py:174
  565.9 1215.4 %all-gather.21.cloned.1.call-start = ((), (), s32[]{:S(2)}) async-start(), calls=%async_computation.19 | async-start | bytes 12976128 | tf_op jit(solution)/shard_map/all_gather | solution.py:106
  566.5 1224.1 %all-gather.23.cloned.1.call-start = ((), (), s32[]{:S(2)}) async-start(), calls=%async_computation.20 | async-start | bytes 12976128 | tf_op jit(solution)/shard_map/all_gather | solution.py:107
  1249.3 552.0 %all-to-all-start.1 = ((bf16[32,128,2048]{2,1,0:T(8,128)(2,1)}), bf16[32,128,2048]{2,1,0:T(8,128)(2,1)}, u32[]{:S(2)}, u32[]{:S(2)}) async-start(bf16[32,128,2048]{2,1,0:T(8,128)(2,1)} %convolution_convert_fusion), calls=%async_computation.1 | async-start | bytes 33554432 | tf_op jit(solution)/shard_map/all_to_all | solution.py:179
  1254.9 625.3 %all-gather.25.cloned.1.call-start = ((), (), s32[]{:S(2)}) async-start(), calls=%async_computation.21 | async-start | bytes 12976128 | tf_op jit(solution)/shard_map/all_gather | solution.py:108
  1255.7 534.9 %copy-start.55 = (s32[1,256,6]{1,2,0:T(8,128)}, s32[1,256,6]{1,2,0:T(8,128)S(1)}, u32[]{:S(2)}) copy-start(s32[1,256,6]{1,2,0:T(8,128)S(1)} %copy.158) | copy-start | bytes 18436
  1255.9 559.9 %copy-start.2 = (s32[1536]{0:T(1024)}, s32[1536]{0:T(1024)S(1)}, u32[]{:S(2)}) copy-start(s32[1536]{0:T(1024)S(1)} %reshape.431) | copy-start | bytes 18436
  2371.0 379.0 %all-to-all-start.3 = ((bf16[32,128,2048]{2,1,0:T(8,128)(2,1)}), bf16[32,128,2048]{2,1,0:T(8,128)(2,1)}, u32[]{:S(2)}, u32[]{:S(2)}) async-start(bf16[32,128,2048]{2,1,0:T(8,128)(2,1)} %add_convert_fusion), calls=%async_computation.3 | async-start | bytes 33554432 | tf_op jit(solution)/shard_map/all_to_all | solution.py:243
  2375.1 580.1 %reduce-scatter.15.cloned.1.call-start = ((), (), s32[]{:S(2)}) async-start(), calls=%async_computation.23 | async-start | bytes 163840 | tf_op jit(solution)/shard_map/reduce_scatter | solution.py:301
  2386.7 377.9 %copy-start.3 = (s32[1536]{0:T(1024)S(1)}, s32[1536]{0:T(1024)}, u32[]{:S(2)}) copy-start(s32[1536]{0:T(1024)} %copy-done.2) | copy-start | bytes 18436
  2907.7 90.4 %reduce-scatter.13.cloned.1.call-start = ((), (), s32[]{:S(2)}) async-start(), calls=%async_computation.22 | async-start | bytes 10485760 | tf_op jit(solution)/shard_map/reduce_scatter | solution.py:298
  2915.9 219.5 %reduce-scatter.31.cloned.1.call-start = ((), (), s32[]{:S(2)}) async-start(), calls=%async_computation.31 | async-start | bytes 1081344
  2918.7 705.4 %reduce-scatter.29.cloned.1.call-start = ((), (), s32[]{:S(2)}) async-start(), calls=%async_computation.30 | async-start | bytes 23789568 | tf_op jit(solution)/shard_map/reduce_scatter | solution.py:352
  2929.7 1185.4 %reduce-scatter.27.cloned.1.call-start = ((), (), s32[]{:S(2)}) async-start(), calls=%async_computation.29 | async-start | bytes 23789568 | tf_op jit(solution)/shard_map/reduce_scatter | solution.py:351
  2944.0 1662.1 %reduce-scatter.25.cloned.1.call-start = ((), (), s32[]{:S(2)}) async-start(), calls=%async_computation.28 | async-start | bytes 23789568 | tf_op jit(solution)/shard_map/reduce_scatter | solution.py:350
  2955.1 1801.3 %reduce-scatter.19.cloned.1.call-start = ((), (), s32[]{:S(2)}) async-start(), calls=%async_computation.25 | async-start | bytes 5406720 | tf_op jit(solution)/shard_map/reduce_scatter | solution.py:344
  3006.0 1935.5 %reduce-scatter.21.cloned.1.call-start = ((), (), s32[]{:S(2)}) async-start(), calls=%async_computation.26 | async-start | bytes 8650752 | tf_op jit(solution)/shard_map/reduce_scatter | solution.py:346
  3012.3 2289.8 %reduce-scatter.23.cloned.1.call-start = ((), (), s32[]{:S(2)}) async-start(), calls=%async_computation.27 | async-start | bytes 17301504 | tf_op jit(solution)/shard_map/reduce_scatter | solution.py:347
  3023.2 2531.6 %reduce-scatter.17.cloned.1.call-start = ((), (), s32[]{:S(2)}) async-start(), calls=%async_computation.24 | async-start | bytes 25952256 | tf_op jit(solution)/shard_map/reduce_scatter | solution.py:343
  3188.8 2366.0 %copy-start.1 = (bf16[1,704,2048]{2,1,0:T(8,128)(2,1)S(1)}, bf16[1,704,2048]{2,1,0:T(8,128)(2,1)}, u32[]{:S(2)}) copy-start(bf16[1,704,2048]{2,1,0:T(8,128)(2,1)} %param.33) | copy-start | bytes 8650756
  (76 other events, 1202.7 us)
Sparse Core Ops, SparseCore 0:
  10.1 56.4 all-gather.10
  68.7 71.5 all-gather.12
  145.4 57.2 all-gather.14
  204.8 176.4 all-gather.16
  383.2 123.1 all-gather.18
  568.6 432.9 all-gather.20
  1003.8 211.9 all-gather.22
  1258.0 433.5 all-gather.24
  2907.8 15.8 reduce-scatter.14
  2926.3 71.6 reduce-scatter.12
  3000.3 135.0 reduce-scatter.30
  3138.3 485.7 reduce-scatter.28
  3627.0 488.0 reduce-scatter.26
  4118.0 488.0 reduce-scatter.24
  4608.9 147.4 reduce-scatter.18
  4759.2 182.2 reduce-scatter.20
  4944.3 357.7 reduce-scatter.22
  5310.1 244.6 reduce-scatter.16
where the time goes:
time: 5570 us; the launch traced here: 5560 us
  waiting for transfers between devices  3710 us (67%)
  blocking collectives  1000 us (18%)
  matrix products  439 us (8%)
  local copies, waits for them, and re-layouts  238 us (4%)
  other arithmetic  141 us (3%)
    all_to_all x1, waiting for transfers between devices, on_device(): lax.all_to_all(outgoing, ('ctx', 'shard'), split_axis=0, concat_axis=0, t...  626 us
    all_gather x1, blocking collectives, on_device(): lax.all_gather(w_router, 'shard', axis=0, tiled=True)  523 us
    reduce_scatter x1, waiting for transfers between devices, on_device(): lax.psum_scatter(d_up_proj, ('ctx', 'shard'), scatter_dimension=0, tiled=...  491 us
    reduce_scatter x1, waiting for transfers between devices, on_device(): lax.psum_scatter(d_gate_proj, ('ctx', 'shard'), scatter_dimension=0, tile...  491 us
    reduce_scatter x1, waiting for transfers between devices, on_device(): lax.psum_scatter(d_down_proj, ('ctx', 'shard'), scatter_dimension=0, tile...  373 us
    all_to_all x1, blocking collectives, on_device(): lax.all_to_all(incoming, ('ctx', 'shard'), split_axis=0, concat_axis=0, t...  367 us
    all_to_all x1, waiting for transfers between devices, on_device(): lax.all_to_all(d_rows.astype(jnp.bfloat16), ('ctx', 'shard'), split_axis=...  363 us
    reduce_scatter x1, waiting for transfers between devices, on_device(): lax.psum_scatter(d_out_proj, ('ctx', 'shard'), scatter_dimension=0, tiled...  361 us
  transfers between devices with their start and end apart: 21, of which 16 were waited for; matrix products, arithmetic and copies ran while one was open for 8% of the time, Pallas kernels for 0%

commit v1 on v0

v1 whole, which is shorter than its diff:
```python
import functools

import jax
import jax.numpy as jnp
from jax import lax
from jax.experimental import pallas as pl
from jax.experimental.pallas import tpu as pltpu
from jax.sharding import PartitionSpec as P

H = 16
DN = 128
DR = 64
DV = 128
LAT = 512
TOP = 6
BLOCK = 256
LANES = 128

epsilon = 1e-06
base_freq = 10000.0
f32 = jnp.float32
bf16 = jnp.bfloat16


def tables(position, width):
    half = width // 2
    freqs = base_freq ** (-jnp.arange(half, dtype=f32) / half)
    angle = position.astype(f32)[:, None] * freqs[None, :]
    return (jnp.cos(angle), jnp.sin(angle))


def rotate(values, cosine, sine):
    half = values.shape[-1] // 2
    first = values[..., :half]
    second = values[..., half:]
    return jnp.concatenate([first * cosine - second * sine, second * cosine + first * sine], -1)


def rotate_back(grads, cosine, sine):
    return rotate(grads, cosine, -sine)


def inverse_root(values):
    return lax.rsqrt(jnp.mean(values * values, axis=-1, keepdims=True) + epsilon)


def norm_back(values, factor, gain, grads):
    scaled = grads * gain
    d_values = factor * scaled - values * factor**3 * jnp.mean(
        values * scaled, axis=-1, keepdims=True
    )
    return (d_values, jnp.sum(grads * values * factor, axis=0))


def silu_parts(values):
    sigma = jax.nn.sigmoid(values)
    return (values * sigma, sigma * (1.0 + values * (1.0 - sigma)))


def mm(left, right):
    return jnp.dot(left, right, preferred_element_type=f32)


def mm_nt(left, right):
    return lax.dot_general(left, right, (((1,), (1,)), ((), ())), preferred_element_type=f32)


def mm_tn(left, right):
    return lax.dot_general(left, right, (((0,), (0,)), ((), ())), preferred_element_type=f32)


def core_swap(value):
    count = lax.axis_size("ctx")
    return lax.ppermute(value, "ctx", [(i, i ^ 1) for i in range(count)])


def x_shift(value):
    count = lax.axis_size("ctx")
    return lax.ppermute(value, "ctx", [(i, (i + 2) % count) for i in range(count)])


def half_swap(value):
    count = lax.axis_size("shard")
    return lax.ppermute(value, "shard", [(i, i ^ 1) for i in range(count)])


def q_shift(value):
    count = lax.axis_size("shard")
    return lax.ppermute(value, "shard", [(i, (i + 2) % count) for i in range(count)])


def ring_sum(terms, shift):
    if len(terms) == 1:
        return terms[0].astype(f32)
    total = terms[1]
    for term in list(terms[2:]) + [terms[0]]:
        total = shift(total.astype(bf16)).astype(f32) + term.astype(f32)
    return total


def gather_x(block):
    found = [block]
    for _ in range(lax.axis_size("ctx") // 2 - 1):
        found.append(x_shift(found[-1]))
    return [[item, core_swap(item)] for item in found]


def scatter_x(terms):
    pairs = [item[0].astype(f32) + core_swap(item[1].astype(bf16)).astype(f32) for item in terms]
    return ring_sum(pairs, x_shift)


def place_of(dx, dc):
    ctx = lax.axis_index("ctx")
    chips = lax.axis_size("ctx") // 2
    return ((ctx // 2 - dx + chips) % chips) * 2 + (ctx % 2 + dc) % 2


def gather_ctx(block):
    rows = block.shape[0]
    full = jnp.zeros((rows * lax.axis_size("ctx"),) + block.shape[1:], block.dtype)
    for dx, pair in enumerate(gather_x(block)):
        for dc, item in enumerate(pair):
            full = lax.dynamic_update_slice_in_dim(full, item, place_of(dx, dc) * rows, 0)
    return full


def scatter_ctx(full):
    count = lax.axis_size("ctx")
    rows = full.shape[0] // count
    terms = [
        [lax.dynamic_slice_in_dim(full, place_of(dx, dc) * rows, rows, 0) for dc in range(2)]
        for dx in range(count // 2)
    ]
    return scatter_x(terms)


def scatter_shard(full):
    count = lax.axis_size("shard")
    me = lax.axis_index("shard")
    ring = count // 2
    sums = []
    for dq in range(ring):
        base = ((me // 2 - dq + ring) % ring) * 2
        own = lax.dynamic_index_in_dim(full, base + me % 2, 0, False)
        other = lax.dynamic_index_in_dim(full, base + 1 - me % 2, 0, False)
        sums.append(own.astype(f32) + half_swap(other.astype(bf16)).astype(f32))
    return ring_sum(sums, q_shift)


def attn_parts(q_ref, r_ref, p_ref, k_ref, block, scale):
    size = (block + 1) * BLOCK
    at = pl.ds(block * BLOCK, BLOCK)
    query = q_ref[at, :]
    rope = r_ref[0, at, :]
    keys = p_ref[0:size, 0:DN]
    values = p_ref[0:size, DN : DN + DV]
    key_rope = k_ref[0:size, :]
    scores = (mm_nt(query, keys) + mm_nt(rope, key_rope)) * scale
    weights = jnp.exp(scores - jnp.max(scores, axis=-1, keepdims=True))
    probs = weights / jnp.sum(weights, axis=-1, keepdims=True)
    return query, rope, keys, values, key_rope, probs, size, at


def attn_fwd_kernel(scale, q_ref, r_ref, p_ref, k_ref, o_ref):
    for block in range(q_ref.shape[0] // BLOCK):
        _, _, _, values, _, probs, _, at = attn_parts(q_ref, r_ref, p_ref, k_ref, block, scale)
        o_ref[at, :] = mm(probs.astype(bf16), values).astype(bf16)


def attn_bwd_kernel(scale, q_ref, r_ref, p_ref, k_ref, g_ref, dq_ref, dr_ref, dp_ref, dk_ref, sum_ref):
    @pl.when(pl.program_id(0) == 0)
    def _():
        dk_ref[...] = jnp.zeros_like(dk_ref)

    sum_ref[...] = jnp.zeros_like(sum_ref)
    for block in range(q_ref.shape[0] // BLOCK):
        query, rope, keys, values, key_rope, probs, size, at = attn_parts(
            q_ref, r_ref, p_ref, k_ref, block, scale
        )
        grad = g_ref[at, :]
        low = probs.astype(bf16)
        d_probs = mm_nt(grad, values)
        d_scores = probs * (d_probs - jnp.sum(probs * d_probs, axis=-1, keepdims=True))
        d_scores = d_scores.astype(bf16)
        dq_ref[at, :] = (mm(d_scores, keys) * scale).astype(bf16)
        dr_ref[0, at, :] = mm(d_scores, key_rope) * scale
        sum_ref[0:size, 0:DN] += mm_tn(d_scores, query) * scale
        sum_ref[0:size, DN : DN + DV] += mm_tn(low, grad)
        dk_ref[0:size, :] += mm_tn(d_scores, rope) * scale
    dp_ref[...] = sum_ref[...].astype(bf16)


def attn_specs(seq):
    return [
        pl.BlockSpec((seq, DN), lambda i: (0, i)),
        pl.BlockSpec((1, seq, DR), lambda i: (i, 0, 0)),
        pl.BlockSpec((seq, DN + DV), lambda i: (0, i)),
        pl.BlockSpec((seq, DR), lambda i: (0, 0)),
    ]


def attend(query, rope, pairs, key_rope, scale):
    seq = query.shape[0]
    heads = rope.shape[0]
    return pl.pallas_call(
        functools.partial(attn_fwd_kernel, scale),
        grid=(heads,),
        in_specs=attn_specs(seq),
        out_specs=pl.BlockSpec((seq, DV), lambda i: (0, i)),
        out_shape=jax.ShapeDtypeStruct((seq, heads * DV), bf16),
        compiler_params=pltpu.CompilerParams(vmem_limit_bytes=40 * 1024 * 1024),
        name="attend",
    )(query, rope, pairs, key_rope)


def attend_back(query, rope, pairs, key_rope, grad, scale):
    seq = query.shape[0]
    heads = rope.shape[0]
    return pl.pallas_call(
        functools.partial(attn_bwd_kernel, scale),
        grid=(heads,),
        in_specs=attn_specs(seq) + [pl.BlockSpec((seq, DV), lambda i: (0, i))],
        out_specs=[
            pl.BlockSpec((seq, DN), lambda i: (0, i)),
            pl.BlockSpec((1, seq, DR), lambda i: (i, 0, 0)),
            pl.BlockSpec((seq, DN + DV), lambda i: (0, i)),
            pl.BlockSpec((seq, DR), lambda i: (0, 0)),
        ],
        out_shape=[
            jax.ShapeDtypeStruct((seq, heads * DN), bf16),
            jax.ShapeDtypeStruct((heads, seq, DR), f32),
            jax.ShapeDtypeStruct((seq, heads * (DN + DV)), bf16),
            jax.ShapeDtypeStruct((seq, DR), f32),
        ],
        scratch_shapes=[pltpu.VMEM((seq, DN + DV), f32)],
        compiler_params=pltpu.CompilerParams(vmem_limit_bytes=40 * 1024 * 1024),
        name="attend_back",
    )(query, rope, pairs, key_rope, grad)


def on_device(
    tokens,
    target,
    routes,
    attn_gain,
    w_query,
    w_latent_in,
    latent_gain,
    w_latent_out,
    w_attn_out,
    ffn_gain,
    w_router,
    shared_gate,
    shared_up,
    shared_down,
    expert_gate,
    expert_up,
    expert_down,
):
    rows = tokens.shape[1]
    width = tokens.shape[2]
    ctx_count = lax.axis_size("ctx")
    shard_count = lax.axis_size("shard")
    chips = ctx_count // 2
    ring = shard_count // 2
    experts = ctx_count * ring
    capacity = max(2, (rows * TOP * 4 + experts * 3 - 1) // (experts * 3))
    seq_len = rows * ctx_count
    own_heads = H // ctx_count
    scale = (DN + DR) ** (-0.5)
    ctx = lax.axis_index("ctx")
    shard = lax.axis_index("shard")
    expert = ctx * ring + shard // 2
    devices = ctx_count * shard_count
    piece = width // devices

    gates_w = [expert_gate[0], half_swap(expert_gate[0])]
    ups_w = [expert_up[0], half_swap(expert_up[0])]
    downs_w = [expert_down[0], half_swap(expert_down[0])]

    depth = w_query.shape[0]
    small = jnp.concatenate([attn_gain, ffn_gain, latent_gain, w_router.reshape(-1)])
    small = lax.all_gather(small, "shard", axis=0, tiled=False)
    gain_attn = small[:, :depth].reshape(width).astype(f32)
    gain_ffn = small[:, depth : 2 * depth].reshape(width).astype(f32)
    lat_rows = latent_gain.shape[0]
    gain_latent = small[:, 2 * depth : 2 * depth + lat_rows].reshape(LAT).astype(f32)
    router_proj = small[:, 2 * depth + lat_rows :].reshape(width, experts)

    own_query = lax.dynamic_slice_in_dim(
        w_query, ctx * own_heads * (DN + DR), own_heads * (DN + DR), 1
    ).reshape(depth, own_heads, DN + DR)
    plain_cols = own_heads * DN
    rope_cols = own_heads * DR
    packed = jnp.concatenate(
        [
            own_query[..., :DN].reshape(depth, plain_cols),
            own_query[..., DN:].reshape(depth, rope_cols),
            w_latent_in,
        ],
        1,
    )
    packed = lax.all_gather(packed, "shard", axis=0, tiled=True)
    plain_proj = packed[:, :plain_cols]
    rope_proj = packed[:, plain_cols : plain_cols + rope_cols]
    latent_down = packed[:, plain_cols + rope_cols :]
    own_pairs = own_heads * (DN + DV)
    latent_up = lax.all_gather(
        lax.dynamic_slice_in_dim(w_latent_out, ctx * own_pairs, own_pairs, 1),
        "shard",
        axis=0,
        tiled=True,
    )
    out_piece = 0.0
    for j in range(ctx_count):
        moves = []
        for t in range(shard_count):
            to = t * ctx_count + j
            base = (to // shard_count) * shard_count
            moves.append((base + t, to))
        out_piece = out_piece + lax.ppermute(
            w_attn_out[j * piece : (j + 1) * piece], ("ctx", "shard"), moves
        )
    out_proj = lax.all_gather(out_piece, "shard", axis=0, tiled=True)

    slice_rows = shared_down.shape[0] // ctx_count
    down_own = lax.dynamic_slice_in_dim(shared_down, ctx * slice_rows, slice_rows, 0)
    shared_down_w = jnp.concatenate([down_own, half_swap(down_own)], 0)
    both = jnp.stack([shared_gate, shared_up], 1).reshape(
        depth, 2, shard_count, ctx_count, slice_rows
    )
    both = lax.dynamic_index_in_dim(both, ctx, 3, False)
    both = both.transpose(2, 0, 1, 3).reshape(shard_count, depth, 2 * slice_rows)
    both = lax.all_to_all(both, "shard", split_axis=0, concat_axis=0, tiled=True)
    both = both.reshape(width, 2 * slice_rows)
    both_other = half_swap(both)
    shared_gate_w = jnp.concatenate([both[:, :slice_rows], both_other[:, :slice_rows]], 1)
    shared_up_w = jnp.concatenate([both[:, slice_rows:], both_other[:, slice_rows:]], 1)

    source = tokens[0].astype(f32)
    factor_attn = inverse_root(source)
    all_source = gather_ctx(tokens[0]).astype(f32)
    attn_in = (all_source * inverse_root(all_source) * gain_attn).astype(bf16)
    cosine, sine = tables(jnp.arange(seq_len), DR)
    query = mm(attn_in, plain_proj).astype(bf16)
    query_rope = jnp.einsum(
        "td,dhk->htk",
        attn_in,
        rope_proj.reshape(width, own_heads, DR),
        preferred_element_type=f32,
    )
    query_rope = rotate(query_rope, cosine, sine).astype(bf16)
    latent_raw = mm(attn_in, latent_down)
    latent_part = latent_raw[:, :LAT]
    latent = (latent_part * inverse_root(latent_part) * gain_latent).astype(bf16)
    key_rope = rotate(latent_raw[:, LAT:], cosine, sine).astype(bf16)
    pairs = mm(latent, latent_up).astype(bf16)
    heads = attend(query, query_rope, pairs, key_rope, scale)
    middle = source + scatter_ctx(mm(heads, out_proj).astype(bf16))

    factor_ffn = inverse_root(middle)
    ffn_in = (middle * factor_ffn * gain_ffn).astype(bf16)
    router = jax.nn.softmax(mm(ffn_in, router_proj), axis=-1)
    chosen_any = jnp.any(
        routes[0][:, :, None] == jnp.arange(experts, dtype=jnp.int32)[None, None, :], axis=1
    )
    weight = jnp.where(chosen_any, router, -1.0)
    weight_high = weight.astype(bf16)
    weight_low = (weight - weight_high.astype(f32)).astype(bf16)
    info = jnp.concatenate(
        [
            weight_high,
            weight_low,
            jnp.zeros((rows, max(0, LANES - 2 * experts)), bf16),
        ],
        1,
    )
    info_cols = info.shape[1]

    def spread(block):
        found = []
        for step in range(ring):
            if step:
                block = q_shift(block)
            pairs_of = gather_x(block)
            found.append(jnp.stack([item for pair in pairs_of for item in pair], 0))
        return found

    def unspread(chunks):
        sums = []
        for chunk in chunks:
            terms = [[chunk[2 * dx], chunk[2 * dx + 1]] for dx in range(chips)]
            sums.append(scatter_x(terms))
        return ring_sum(sums, q_shift)

    before = (jnp.arange(rows)[:, None] <= jnp.arange(rows)[None, :]).astype(bf16)
    column = jnp.arange(info_cols)
    is_high = column == expert
    is_low = column == experts + expert

    kept = []
    outs = []
    for chunk in spread(jnp.concatenate([ffn_in, info], 1)):
        rows_in = chunk[..., :width]
        weights = jnp.sum(
            jnp.where(is_high | is_low, chunk[..., width:].astype(f32), 0.0), axis=-1
        )
        chosen = weights >= 0.0
        slot = jnp.einsum(
            "bt,tu->bu", chosen.astype(bf16), before, preferred_element_type=f32
        ).astype(jnp.int32)
        pick = (
            chosen[:, None, :]
            & (slot[:, None, :] == 1 + jnp.arange(capacity, dtype=jnp.int32)[None, :, None])
        )
        weight_row = jnp.sum(jnp.where(pick, weights[:, None, :], 0.0), axis=-1).reshape(-1, 1)
        pick = pick.astype(bf16)
        taken = (
            jnp.einsum("bjt,btd->bjd", pick, rows_in, preferred_element_type=f32)
            .astype(bf16)
            .reshape(-1, width)
        )
        gate_vals = [mm(taken, w) for w in gates_w]
        up_vals = [mm(taken, w) for w in ups_w]
        hidden = [g * jax.nn.sigmoid(g) * u for g, u in zip(gate_vals, up_vals)]
        scaled = [(v * weight_row).astype(bf16) for v in hidden]
        made = sum(mm(v, w) for v, w in zip(scaled, downs_w)).astype(bf16)
        flat = rows_in.reshape(-1, width)
        shared_gate_val = mm(flat, shared_gate_w)
        shared_up_val = mm(flat, shared_up_w)
        shared_hidden = (
            shared_gate_val * jax.nn.sigmoid(shared_gate_val) * shared_up_val
        ).astype(bf16)
        out = jnp.einsum(
            "bjt,bjd->btd",
            pick,
            made.reshape(-1, capacity, width),
            preferred_element_type=f32,
        ) + mm(shared_hidden, shared_down_w).reshape(rows_in.shape)
        outs.append(out.astype(bf16))
        kept.append(
            (
                flat,
                pick,
                weight_row,
                taken,
                gate_vals,
                up_vals,
                scaled,
                shared_gate_val,
                shared_up_val,
                shared_hidden,
            )
        )
    final = middle + unspread(outs)
    error = final - target[0].astype(f32)
    loss_part = jnp.sum(error * error)

    d_chunks = []
    grads = []
    for chunk, saved in zip(spread(error.astype(bf16)), kept):
        (
            flat,
            pick,
            weight_row,
            taken,
            gate_vals,
            up_vals,
            scaled,
            shared_gate_val,
            shared_up_val,
            shared_hidden,
        ) = saved
        d_flat = chunk.reshape(-1, width)
        d_taken = (
            jnp.einsum("bjt,btd->bjd", pick, chunk, preferred_element_type=f32)
            .astype(bf16)
            .reshape(-1, width)
        )
        d_weight = 0.0
        d_gates = []
        d_ups = []
        for g, u, w in zip(gate_vals, up_vals, downs_w):
            act, slope = silu_parts(g)
            d_plain = mm_nt(d_taken, w)
            d_weight = d_weight + jnp.sum(
                (act * u).astype(bf16).astype(f32) * d_plain, axis=-1, keepdims=True
            )
            d_hidden = d_plain * weight_row
            d_gates.append((d_hidden * u * slope).astype(bf16))
            d_ups.append((d_hidden * act).astype(bf16))
        d_rows = sum(mm_nt(v, w) for v, w in zip(d_gates, gates_w)) + sum(
            mm_nt(v, w) for v, w in zip(d_ups, ups_w)
        )
        shared_act, shared_slope = silu_parts(shared_gate_val)
        d_shared_hidden = mm_nt(d_flat, shared_down_w)
        d_shared_gate = (d_shared_hidden * shared_up_val * shared_slope).astype(bf16)
        d_shared_up = (d_shared_hidden * shared_act).astype(bf16)
        d_block = jnp.einsum(
            "bjt,bjd->btd",
            pick,
            d_rows.astype(bf16).reshape(-1, capacity, width),
            preferred_element_type=f32,
        ) + (mm_nt(d_shared_gate, shared_gate_w) + mm_nt(d_shared_up, shared_up_w)).reshape(
            chunk.shape
        )
        d_weight = jnp.sum(
            jnp.where(pick > 0, d_weight.reshape(-1, capacity, 1), 0.0), axis=1
        )[..., None]
        d_high = d_weight.astype(bf16)
        d_low = (d_weight - d_high.astype(f32)).astype(bf16)
        zero = jnp.zeros((), bf16)
        d_info = jnp.where(is_high, d_high, jnp.where(is_low, d_low, zero))
        d_chunks.append(jnp.concatenate([d_block.astype(bf16), d_info], -1))
        grads.append(
            (
                taken,
                d_taken,
                scaled,
                d_gates,
                d_ups,
                mm_tn(shared_hidden, d_flat),
                mm_tn(flat, d_shared_gate),
                mm_tn(flat, d_shared_up),
            )
        )
    d_all = unspread(d_chunks)
    d_ffn = d_all[:, :width]
    d_info = d_all[:, width:]
    d_router = d_info[:, :experts] + d_info[:, experts : 2 * experts]
    d_router = jnp.where(chosen_any, d_router, 0.0)

    taken = jnp.concatenate([item[0] for item in grads], 0)
    d_taken = jnp.concatenate([item[1] for item in grads], 0)
    d_expert = []
    for half in (1, 0):
        scaled = jnp.concatenate([item[2][half] for item in grads], 0)
        d_gates = jnp.concatenate([item[3][half] for item in grads], 0)
        d_ups = jnp.concatenate([item[4][half] for item in grads], 0)
        d_expert.append((mm_tn(taken, d_gates), mm_tn(taken, d_ups), mm_tn(scaled, d_taken)))
    d_expert = [own + half_swap(other.astype(bf16)).astype(f32) for other, own in zip(*d_expert)]

    def halves(value, axis):
        own = lax.slice_in_dim(value, 0, slice_rows, axis=axis)
        other = lax.slice_in_dim(value, slice_rows, 2 * slice_rows, axis=axis)
        return own, other

    d_shared_down = sum(item[5] for item in grads)
    d_shared_gate = sum(item[6] for item in grads)
    d_shared_up = sum(item[7] for item in grads)
    own, other = halves(d_shared_down, 0)
    d_shared_down = own + half_swap(other.astype(bf16)).astype(f32)
    moves = []
    for a in range(ctx_count):
        for b in range(shard_count):
            moves.append((a * shard_count + b, b * ctx_count + a))
    g_down = lax.ppermute(d_shared_down.astype(bf16), ("ctx", "shard"), moves).astype(f32)
    gate_own, gate_other = halves(d_shared_gate, 1)
    up_own, up_other = halves(d_shared_up, 1)
    d_both = jnp.concatenate([gate_own, up_own], 1) + half_swap(
        jnp.concatenate([gate_other, up_other], 1).astype(bf16)
    ).astype(f32)
    d_both = lax.all_to_all(
        d_both.astype(bf16).reshape(devices, piece, 2 * slice_rows),
        ("ctx", "shard"),
        split_axis=0,
        concat_axis=0,
        tiled=True,
    )
    d_both = d_both.reshape(ctx_count, shard_count, piece, 2, slice_rows)
    d_both = d_both.transpose(3, 2, 1, 0, 4).reshape(2, piece, -1).astype(f32)
    g_gate = d_both[0]
    g_up = d_both[1]

    d_logits = (router * (d_router - jnp.sum(router * d_router, axis=-1, keepdims=True))).astype(
        bf16
    )
    d_router_proj = mm_tn(ffn_in, d_logits)
    d_ffn = d_ffn + mm_nt(d_logits, router_proj)
    d_middle_norm, d_gain_ffn = norm_back(middle, factor_ffn, gain_ffn, d_ffn)
    d_middle = error + d_middle_norm

    d_branch = gather_ctx(d_middle.astype(bf16))
    d_out_proj = mm_tn(heads, d_branch)
    g_attn_out = scatter_shard(d_out_proj.reshape(shard_count, piece, width))
    d_heads = mm_nt(d_branch, out_proj).astype(bf16)
    d_query, d_rope, d_pairs, d_key_rope = attend_back(
        query, query_rope, pairs, key_rope, d_heads, scale
    )
    d_rope = rotate_back(d_rope, cosine, sine).astype(bf16)
    d_rope = d_rope.transpose(1, 0, 2).reshape(seq_len, rope_cols)
    d_latent_up = mm_tn(latent, d_pairs)
    d_latent = scatter_ctx(jnp.concatenate([mm_nt(d_pairs, latent_up), d_key_rope], 1))
    first = ctx * rows
    own_latent = lax.dynamic_slice_in_dim(latent_part, first, rows, 0)
    d_latent_part, d_gain_latent = norm_back(
        own_latent, inverse_root(own_latent), gain_latent, d_latent[:, :LAT]
    )
    own_cosine = lax.dynamic_slice_in_dim(cosine, first, rows, 0)
    own_sine = lax.dynamic_slice_in_dim(sine, first, rows, 0)
    d_latent_raw = jnp.concatenate(
        [d_latent_part, rotate_back(d_latent[:, LAT:], own_cosine, own_sine)], -1
    ).astype(bf16)
    latent_cols = (LAT + DR) // ctx_count
    d_latent_all = lax.dynamic_slice_in_dim(
        gather_ctx(d_latent_raw), ctx * latent_cols, latent_cols, 1
    )
    d_packed = mm_tn(attn_in, jnp.concatenate([d_query, d_rope, d_latent_all], 1)).astype(bf16)
    d_attn_in = scatter_ctx(
        (mm_nt(d_query, plain_proj) + mm_nt(d_rope, rope_proj)).astype(bf16)
    ) + mm_nt(d_latent_raw, latent_down)
    d_source_norm, d_gain_attn = norm_back(source, factor_attn, gain_attn, d_attn_in)
    token_grad = d_middle + d_source_norm

    def to_rows(value):
        cols = value.shape[1]
        value = value.reshape(ctx_count, shard_count, -1, cols).transpose(1, 0, 2, 3)
        value = scatter_shard(value).astype(bf16)
        return lax.all_to_all(value, "ctx", split_axis=0, concat_axis=0, tiled=True).astype(f32)

    g_packed = to_rows(d_packed)
    g_plain = g_packed[..., :plain_cols].reshape(ctx_count, piece, own_heads, DN)
    g_rope = g_packed[..., plain_cols : plain_cols + rope_cols]
    g_rope = g_rope.reshape(ctx_count, piece, own_heads, DR)
    g_query = jnp.concatenate([g_plain, g_rope], -1).transpose(1, 0, 2, 3).reshape(piece, -1)
    g_latent_in = g_packed[..., plain_cols + rope_cols :].transpose(1, 0, 2).reshape(piece, -1)
    g_latent_out = to_rows(d_latent_up)
    g_latent_out = g_latent_out.transpose(1, 0, 2).reshape(LAT // devices, -1)

    early = jnp.concatenate(
        [
            d_gain_ffn.reshape(devices, piece),
            d_router_proj.reshape(devices, piece * experts),
            jnp.broadcast_to(loss_part, (devices, 1)),
        ],
        1,
    )
    early = lax.psum_scatter(early, ("ctx", "shard"), scatter_dimension=0, tiled=True)[0]
    g_ffn = early[:piece]
    g_router = early[piece : piece + piece * experts].reshape(piece, experts)
    loss = early[-1] / (rows * devices * width)
    late = jnp.concatenate(
        [d_gain_attn.reshape(devices, piece), d_gain_latent.reshape(devices, -1)], 1
    )
    late = lax.psum_scatter(late, ("ctx", "shard"), scatter_dimension=0, tiled=True)[0]
    g_attn = late[:piece]
    g_latent = late[piece:]

    return (
        final.astype(bf16)[None],
        loss,
        token_grad[None],
        g_attn,
        g_query,
        g_latent_in,
        g_latent,
        g_latent_out,
        g_attn_out,
        g_ffn,
        g_router,
        g_gate,
        g_up,
        g_down,
        d_expert[0][None],
        d_expert[1][None],
        d_expert[2][None],
    )


def solution(mesh):
    in_specs = (
        P("shard", "ctx", None),
        P("shard", "ctx", None),
        P("shard", "ctx", None),
        P("shard"),
        P("shard", None),
        P("shard", None),
        P("shard"),
        P("shard", None),
        P("shard", None),
        P("shard"),
        P("shard", None),
        P("shard", None),
        P("shard", None),
        P("shard", None),
        P(("ctx", "shard"), None, None),
        P(("ctx", "shard"), None, None),
        P(("ctx", "shard"), None, None),
    )
    out_specs = (
        P("shard", "ctx", None),
        P(),
        P("shard", "ctx", None),
        P(("ctx", "shard")),
        P(("ctx", "shard"), None),
        P(("ctx", "shard"), None),
        P(("ctx", "shard")),
        P(("ctx", "shard"), None),
        P(("ctx", "shard"), None),
        P(("ctx", "shard")),
        P(("ctx", "shard"), None),
        P(("ctx", "shard"), None),
        P(("ctx", "shard"), None),
        P(("ctx", "shard"), None),
        P(("ctx", "shard"), None, None),
        P(("ctx", "shard"), None, None),
        P(("ctx", "shard"), None, None),
    )
    return jax.shard_map(
        on_device, mesh=mesh, in_specs=in_specs, out_specs=out_specs, check_vma=False
    )
```

time: 5570 us -> 1830 us (0.33)
  waiting for transfers between devices: 3710 us -> 620 us
  blocking collectives: 1000 us -> 40 us
  starting transfers between devices: 14.3 us -> 223 us
    reduce_scatter x9 -> x0, waiting for transfers between devices: 2350 us -> none  [the longest x1 491 us: on_device(): lax.psum_scatter(d_up_proj, ('ctx', 'shard'), scatter_dimension=0, tiled=...]
    all_to_all x3 -> x4, waiting for transfers between devices: 990 us -> 7.76 us  [the longest x2 7.76 us: to_rows(): lax.all_to_all(value, 'ctx', split_axis=0, concat_axis=0, tiled=True)]
    all_gather x4 -> x0, blocking collectives: 563 us -> none  [the longest x1 523 us: on_device(): lax.all_gather(w_router, 'shard', axis=0, tiled=True)]
    all_to_all x1 -> x0, blocking collectives: 367 us -> none  [on_device(): lax.all_to_all(incoming, ('ctx', 'shard'), split_axis=0, concat_axis=0, t...]
    ppermute x0 -> x114, waiting for transfers between devices: none -> 319 us  [the longest x22 148 us: x_shift(): lax.ppermute(value, 'ctx', [(i, (i + 2) % count) for i in range(count)])]
    ppermute x0 -> x114, starting transfers between devices: none -> 207 us  [the longest x44 133 us: core_swap(): return lax.ppermute(value, 'ctx', [(i, i ^ 1) for i in range(count)])]
    all_gather x8 -> x3, waiting for transfers between devices: 285 us -> 124 us  [the longest x1 71.9 us: on_device(): packed = lax.all_gather(packed, 'shard', axis=0, tiled=True)]
    gather x4 -> x0, local copies, waits for them, and re-layouts: 108 us -> none  [the longest x2 53.9 us: on_device(): routed_rows = combined[choose, slots]]
  transfers between devices with their start and end apart: 21 -> 123, of which waited for: 16 -> 39; matrix products, arithmetic and copies ran while one was open for 8% -> 42% of each run, Pallas kernels for 0% -> 2%
where the time goes in v1:
time: 1830 us; the launch traced here: 1820 us
  waiting for transfers between devices  620 us (34%)
  matrix products  479 us (26%)
  local copies, waits for them, and re-layouts  271 us (15%)
  starting transfers between devices  223 us (12%)
  other arithmetic  137 us (7%)
  blocking collectives  40 us (2%)
  Pallas kernels  32.6 us (2%)
  between operations  20.9 us (1%)
    unnamed x7, waiting for transfers between devices  169 us
    dot_general x41, matrix products, mm(): return jnp.dot(left, right, preferred_element_type=f32)  158 us
    dot_general x42, matrix products, mm_nt(): lax.dot_general(left, right, (((1,), (1,)), ((), ())), preferred_element_...  156 us
    ppermute x22, waiting for transfers between devices, x_shift(): lax.ppermute(value, 'ctx', [(i, (i + 2) % count) for i in range(count)])  148 us
    ppermute x44, starting transfers between devices, core_swap(): return lax.ppermute(value, 'ctx', [(i, i ^ 1) for i in range(count)])  133 us
    dot_general x22, matrix products, mm_tn(): lax.dot_general(left, right, (((0,), (0,)), ((), ())), preferred_element_...  110 us
    ppermute x21, waiting for transfers between devices, q_shift(): lax.ppermute(value, 'shard', [(i, (i + 2) % count) for i in range(count)])  90 us
    ppermute x22, waiting for transfers between devices, half_swap(): return lax.ppermute(value, 'shard', [(i, i ^ 1) for i in range(count)])  73.5 us
  transfers between devices with their start and end apart: 123, of which 39 were waited for; matrix products, arithmetic and copies ran while one was open for 42% of the time, Pallas kernels for 2%

profile of v1, /device:TPU:0, one launch (start us, length us, event | category | flops | bytes accessed | tf_op | source)
XLA Modules:
  0.0 1823.5 jit_solution(17245505306463881534)
XLA Ops:
  34.9 56.6 %all-reduce.6.cloned.1.call-done = bf16[37376]{0:T(1024)(128)(2,1)} async-done(((bf16[37376]{0:T(1024)(128)(2,1)}), bf16[37376]{0:T(1024)(128)(2,1)}) %all-reduce.6.cloned.1.call-update) | async-done | bytes 74768
  112.5 71.9 %all-gather.5.cloned.1.call-done = bf16[2048,1344]{0,1:T(8,128)(2,1)} async-done(((bf16[256,1344]{0,1:T(8,128)(2,1)}), bf16[2048,1344]{0,1:T(8,128)(2,1)}) %all-gather.5.cloned.1.call-update) | async-done | bytes 5505040 | tf_op jit(solution)/shard_map/all_gather | solution.py:304
  201.3 24.2 %all-gather.7.cloned.1.call-done = bf16[512,1024]{1,0:T(8,128)(2,1)} async-done(((bf16[64,1024]{1,0:T(8,128)(2,1)}), bf16[512,1024]{1,0:T(8,128)(2,1)}) %all-gather.7.cloned.1.call-update) | async-done | bytes 1048592 | tf_op jit(solution)/shard_map/all_gather | solution.py:309
  234.7 12.3 attend.1
  248.0 28.3 %all-gather.9.cloned.1.call-done = bf16[512,2048]{1,0:T(8,128)(2,1)} async-done(((bf16[64,2048]{1,0:T(8,128)(2,1)}), bf16[512,2048]{1,0:T(8,128)(2,1)}) %all-gather.9.cloned.1.call-update) | async-done | bytes 2097168 | tf_op jit(solution)/shard_map/all_gather | solution.py:325
  299.8 13.0 collective-permute-done.8
  330.1 17.3 collective-permute-done.10
  348.7 52.5 %collective-permute-done.17 = bf16[2048,176]{0,1:T(8,128)(2,1)} collective-permute-done((bf16[2048,176]{0,1:T(8,128)(2,1)}, bf16[2048,176]{0,1:T(8,128)(2,1)}, u32[]{:S(2)}, u32[]{:S(2)}) %collective-permute-start.17) | collective-permute-done | bytes 720928 | tf_op jit(solution)/shard_map/ppermute | solution.py:84
  438.5 8.8 copy.315
  678.4 19.5 %collective-permute-done.20 = bf16[256,2048]{0,1:T(8,128)(2,1)} collective-permute-done((bf16[256,2048]{0,1:T(8,128)(2,1)S(1)}, bf16[256,2048]{0,1:T(8,128)(2,1)}, u32[]{:S(2)}, u32[]{:S(2)}) %collective-permute-start.20) | collective-permute-done | bytes 1048608 | tf_op jit(solution)/shard_map/ppermute | solution.py:79
  703.4 16.9 collective-permute-done.28
  729.2 13.5 collective-permute-done.36
  754.7 9.7 collective-permute-done.43
  764.4 12.4 collective-permute-done.38
  783.5 20.3 %collective-permute-done.70 = bf16[256,2048]{0,1:T(8,128)(2,1)S(1)} collective-permute-done((bf16[256,2048]{0,1:T(8,128)(2,1)}, bf16[256,2048]{0,1:T(8,128)(2,1)S(1)}, u32[]{:S(2)}, u32[]{:S(2)}) %collective-permute-start.70) | collective-permute-done | bytes 1048608 | tf_op jit(solution)/shard_map/ppermute | solution.py:79
  1009.5 8.8 copy.326
  1036.8 9.5 convolution_convert_fusion.4
  1055.5 8.9 multiply_convert_fusion.8
  1072.2 10.4 convolution_convert_fusion.3
  1114.9 8.9 copy.331
  1159.6 127.1 %collective-permute-start.51 = (bf16[256,2176]{0,1:T(8,128)(2,1)}, bf16[256,2176]{0,1:T(8,128)(2,1)S(1)}, u32[]{:S(2)}, u32[]{:S(2)}) collective-permute-start(bf16[256,2176]{0,1:T(8,128)(2,1)} %get-tuple-element.163), channel_id=1, source_target_pairs={{0,8},{8,0},{16,24},{24,16},{1,9},{9,1},{17,25},{25,17},{2,10},{10... | collective-permute-start | bytes 3342344 | tf_op jit(solution)/shard_map/ppermute | solution.py:74
  1296.4 21.5 %collective-permute-done.50 = bf16[256,2176]{0,1:T(8,128)(2,1)S(1)} collective-permute-done((bf16[256,2176]{0,1:T(8,128)(2,1)S(1)}, bf16[256,2176]{0,1:T(8,128)(2,1)S(1)}, u32[]{:S(2)}, u32[]{:S(2)}) %collective-permute-start.50) | collective-permute-done | bytes 1114144 | tf_op jit(solution)/shard_map/ppermute | solution.py:79
  1354.5 12.7 add_bitcast_fusion
  1385.8 12.7 add_bitcast_fusion.1
  1400.6 11.8 collective-permute-done.68
  1422.0 10.5 add_bitcast_fusion.2
  1434.8 11.1 collective-permute-done.76
  1457.0 112.3 %all-reduce.8.cloned.1.call-done = f32[32,1089]{1,0:T(8,128)} async-done(((f32[32,1089]{1,0:T(8,128)}), f32[32,1089]{1,0:T(8,128)}) %all-reduce.8.cloned.1.call-update) | async-done | bytes 139408
  1599.9 20.3 %attend_back.1 = (bf16[1024,512]{1,0:T(8,128)(2,1)S(1)}, f32[4,1024,64]{2,1,0:T(8,128)S(1)}, bf16[1024,1024]{1,0:T(8,128)(2,1)S(1)}, f32[1024,64]{1,0:T(8,128)S(1)}) custom-call(bf16[1024,512]{1,0:T(8,128)(2,1)S(1)} %copy-done.7, bf16[4,1024,64]{2,1,0:T(8,128)(2,1)S(1)} %pad_maximum_fusion.24.r_ref, bf16[1024,1024]{1,0:T(8,128)(2,1)S(1)} %copy-done.3, ...), custom_call_target="tpu_custom_call" | custom-call | tf_op jit(solution)/shard_map/attend_back/pallas_call | solution.py:220
  1685.8 9.3 convolution_convert_fusion.1
  1723.9 9.4 collective-permute-done.89
  1756.9 40.0 %all-reduce.2 = f32[32,80]{1,0:T(8,128)S(1)} all-reduce(f32[32,80]{1,0:T(8,128)S(1)} %pad_maximum_fusion.32), channel_id=4, replica_groups=mesh['ctx'=4,'shard'=8] {'ctx','shard'}, use_global_device_ids=true, to_apply=%region_37.38.clone | all-reduce | flops 2560 | bytes 20480
  (1153 shorter events, 980.3 us)
Async XLA Ops:
  7.2 84.3 %all-reduce.6.cloned.1.call-start = ((), (), s32[]{:S(2)}) async-start(), calls=%async_computation.7 | async-start | bytes 151552
  13.4 171.0 %all-gather.5.cloned.1.call-start = ((), (), s32[]{:S(2)}) async-start(), calls=%async_computation.4 | async-start | bytes 6193152 | tf_op jit(solution)/shard_map/all_gather | solution.py:304
  14.6 210.9 %all-gather.7.cloned.1.call-start = ((), (), s32[]{:S(2)}) async-start(), calls=%async_computation.5 | async-start | bytes 1179648 | tf_op jit(solution)/shard_map/all_gather | solution.py:309
  15.2 87.9 %collective-permute-start = (bf16[256,2048]{0,1:T(8,128)(2,1)S(1)}, bf16[256,2048]{0,1:T(8,128)(2,1)}, u32[]{:S(2)}, u32[]{:S(2)}) collective-permute-start(bf16[256,2048]{0,1:T(8,128)(2,1)S(1)} %bitcast.629), channel_id=1, source_target_pairs={{0,8},{8,0},{16,24},{24,16},{1,9},{9,1},{17,25},{25,17},{2,10},{10... | collective-permute-start | bytes 3145736 | tf_op jit(solution)/shard_map/ppermute | solution.py:74
  15.8 81.3 %collective-permute-start.1 = (bf16[256,2048]{0,1:T(8,128)(2,1)S(1)}, bf16[256,2048]{0,1:T(8,128)(2,1)}, u32[]{:S(2)}, u32[]{:S(2)}) collective-permute-start(bf16[256,2048]{0,1:T(8,128)(2,1)S(1)} %bitcast.630), channel_id=1, source_target_pairs={{0,16},{8,24},{16,0},{24,8},{1,17},{9,25},{17,1},{25,9},{2,18},{10... | collective-permute-start | bytes 3145736 | tf_op jit(solution)/shard_map/ppermute | solution.py:79
  19.9 256.4 %all-gather.9.cloned.1.call-start = ((), (), s32[]{:S(2)}) async-start(), calls=%async_computation.6 | async-start | bytes 2359296 | tf_op jit(solution)/shard_map/all_gather | solution.py:325
  22.0 70.5 %collective-permute-start.3 = (bf16[64,2048]{1,0:T(8,128)(2,1)}, bf16[64,2048]{1,0:T(8,128)(2,1)S(1)}, u32[]{:S(2)}, u32[]{:S(2)}) collective-permute-start(bf16[64,2048]{1,0:T(8,128)(2,1)} %get-tuple-element.243), channel_id=1, source_target_pairs={{0,0},{1,4},{10,8},{11,12},{20,16},{21,20},{30,24},{31,28}} | collective-permute-start | bytes 786440 | tf_op jit(solution)/shard_map/ppermute | solution.py:322
  23.6 73.7 %collective-permute-start.4 = (bf16[64,2048]{1,0:T(8,128)(2,1)}, bf16[64,2048]{1,0:T(8,128)(2,1)S(1)}, u32[]{:S(2)}, u32[]{:S(2)}) collective-permute-start(bf16[64,2048]{1,0:T(8,128)(2,1)} %get-tuple-element.242), channel_id=1, source_target_pairs={{0,1},{1,5},{10,9},{11,13},{20,17},{21,21},{30,25},{31,29}} | collective-permute-start | bytes 786440 | tf_op jit(solution)/shard_map/ppermute | solution.py:322
  322.3 212.7 %collective-permute-start.14 = (bf16[2048,704]{0,1:T(8,128)(2,1)}, bf16[2048,704]{0,1:T(8,128)(2,1)}, u32[]{:S(2)}, u32[]{:S(2)}) collective-permute-start(bf16[2048,704]{0,1:T(8,128)(2,1)} %bitcast.14), channel_id=1, source_target_pairs={{0,1},{1,0},{2,3},{3,2},{4,5},{5,4},{6,7},{7,6},{8,9},{9,8},{10,11... | collective-permute-start | bytes 8650760 | tf_op jit(solution)/shard_map/ppermute | solution.py:84
  324.9 76.3 %collective-permute-start.17 = (bf16[2048,176]{0,1:T(8,128)(2,1)}, bf16[2048,176]{0,1:T(8,128)(2,1)}, u32[]{:S(2)}, u32[]{:S(2)}) collective-permute-start(bf16[2048,176]{0,1:T(8,128)(2,1)} %bitcast.198), channel_id=1, source_target_pairs={{0,1},{1,0},{2,3},{3,2},{4,5},{5,4},{6,7},{7,6},{8,9},{9,8},{10,11... | collective-permute-start | bytes 2162696 | tf_op jit(solution)/shard_map/ppermute | solution.py:84
  330.1 74.3 %collective-permute-start.39 = (bf16[256,2176]{0,1:T(8,128)(2,1)}, bf16[256,2176]{0,1:T(8,128)(2,1)S(1)}, u32[]{:S(2)}, u32[]{:S(2)}) collective-permute-start(bf16[256,2176]{0,1:T(8,128)(2,1)} %maximum_maximum_fusion), channel_id=1, source_target_pairs={{0,8},{8,0},{16,24},{24,16},{1,9},{9,1},{17,25},{25,17},{2,10},{10... | collective-permute-start | bytes 3342344 | tf_op jit(solution)/shard_map/ppermute | solution.py:74
  447.4 91.8 %collective-permute-start.15 = (bf16[2048,704]{0,1:T(8,128)(2,1)}, bf16[2048,704]{0,1:T(8,128)(2,1)}, u32[]{:S(2)}, u32[]{:S(2)}) collective-permute-start(bf16[2048,704]{0,1:T(8,128)(2,1)} %bitcast.582), channel_id=1, source_target_pairs={{0,1},{1,0},{2,3},{3,2},{4,5},{5,4},{6,7},{7,6},{8,9},{9,8},{10,11... | collective-permute-start | bytes 8650760 | tf_op jit(solution)/shard_map/ppermute | solution.py:84
  481.4 101.6 %collective-permute-start.16 = (bf16[704,2048]{1,0:T(8,128)(2,1)}, bf16[704,2048]{1,0:T(8,128)(2,1)}, u32[]{:S(2)}, u32[]{:S(2)}) collective-permute-start(bf16[704,2048]{1,0:T(8,128)(2,1)} %bitcast.581), channel_id=1, source_target_pairs={{0,1},{1,0},{2,3},{3,2},{4,5},{5,4},{6,7},{7,6},{8,9},{9,8},{10,11... | collective-permute-start | bytes 8650760 | tf_op jit(solution)/shard_map/ppermute | solution.py:84
  591.6 78.4 %collective-permute-start.19 = (bf16[256,2048]{0,1:T(8,128)(2,1)}, bf16[256,2048]{0,1:T(8,128)(2,1)}, u32[]{:S(2)}, u32[]{:S(2)}) collective-permute-start(bf16[256,2048]{0,1:T(8,128)(2,1)} %get-tuple-element.196), channel_id=1, source_target_pairs={{0,8},{8,0},{16,24},{24,16},{1,9},{9,1},{17,25},{25,17},{2,10},{10... | collective-permute-start | bytes 3145736 | tf_op jit(solution)/shard_map/ppermute | solution.py:74
  591.6 85.4 %collective-permute-start.21 = (bf16[256,2048]{0,1:T(8,128)(2,1)}, bf16[256,2048]{0,1:T(8,128)(2,1)}, u32[]{:S(2)}, u32[]{:S(2)}) collective-permute-start(bf16[256,2048]{0,1:T(8,128)(2,1)} %get-tuple-element.197), channel_id=1, source_target_pairs={{0,8},{8,0},{16,24},{24,16},{1,9},{9,1},{17,25},{25,17},{2,10},{10... | collective-permute-start | bytes 3145736 | tf_op jit(solution)/shard_map/ppermute | solution.py:74
  611.9 90.7 %collective-permute-start.29 = (bf16[256,2048]{0,1:T(8,128)(2,1)}, bf16[256,2048]{0,1:T(8,128)(2,1)}, u32[]{:S(2)}, u32[]{:S(2)}) collective-permute-start(bf16[256,2048]{0,1:T(8,128)(2,1)} %get-tuple-element.199), channel_id=1, source_target_pairs={{0,8},{8,0},{16,24},{24,16},{1,9},{9,1},{17,25},{25,17},{2,10},{10... | collective-permute-start | bytes 3145736 | tf_op jit(solution)/shard_map/ppermute | solution.py:74
  807.4 74.3 %collective-permute-start.46 = (bf16[256,2048]{0,1:T(8,128)(2,1)}, bf16[256,2048]{0,1:T(8,128)(2,1)}, u32[]{:S(2)}, u32[]{:S(2)}) collective-permute-start(bf16[256,2048]{0,1:T(8,128)(2,1)} %collective-permute-done.45), channel_id=1, source_target_pairs={{0,8},{8,0},{16,24},{24,16},{1,9},{9,1},{17,25},{25,17},{2,10},{10... | collective-permute-start | bytes 3145736 | tf_op jit(solution)/shard_map/ppermute | solution.py:74
  844.6 73.0 %collective-permute-start.61 = (bf16[256,2048]{0,1:T(8,128)(2,1)}, bf16[256,2048]{0,1:T(8,128)(2,1)}, u32[]{:S(2)}, u32[]{:S(2)}) collective-permute-start(bf16[256,2048]{0,1:T(8,128)(2,1)} %collective-permute-done.53), channel_id=1, source_target_pairs={{0,2},{1,3},{2,4},{3,5},{4,6},{5,7},{6,0},{7,1},{8,10},{9,11},{10,... | collective-permute-start | bytes 3145736 | tf_op jit(solution)/shard_map/ppermute | solution.py:89
  871.6 84.6 %collective-permute-start.54 = (bf16[256,2048]{0,1:T(8,128)(2,1)}, bf16[256,2048]{0,1:T(8,128)(2,1)}, u32[]{:S(2)}, u32[]{:S(2)}) collective-permute-start(bf16[256,2048]{0,1:T(8,128)(2,1)} %collective-permute-done.53), channel_id=1, source_target_pairs={{0,8},{8,0},{16,24},{24,16},{1,9},{9,1},{17,25},{25,17},{2,10},{10... | collective-permute-start | bytes 3145736 | tf_op jit(solution)/shard_map/ppermute | solution.py:74
  917.6 82.8 %collective-permute-start.63 = (bf16[256,2048]{0,1:T(8,128)(2,1)}, bf16[256,2048]{0,1:T(8,128)(2,1)}, u32[]{:S(2)}, u32[]{:S(2)}) collective-permute-start(bf16[256,2048]{0,1:T(8,128)(2,1)} %collective-permute-done.61), channel_id=1, source_target_pairs={{0,16},{8,24},{16,0},{24,8},{1,17},{9,25},{17,1},{25,9},{2,18},{10... | collective-permute-start | bytes 3145736 | tf_op jit(solution)/shard_map/ppermute | solution.py:79
  918.3 110.8 %collective-permute-start.62 = (bf16[256,2048]{0,1:T(8,128)(2,1)}, bf16[256,2048]{0,1:T(8,128)(2,1)}, u32[]{:S(2)}, u32[]{:S(2)}) collective-permute-start(bf16[256,2048]{0,1:T(8,128)(2,1)} %collective-permute-done.61), channel_id=1, source_target_pairs={{0,8},{8,0},{16,24},{24,16},{1,9},{9,1},{17,25},{25,17},{2,10},{10... | collective-permute-start | bytes 3145736 | tf_op jit(solution)/shard_map/ppermute | solution.py:74
  1099.4 189.3 %collective-permute-start.49 = (bf16[256,2176]{0,1:T(8,128)(2,1)}, bf16[256,2176]{0,1:T(8,128)(2,1)}, u32[]{:S(2)}, u32[]{:S(2)}) collective-permute-start(bf16[256,2176]{0,1:T(8,128)(2,1)} %get-tuple-element.162), channel_id=1, source_target_pairs={{0,8},{8,0},{16,24},{24,16},{1,9},{9,1},{17,25},{25,17},{2,10},{10... | collective-permute-start | bytes 3342344 | tf_op jit(solution)/shard_map/ppermute | solution.py:74
  1143.6 210.8 %collective-permute-start.113 = (bf16[704,2048]{1,0:T(8,128)(2,1)}, bf16[704,2048]{1,0:T(8,128)(2,1)}, u32[]{:S(2)}, u32[]{:S(2)}) collective-permute-start(bf16[704,2048]{1,0:T(8,128)(2,1)} %convolution_convert_fusion.4), channel_id=1, source_target_pairs={{0,1},{1,0},{2,3},{3,2},{4,5},{5,4},{6,7},{7,6},{8,9},{9,8},{10,11... | collective-permute-start | bytes 8650760 | tf_op jit(solution)/shard_map/ppermute | solution.py:84
  1144.3 241.5 %collective-permute-start.112 = (bf16[2048,704]{0,1:T(8,128)(2,1)}, bf16[2048,704]{0,1:T(8,128)(2,1)}, u32[]{:S(2)}, u32[]{:S(2)}) collective-permute-start(bf16[2048,704]{0,1:T(8,128)(2,1)} %convolution_convert_fusion.2), channel_id=1, source_target_pairs={{0,1},{1,0},{2,3},{3,2},{4,5},{5,4},{6,7},{7,6},{8,9},{9,8},{10,11... | collective-permute-start | bytes 8650760 | tf_op jit(solution)/shard_map/ppermute | solution.py:84
  1145.7 145.0 %collective-permute-start.57 = (bf16[256,2176]{0,1:T(8,128)(2,1)}, bf16[256,2176]{0,1:T(8,128)(2,1)}, u32[]{:S(2)}, u32[]{:S(2)}) collective-permute-start(bf16[256,2176]{0,1:T(8,128)(2,1)} %get-tuple-element.164), channel_id=1, source_target_pairs={{0,8},{8,0},{16,24},{24,16},{1,9},{9,1},{17,25},{25,17},{2,10},{10... | collective-permute-start | bytes 3342344 | tf_op jit(solution)/shard_map/ppermute | solution.py:74
  1154.5 166.5 %all-to-all-start.3 = ((bf16[32,64,176]{2,1,0:T(8,128)(2,1)}), bf16[32,64,176]{2,1,0:T(8,128)(2,1)S(1)}, u32[]{:S(2)}, u32[]{:S(2)}) async-start(bf16[32,64,176]{2,1,0:T(8,128)(2,1)} %bitcast.644), calls=%async_computation.3 | async-start | bytes 2097152 | tf_op jit(solution)/shard_map/all_to_all | solution.py:564
  1159.6 409.8 %all-reduce.8.cloned.1.call-start = ((), (), s32[]{:S(2)}) async-start(), calls=%async_computation.8 | async-start | bytes 294912
  1159.6 136.2 %collective-permute-start.51 = (bf16[256,2176]{0,1:T(8,128)(2,1)}, bf16[256,2176]{0,1:T(8,128)(2,1)S(1)}, u32[]{:S(2)}, u32[]{:S(2)}) collective-permute-start(bf16[256,2176]{0,1:T(8,128)(2,1)} %get-tuple-element.163), channel_id=1, source_target_pairs={{0,8},{8,0},{16,24},{24,16},{1,9},{9,1},{17,25},{25,17},{2,10},{10... | collective-permute-start | bytes 3342344 | tf_op jit(solution)/shard_map/ppermute | solution.py:74
  1335.5 85.7 %collective-permute-start.111 = (bf16[2048,704]{0,1:T(8,128)(2,1)}, bf16[2048,704]{0,1:T(8,128)(2,1)}, u32[]{:S(2)}, u32[]{:S(2)}) collective-permute-start(bf16[2048,704]{0,1:T(8,128)(2,1)} %convolution_convert_fusion.3), channel_id=1, source_target_pairs={{0,1},{1,0},{2,3},{3,2},{4,5},{5,4},{6,7},{7,6},{8,9},{9,8},{10,11... | collective-permute-start | bytes 8650760 | tf_op jit(solution)/shard_map/ppermute | solution.py:84
  1420.1 155.5 %collective-permute-start.75 = (bf16[256,2048]{0,1:T(8,128)(2,1)}, bf16[256,2048]{0,1:T(8,128)(2,1)}, u32[]{:S(2)}, u32[]{:S(2)}) collective-permute-start(bf16[256,2048]{0,1:T(8,128)(2,1)} %get-tuple-element.148), channel_id=1, source_target_pairs={{0,8},{8,0},{16,24},{24,16},{1,9},{9,1},{17,25},{25,17},{2,10},{10... | collective-permute-start | bytes 3145736 | tf_op jit(solution)/shard_map/ppermute | solution.py:74
  1445.9 135.3 %collective-permute-start.77 = (bf16[256,2048]{0,1:T(8,128)(2,1)}, bf16[256,2048]{0,1:T(8,128)(2,1)}, u32[]{:S(2)}, u32[]{:S(2)}) collective-permute-start(bf16[256,2048]{0,1:T(8,128)(2,1)} %collective-permute-done.76), channel_id=1, source_target_pairs={{0,8},{8,0},{16,24},{24,16},{1,9},{9,1},{17,25},{25,17},{2,10},{10... | collective-permute-start | bytes 3145736 | tf_op jit(solution)/shard_map/ppermute | solution.py:74
  1593.8 84.5 %collective-permute-start.105 = (bf16[64,2048]{1,0:T(8,128)(2,1)}, bf16[64,2048]{1,0:T(8,128)(2,1)}, u32[]{:S(2)}, u32[]{:S(2)}) collective-permute-start(bf16[64,2048]{1,0:T(8,128)(2,1)} %get-tuple-element.188), channel_id=1, source_target_pairs={{0,1},{1,0},{2,3},{3,2},{4,5},{5,4},{6,7},{7,6},{8,9},{9,8},{10,11... | collective-permute-start | bytes 786440 | tf_op jit(solution)/shard_map/ppermute | solution.py:84
  (379 other events, 6748.0 us)
Sparse Core Ops, SparseCore 0:
  13.5 77.9 all-reduce.5
  94.1 90.2 all-gather.4
  187.1 38.3 all-gather.6
  228.1 48.1 all-gather.8
  1451.6 117.7 all-reduce.7

commit v2 on v1

v2 whole, which is shorter than its diff:
```python
import functools

import jax
import jax.numpy as jnp
from jax import lax
from jax.experimental import pallas as pl
from jax.experimental.pallas import tpu as pltpu
from jax.sharding import PartitionSpec as P

H = 16
DN = 128
DR = 64
DV = 128
LAT = 512
TOP = 6
BLOCK = 256
LANES = 128

epsilon = 1e-06
base_freq = 10000.0
f32 = jnp.float32
bf16 = jnp.bfloat16


def tables(position, width):
    half = width // 2
    freqs = base_freq ** (-jnp.arange(half, dtype=f32) / half)
    angle = position.astype(f32)[:, None] * freqs[None, :]
    return (jnp.cos(angle), jnp.sin(angle))


def rotate(values, cosine, sine):
    half = values.shape[-1] // 2
    first = values[..., :half]
    second = values[..., half:]
    return jnp.concatenate([first * cosine - second * sine, second * cosine + first * sine], -1)


def rotate_back(grads, cosine, sine):
    return rotate(grads, cosine, -sine)


def inverse_root(values):
    return lax.rsqrt(jnp.mean(values * values, axis=-1, keepdims=True) + epsilon)


def norm_back(values, factor, gain, grads):
    scaled = grads * gain
    d_values = factor * scaled - values * factor**3 * jnp.mean(
        values * scaled, axis=-1, keepdims=True
    )
    return (d_values, jnp.sum(grads * values * factor, axis=0))


def silu_parts(values):
    sigma = jax.nn.sigmoid(values)
    return (values * sigma, sigma * (1.0 + values * (1.0 - sigma)))


def mm(left, right):
    return jnp.dot(left, right, preferred_element_type=f32)


def mm_nt(left, right):
    return lax.dot_general(left, right, (((1,), (1,)), ((), ())), preferred_element_type=f32)


def mm_tn(left, right):
    return lax.dot_general(left, right, (((0,), (0,)), ((), ())), preferred_element_type=f32)


def core_swap(value):
    count = lax.axis_size("ctx")
    return lax.ppermute(value, "ctx", [(i, i ^ 1) for i in range(count)])


def x_shift(value):
    count = lax.axis_size("ctx")
    return lax.ppermute(value, "ctx", [(i, (i + 2) % count) for i in range(count)])


def half_swap(value):
    count = lax.axis_size("shard")
    return lax.ppermute(value, "shard", [(i, i ^ 1) for i in range(count)])


def both_halves(value):
    count = lax.axis_size("shard")
    groups = [[i, i + 1] for i in range(0, count, 2)]
    return lax.all_gather(value, "shard", axis=0, tiled=False, axis_index_groups=groups)


def q_shift(value):
    count = lax.axis_size("shard")
    return lax.ppermute(value, "shard", [(i, (i + 2) % count) for i in range(count)])


def ring_sum(terms, shift, each=None):
    if len(terms) == 1:
        return terms[0].astype(f32)
    total = terms[1]
    for place, term in enumerate(list(terms[2:]) + [terms[0]]):
        total = shift(total.astype(bf16)).astype(f32) + term.astype(f32)
        if each is not None:
            total = each(place, total)
    return total


def gather_x(block):
    found = [block]
    for _ in range(lax.axis_size("ctx") // 2 - 1):
        found.append(x_shift(found[-1]))
    return [[item, core_swap(item)] for item in found]


def scatter_x(terms, last=None):
    pairs = [item[0].astype(f32) + core_swap(item[1].astype(bf16)).astype(f32) for item in terms]
    if last is not None:
        pairs[0] = last(pairs[0])
    return ring_sum(pairs, x_shift)


def place_of(dx, dc):
    ctx = lax.axis_index("ctx")
    chips = lax.axis_size("ctx") // 2
    return ((ctx // 2 - dx + chips) % chips) * 2 + (ctx % 2 + dc) % 2


def sum_ctx(value):
    total = value.astype(f32) + core_swap(value.astype(bf16)).astype(f32)
    moving = total.astype(bf16)
    for _ in range(lax.axis_size("ctx") // 2 - 1):
        moving = x_shift(moving)
        total = total + moving.astype(f32)
    return total


def scatter_ctx(full):
    count = lax.axis_size("ctx")
    rows = full.shape[0] // count
    terms = [
        [lax.dynamic_slice_in_dim(full, place_of(dx, dc) * rows, rows, 0) for dc in range(2)]
        for dx in range(count // 2)
    ]
    return scatter_x(terms)


def after(value, *others):
    operands = [value] + jax.tree.leaves(others)
    anywhere = pl.BlockSpec(memory_space=pl.ANY)
    return pl.pallas_call(
        lambda *refs: None,
        in_specs=[anywhere] * len(operands),
        out_specs=anywhere,
        out_shape=jax.ShapeDtypeStruct(value.shape, value.dtype),
        input_output_aliases={0: 0},
        name="after",
    )(*operands)


def both_of(own, other, bit):
    first = jnp.where(bit == 0, own, other)
    second = jnp.where(bit == 0, other, own)
    return jnp.concatenate([first, second], 0)


def ring_full(block, shift, count, me, each=None):
    if count == 1:
        return block
    rows = block.shape[0]
    full = jnp.zeros((count * rows,) + block.shape[1:], block.dtype)
    for step in range(count):
        if step:
            block = shift(block)
            if each is not None:
                block = each(block)
        full = lax.dynamic_update_slice_in_dim(full, block, ((me - step + count) % count) * rows, 0)
    return full


def gather_shard_from(pair, each=None):
    ring = lax.axis_size("shard") // 2
    return ring_full(pair, q_shift, ring, lax.axis_index("shard") // 2, each)


def gather_ctx_rows(block, between=None):
    ctx = lax.axis_index("ctx")
    chips = lax.axis_size("ctx") // 2
    lane = ring_full(block, x_shift, chips, ctx // 2)
    if between is not None:
        lane = between(lane)
    other = core_swap(lane)
    shape = (chips, 1) + block.shape
    lane, other = lane.reshape(shape), other.reshape(shape)
    first = jnp.where(ctx % 2 == 0, lane, other)
    second = jnp.where(ctx % 2 == 0, other, lane)
    return jnp.concatenate([first, second], 1).reshape((-1,) + block.shape[1:])


def all_sum(value):
    value = lax.all_to_all(value, ("ctx", "shard"), split_axis=0, concat_axis=0, tiled=True)
    return jnp.sum(value, axis=0)


def ring_shard(full, each=None):
    ring = lax.axis_size("shard") // 2
    me = lax.axis_index("shard") // 2
    full = full.reshape((ring, 2) + full.shape[1:])
    terms = [lax.dynamic_index_in_dim(full, (me - dq + ring) % ring, 0, False) for dq in range(ring)]
    return ring_sum(terms, q_shift, each)


def swap_halves(value):
    bit = lax.axis_index("shard") % 2
    own = lax.dynamic_index_in_dim(value, bit, 0, False)
    other = lax.dynamic_index_in_dim(value, 1 - bit, 0, False)
    return own.astype(f32) + half_swap(other.astype(bf16)).astype(f32)


def attn_parts(q_ref, r_ref, p_ref, k_ref, block, scale):
    size = (block + 1) * BLOCK
    at = pl.ds(block * BLOCK, BLOCK)
    query = q_ref[at, :]
    rope = r_ref[0, at, :]
    keys = p_ref[0:size, 0:DN]
    values = p_ref[0:size, DN : DN + DV]
    key_rope = k_ref[0:size, :]
    scores = (mm_nt(query, keys) + mm_nt(rope, key_rope)) * scale
    weights = jnp.exp(scores - jnp.max(scores, axis=-1, keepdims=True))
    probs = weights / jnp.sum(weights, axis=-1, keepdims=True)
    return query, rope, keys, values, key_rope, probs, size, at


def attn_fwd_kernel(scale, q_ref, r_ref, p_ref, k_ref, o_ref):
    for block in range(q_ref.shape[0] // BLOCK):
        _, _, _, values, _, probs, _, at = attn_parts(q_ref, r_ref, p_ref, k_ref, block, scale)
        o_ref[at, :] = mm(probs.astype(bf16), values).astype(bf16)


def attn_bwd_kernel(scale, q_ref, r_ref, p_ref, k_ref, g_ref, dq_ref, dr_ref, dp_ref, dk_ref, sum_ref):
    @pl.when(pl.program_id(0) == 0)
    def _():
        dk_ref[...] = jnp.zeros_like(dk_ref)

    sum_ref[...] = jnp.zeros_like(sum_ref)
    for block in range(q_ref.shape[0] // BLOCK):
        query, rope, keys, values, key_rope, probs, size, at = attn_parts(
            q_ref, r_ref, p_ref, k_ref, block, scale
        )
        grad = g_ref[at, :]
        low = probs.astype(bf16)
        d_probs = mm_nt(grad, values)
        d_scores = probs * (d_probs - jnp.sum(probs * d_probs, axis=-1, keepdims=True))
        d_scores = d_scores.astype(bf16)
        dq_ref[at, :] = (mm(d_scores, keys) * scale).astype(bf16)
        dr_ref[0, at, :] = mm(d_scores, key_rope) * scale
        sum_ref[0:size, 0:DN] += mm_tn(d_scores, query) * scale
        sum_ref[0:size, DN : DN + DV] += mm_tn(low, grad)
        dk_ref[0:size, :] += mm_tn(d_scores, rope) * scale
    dp_ref[...] = sum_ref[...].astype(bf16)


def attn_specs(seq):
    return [
        pl.BlockSpec((seq, DN), lambda i: (0, i)),
        pl.BlockSpec((1, seq, DR), lambda i: (i, 0, 0)),
        pl.BlockSpec((seq, DN + DV), lambda i: (0, i)),
        pl.BlockSpec((seq, DR), lambda i: (0, 0)),
    ]


def attend(query, rope, pairs, key_rope, scale):
    seq = query.shape[0]
    heads = rope.shape[0]
    return pl.pallas_call(
        functools.partial(attn_fwd_kernel, scale),
        grid=(heads,),
        in_specs=attn_specs(seq),
        out_specs=pl.BlockSpec((seq, DV), lambda i: (0, i)),
        out_shape=jax.ShapeDtypeStruct((seq, heads * DV), bf16),
        compiler_params=pltpu.CompilerParams(vmem_limit_bytes=40 * 1024 * 1024),
        name="attend",
    )(query, rope, pairs, key_rope)


def attend_back(query, rope, pairs, key_rope, grad, scale):
    seq = query.shape[0]
    heads = rope.shape[0]
    return pl.pallas_call(
        functools.partial(attn_bwd_kernel, scale),
        grid=(heads,),
        in_specs=attn_specs(seq) + [pl.BlockSpec((seq, DV), lambda i: (0, i))],
        out_specs=[
            pl.BlockSpec((seq, DN), lambda i: (0, i)),
            pl.BlockSpec((1, seq, DR), lambda i: (i, 0, 0)),
            pl.BlockSpec((seq, DN + DV), lambda i: (0, i)),
            pl.BlockSpec((seq, DR), lambda i: (0, 0)),
        ],
        out_shape=[
            jax.ShapeDtypeStruct((seq, heads * DN), bf16),
            jax.ShapeDtypeStruct((heads, seq, DR), f32),
            jax.ShapeDtypeStruct((seq, heads * (DN + DV)), bf16),
            jax.ShapeDtypeStruct((seq, DR), f32),
        ],
        scratch_shapes=[pltpu.VMEM((seq, DN + DV), f32)],
        compiler_params=pltpu.CompilerParams(vmem_limit_bytes=40 * 1024 * 1024),
        name="attend_back",
    )(query, rope, pairs, key_rope, grad)


def pick_of(info, tri, expert, experts, capacity):
    lanes = lax.broadcasted_iota(jnp.int32, (8, info.shape[1]), 1)
    mine = ((lanes == expert) | (lanes == experts + expert)).astype(f32).astype(bf16)
    weights = mm_nt(mine, info)[0:1, :]
    chosen = weights >= 0.0
    slot = mm(jnp.broadcast_to(chosen.astype(f32).astype(bf16), (8, info.shape[0])), tri)[0:1, :]
    place = lax.broadcasted_iota(jnp.int32, (capacity, info.shape[0]), 0).astype(f32) + 1.0
    pick = chosen & (slot == place)
    weight_row = jnp.sum(jnp.where(pick, weights, 0.0), axis=-1, keepdims=True)
    return pick.astype(f32).astype(bf16), weight_row


def triangle(rows):
    first = lax.broadcasted_iota(jnp.int32, (rows, rows), 0)
    second = lax.broadcasted_iota(jnp.int32, (rows, rows), 1)
    return (first <= second).astype(f32).astype(bf16)


def start_copies(sources, targets, sems, first):
    copies = [
        pltpu.make_async_copy(source, target, sems.at[first + i])
        for i, (source, target) in enumerate(zip(sources, targets))
    ]
    for item in copies:
        item.start()
    return copies


def wait_all(copies):
    for item in copies:
        item.wait()


def taker(refs):
    refs = list(refs)

    def take(count):
        found = refs[:count]
        del refs[:count]
        return found

    return take


WEIGHT_ORDER = (0, 2, 4, 1, 3, 5)


def halves_of(refs, other):
    return [ref for i in range(3) for ref in (refs[i], refs[3].at[other, i])]


def moe_fwd_kernel(dims, expert_ref, *refs):
    index, blocks, rows, width, experts, capacity, aliased = dims
    take = taker(refs)
    block_refs = take(blocks)
    weight_refs = halves_of(take(4), expert_ref[1])
    shared_refs = take(3)
    take(aliased)
    outs = take(blocks)
    keep_refs = take(6)
    flat, out, taken, gates, ups, scaled, shared_gates, shared_ups, made = take(9)
    weights = take(6)
    shared = take(3)
    (sems,) = take(1)
    picked = blocks * capacity
    here = pl.ds(index * picked, picked)
    tokens = pl.ds(index * blocks * rows, blocks * rows)
    spans = [pl.ds(b * rows, rows) for b in range(blocks)]
    arriving = start_copies(block_refs, [flat.at[span, :] for span in spans], sems, 0)
    moving = start_copies(
        [weight_refs[i] for i in WEIGHT_ORDER], [weights[i] for i in WEIGHT_ORDER], sems, blocks
    )
    moving = dict(zip(WEIGHT_ORDER, moving))
    rest = start_copies(shared_refs, shared, sems, blocks + 6)
    expert = expert_ref[0]
    tri = triangle(rows)
    picks = []
    weight_rows = []
    for b in range(blocks):
        arriving[b].wait()
        pick, weight_row = pick_of(flat[spans[b], width:], tri, expert, experts, capacity)
        picks.append(pick)
        weight_rows.append(weight_row)
        taken[pl.ds(b * capacity, capacity), :] = mm(pick, flat[spans[b], 0:width]).astype(bf16)
    leaving = start_copies([taken], [keep_refs[0].at[here, :]], sems, blocks + 9)
    weight_row = jnp.concatenate(weight_rows, 0)
    for side in range(2):
        moving[side].wait()
        gate = mm_nt(taken[...], weights[side][...])
        gates[side] = gate.astype(bf16)
        act = gate * jax.nn.sigmoid(gate) * weight_row
        moving[2 + side].wait()
        up = mm_nt(taken[...], weights[2 + side][...])
        ups[side] = up.astype(bf16)
        scaled[side] = (act * up).astype(bf16)
        moving[4 + side].wait()
        if side:
            made[...] += mm(scaled[side], weights[4 + side][...])
        else:
            made[...] = mm(scaled[side], weights[4 + side][...])
    leaving += start_copies(
        [gates, ups, scaled], [ref.at[:, here, :] for ref in keep_refs[1:4]], sems, blocks + 10
    )
    wait_all(rest)
    gate = mm_nt(flat[:, 0:width], shared[0][...])
    up = mm_nt(flat[:, 0:width], shared[1][...])
    shared_gates[...] = gate
    shared_ups[...] = up
    leaving += start_copies(
        [shared_gates, shared_ups], [ref.at[tokens, :] for ref in keep_refs[4:6]], sems, blocks + 13
    )
    hidden = (gate * jax.nn.sigmoid(gate) * up).astype(bf16)
    for b in range(blocks):
        rows_of = made[pl.ds(b * capacity, capacity), :].astype(bf16)
        out[spans[b], :] = (
            mm_tn(picks[b], rows_of) + mm(hidden[b * rows : (b + 1) * rows, :], shared[2][...])
        ).astype(bf16)
        leaving += start_copies([out.at[spans[b], :]], [outs[b]], sems, blocks + 15 + b)
    wait_all(leaving)


def moe_bwd_kernel(dims, expert_ref, *refs):
    index, blocks, rows, width, experts, capacity, aliased = dims
    take = taker(refs)
    error_refs = take(blocks)
    block_refs = take(blocks)
    weight_refs = halves_of(take(4), expert_ref[1])
    shared_refs = take(3)
    kept_refs = take(4)
    take(aliased)
    outs = take(blocks)
    sum_refs = take(3)
    keep_refs = take(3)
    errors, flat, taken, gates, ups, d_gates, d_ups, shared_gates, shared_ups, made = take(10)
    sums = take(3)
    weights = take(6)
    shared = take(3)
    (sems,) = take(1)
    picked = blocks * capacity
    here = pl.ds(index * picked, picked)
    tokens = pl.ds(index * blocks * rows, blocks * rows)
    spans = [pl.ds(b * rows, rows) for b in range(blocks)]
    arriving = start_copies(error_refs, [errors.at[span, 0:width] for span in spans], sems, 0)
    inputs = start_copies(block_refs, [flat.at[span, :] for span in spans], sems, blocks)
    first = 2 * blocks
    order = (4, 0, 2, 5, 1, 3)
    kept = start_copies(
        [ref.at[:, here, :] for ref in kept_refs[0:2]], [gates, ups], sems, first
    )
    moving = start_copies(
        [weight_refs[i] for i in order], [weights[i] for i in order], sems, first + 2
    )
    moving = dict(zip(order, moving))
    kept_shared = start_copies(
        [ref.at[tokens, :] for ref in kept_refs[2:4]], [shared_gates, shared_ups], sems, first + 8
    )
    rest = start_copies(shared_refs, shared, sems, first + 10)
    first = first + 13
    expert = expert_ref[0]
    tri = triangle(rows)
    picks = []
    weight_rows = []
    for b in range(blocks):
        inputs[b].wait()
        arriving[b].wait()
        pick, weight_row = pick_of(flat[spans[b], width:], tri, expert, experts, capacity)
        picks.append(pick)
        weight_rows.append(weight_row)
        taken[pl.ds(b * capacity, capacity), :] = mm(pick, errors[spans[b], 0:width]).astype(bf16)
    leaving = start_copies([taken], [keep_refs[0].at[here, :]], sems, first)
    weight_row = jnp.concatenate(weight_rows, 0)
    wait_all(kept)
    d_weight = 0.0
    for side in range(2):
        moving[4 + side].wait()
        d_plain = mm_nt(taken[...], weights[4 + side][...])
        gate = gates[side].astype(f32)
        up = ups[side].astype(f32)
        act, slope = silu_parts(gate)
        d_weight = d_weight + jnp.sum(act * up * d_plain, axis=-1, keepdims=True)
        d_hidden = d_plain * weight_row
        d_gates[side] = (d_hidden * up * slope).astype(bf16)
        d_ups[side] = (d_hidden * act).astype(bf16)
        moving[side].wait()
        moving[2 + side].wait()
        back = mm(d_gates[side], weights[side][...]) + mm(d_ups[side], weights[2 + side][...])
        if side:
            made[...] += back
        else:
            made[...] = back
    leaving += start_copies(
        [d_gates, d_ups], [ref.at[:, here, :] for ref in keep_refs[1:3]], sems, first + 1
    )
    wait_all(rest)
    wait_all(kept_shared)
    act, slope = silu_parts(shared_gates[...])
    shared_up = shared_ups[...]
    d_hidden = mm_nt(errors[:, 0:width], shared[2][...])
    d_gate = (d_hidden * shared_up * slope).astype(bf16)
    d_up = (d_hidden * act).astype(bf16)
    sums[0][...] = mm_tn(d_gate, flat[:, 0:width])
    sums[1][...] = mm_tn(d_up, flat[:, 0:width])
    sums[2][...] = mm_tn((act * shared_up).astype(bf16), errors[:, 0:width])
    leaving += start_copies(sums, sum_refs, sems, first + 3)
    info_cols = flat.shape[1] - width
    lanes = lax.broadcasted_iota(jnp.int32, (capacity, info_cols), 1)
    for b in range(blocks):
        rows_of = made[pl.ds(b * capacity, capacity), :].astype(bf16)
        span = slice(b * rows, (b + 1) * rows)
        errors[spans[b], 0:width] = (
            mm_tn(picks[b], rows_of)
            + mm(d_gate[span, :], shared[0][...])
            + mm(d_up[span, :], shared[1][...])
        ).astype(bf16)
        column = d_weight[b * capacity : (b + 1) * capacity, :]
        high = column.astype(bf16).astype(f32)
        found = jnp.where(lanes == expert, high, 0.0)
        found = jnp.where(lanes == experts + expert, column - high, found)
        errors[spans[b], width:] = mm_tn(picks[b], found.astype(bf16)).astype(bf16)
        leaving += start_copies([errors.at[spans[b], :]], [outs[b]], sems, first + 6 + b)
    wait_all(leaving)


def moe_call(kernel, dims, expert, groups, before, out_blocks, out_plain, out_kept, scratch, copies, cost, name):
    operands = [item for group in groups for item in group] + list(before)
    anywhere = pl.BlockSpec(memory_space=pl.ANY)
    shapes = out_blocks + out_plain + out_kept
    first = 1 + len(operands) - len(before)
    return pl.pallas_call(
        functools.partial(kernel, dims + (len(before),)),
        in_specs=[pl.BlockSpec(memory_space=pltpu.SMEM)] + [anywhere] * len(operands),
        out_specs=[anywhere] * len(shapes),
        out_shape=shapes,
        scratch_shapes=scratch + [pltpu.SemaphoreType.DMA((copies,))],
        input_output_aliases={
            first + i: len(out_blocks) + len(out_plain) + i for i in range(len(before))
        },
        compiler_params=pltpu.CompilerParams(vmem_limit_bytes=60 * 1024 * 1024),
        cost_estimate=cost,
        name=name,
    )(expert, *operands)


def moe_fwd(index, chunks, expert, experts, capacity, blocks, weights, shared, kept):
    count = len(blocks)
    rows = blocks[0].shape[0]
    half, width = weights[0].shape
    hidden = shared[0].shape[0]
    taken = count * capacity
    tokens = count * rows
    shape = jax.ShapeDtypeStruct
    result = moe_call(
        moe_fwd_kernel,
        (index, count, rows, width, experts, capacity),
        expert,
        (blocks, weights, shared),
        [] if kept is None else kept,
        [shape((rows, width), bf16)] * count,
        [],
        [shape((chunks * taken, width), bf16)]
        + [shape((2, chunks * taken, half), bf16)] * 3
        + [shape((chunks * tokens, hidden), f32)] * 2,
        [
            pltpu.VMEM((tokens, blocks[0].shape[1]), bf16),
            pltpu.VMEM((tokens, width), bf16),
            pltpu.VMEM((taken, width), bf16),
            pltpu.VMEM((2, taken, half), bf16),
            pltpu.VMEM((2, taken, half), bf16),
            pltpu.VMEM((2, taken, half), bf16),
            pltpu.VMEM((tokens, hidden), f32),
            pltpu.VMEM((tokens, hidden), f32),
            pltpu.VMEM((taken, width), f32),
        ]
        + [pltpu.VMEM((half, width), bf16)] * 6
        + [pltpu.VMEM((hidden, width), bf16)] * 3,
        2 * count + 15,
        pl.CostEstimate(flops=0, bytes_accessed=0, transcendentals=0),
        "moe_fwd",
    )
    return list(result[:count]), list(result[count:])


def moe_bwd(index, chunks, expert, experts, capacity, errors, blocks, weights, shared, kept, before):
    count = len(blocks)
    rows = blocks[0].shape[0]
    half, width = weights[0].shape
    hidden = shared[0].shape[0]
    taken = count * capacity
    tokens = count * rows
    shape = jax.ShapeDtypeStruct
    result = moe_call(
        moe_bwd_kernel,
        (index, count, rows, width, experts, capacity),
        expert,
        (errors, blocks, weights, shared, kept),
        [] if before is None else before,
        [shape(blocks[0].shape, bf16)] * count,
        [shape((hidden, width), f32)] * 3,
        [shape((chunks * taken, width), bf16)] + [shape((2, chunks * taken, half), bf16)] * 2,
        [
            pltpu.VMEM((tokens, blocks[0].shape[1]), bf16),
            pltpu.VMEM((tokens, blocks[0].shape[1]), bf16),
            pltpu.VMEM((taken, width), bf16),
            pltpu.VMEM((2, taken, half), bf16),
            pltpu.VMEM((2, taken, half), bf16),
            pltpu.VMEM((2, taken, half), bf16),
            pltpu.VMEM((2, taken, half), bf16),
            pltpu.VMEM((tokens, hidden), f32),
            pltpu.VMEM((tokens, hidden), f32),
            pltpu.VMEM((taken, width), f32),
        ]
        + [pltpu.VMEM((hidden, width), f32)] * 3
        + [pltpu.VMEM((half, width), bf16)] * 6
        + [pltpu.VMEM((hidden, width), bf16)] * 3,
        3 * count + 19,
        pl.CostEstimate(flops=0, bytes_accessed=0, transcendentals=0),
        "moe_bwd",
    )
    return list(result[:count]), list(result[count : count + 3]), list(result[count + 3 :])


def on_device(
    tokens,
    target,
    routes,
    attn_gain,
    w_query,
    w_latent_in,
    latent_gain,
    w_latent_out,
    w_attn_out,
    ffn_gain,
    w_router,
    shared_gate,
    shared_up,
    shared_down,
    expert_gate,
    expert_up,
    expert_down,
):
    rows = tokens.shape[1]
    width = tokens.shape[2]
    ctx_count = lax.axis_size("ctx")
    shard_count = lax.axis_size("shard")
    chips = ctx_count // 2
    ring = shard_count // 2
    experts = ctx_count * ring
    capacity = max(2, (rows * TOP * 4 + experts * 3 - 1) // (experts * 3))
    seq_len = rows * ctx_count
    own_heads = H // ctx_count
    scale = (DN + DR) ** (-0.5)
    ctx = lax.axis_index("ctx")
    shard = lax.axis_index("shard")
    expert = ctx * ring + shard // 2
    devices = ctx_count * shard_count
    piece = width // devices

    depth = w_query.shape[0]
    lat_rows = latent_gain.shape[0]
    part = depth // ctx_count
    lat_part = lat_rows // ctx_count
    half_bit = shard % 2
    small = jnp.concatenate(
        [
            w_latent_in,
            attn_gain[:, None],
            ffn_gain[:, None],
            jnp.pad(latent_gain.reshape(ctx_count, lat_part), ((0, 0), (0, part - lat_part)))
            .reshape(depth, 1),
            w_router,
        ],
        1,
    )
    small = jnp.pad(small, ((0, 0), (0, -small.shape[1] % LANES)))
    small = lax.dynamic_slice_in_dim(small, ctx * part, part, 0)
    own_query = lax.dynamic_slice_in_dim(
        w_query, ctx * own_heads * (DN + DR), own_heads * (DN + DR), 1
    ).reshape(depth, own_heads, DN + DR)
    plain_cols = own_heads * DN
    rope_cols = own_heads * DR
    packed = jnp.concatenate(
        [
            own_query[..., :DN].reshape(depth, plain_cols),
            own_query[..., DN:].reshape(depth, rope_cols),
        ],
        1,
    )
    own_pairs = own_heads * (DN + DV)
    up_piece = lax.dynamic_slice_in_dim(w_latent_out, ctx * own_pairs, own_pairs, 1)
    packed = jnp.concatenate([packed, up_piece.reshape(depth, -1)], 1)
    packed_pair = both_of(packed, half_swap(packed), half_bit)
    out_piece = 0.0
    for j in range(ctx_count):
        moves = []
        for t in range(shard_count):
            to = t * ctx_count + j
            base = (to // shard_count) * shard_count
            moves.append((base + t, to))
        out_piece = out_piece + lax.ppermute(
            w_attn_out[j * piece : (j + 1) * piece], ("ctx", "shard"), moves
        )
    out_pair = both_of(out_piece, half_swap(out_piece), half_bit)

    slice_rows = shared_down.shape[0] // ctx_count
    down_own = lax.dynamic_slice_in_dim(shared_down, ctx * slice_rows, slice_rows, 0)
    both = jnp.stack([shared_gate, shared_up], 0).reshape(
        2, depth, shard_count, ctx_count, slice_rows
    )
    both = lax.dynamic_index_in_dim(both, ctx, 3, False)
    both = both.transpose(2, 0, 3, 1).reshape(shard_count, 2 * slice_rows, depth)
    both = lax.all_to_all(both, "shard", split_axis=0, concat_axis=0, tiled=True)
    both = both.transpose(1, 0, 2).reshape(2 * slice_rows, width)
    slices = jnp.concatenate([both, down_own], 0)
    slices = jnp.stack([slices, half_swap(slices)], 0).reshape(2, 3, slice_rows, width)
    shared_all = [slices[:, i].reshape(2 * slice_rows, width) for i in range(3)]

    small = gather_shard_from(both_of(small, half_swap(small), half_bit))
    small = after(small, both)
    small = gather_ctx_rows(small).reshape(ctx_count, shard_count, part, -1)
    latent_cols = LAT + DR
    small_gains = small[..., latent_cols : latent_cols + 3].transpose(3, 1, 0, 2)
    gain_attn = small_gains[0].reshape(width).astype(f32)
    gain_ffn = small_gains[1].reshape(width).astype(f32)
    gain_latent = small_gains[2, :, :, :lat_part].reshape(LAT).astype(f32)
    small = small.transpose(1, 0, 2, 3).reshape(width, -1)
    latent_down = small[:, :latent_cols]
    router_proj = small[:, latent_cols + 3 : latent_cols + 3 + experts]

    own_half = [expert_gate[0].T, expert_up[0].T, expert_down[0]]
    weights_all = own_half + [both_halves(jnp.stack(own_half, 0))]

    gathered = gather_shard_from(packed_pair)
    plain_proj = gathered[:, :plain_cols]
    rope_proj = gathered[:, plain_cols : plain_cols + rope_cols]
    packed = gathered[:, : plain_cols + rope_cols]
    latent_up = gathered[:, plain_cols + rope_cols :].reshape(LAT, own_pairs)
    out_proj = gather_shard_from(after(out_pair, gathered, slices))

    source = tokens[0].astype(f32)
    factor_attn = inverse_root(source)
    all_source = gather_ctx_rows(tokens[0]).astype(f32)
    attn_in = (all_source * inverse_root(all_source) * gain_attn).astype(bf16)
    cosine, sine = tables(jnp.arange(seq_len), DR)
    query = mm(attn_in, plain_proj).astype(bf16)
    query_rope = jnp.einsum(
        "td,dhk->htk",
        attn_in,
        rope_proj.reshape(width, own_heads, DR),
        preferred_element_type=f32,
    )
    query_rope = rotate(query_rope, cosine, sine).astype(bf16)
    latent_raw = mm(attn_in, latent_down)
    latent_part = latent_raw[:, :LAT]
    latent = (latent_part * inverse_root(latent_part) * gain_latent).astype(bf16)
    key_rope = rotate(latent_raw[:, LAT:], cosine, sine).astype(bf16)
    pairs = mm(latent, latent_up).astype(bf16)
    heads = attend(query, query_rope, pairs, key_rope, scale)
    middle = source + scatter_ctx(mm(heads, out_proj).astype(bf16))

    factor_ffn = inverse_root(middle)
    ffn_in = (middle * factor_ffn * gain_ffn).astype(bf16)
    router = jax.nn.softmax(mm(ffn_in, router_proj), axis=-1)
    chosen_any = jnp.any(
        routes[0][:, :, None] == jnp.arange(experts, dtype=jnp.int32)[None, None, :], axis=1
    )
    weight = jnp.where(chosen_any, router, -1.0)
    weight_high = weight.astype(bf16)
    weight_low = (weight - weight_high.astype(f32)).astype(bf16)
    info = jnp.concatenate(
        [
            weight_high,
            weight_low,
            jnp.zeros((rows, max(0, LANES - 2 * experts)), bf16),
        ],
        1,
    )
    info_cols = info.shape[1]

    expert_at = jnp.stack([expert, 1 - half_bit]).astype(jnp.int32)

    def through(block, work, last=None, each=None):
        gate = expert_at
        sums = []
        done = []
        for step in range(ring):
            if step:
                block = q_shift(block)
            if step > 1:
                block = after(block, done[-2])
            found = work(step, [item for pair in gather_x(block) for item in pair], gate)
            done.append(found[0])
            pairs = [
                found[2 * i].astype(f32) + core_swap(found[2 * i + 1]).astype(f32)
                for i in range(chips)
            ]
            waits = [pairs[-1]] + (sums[-1:] if step > 1 else [])
            if step == ring - 1 and last is not None:
                pairs[0] = last(pairs[0])
            sums.append(ring_sum(pairs, x_shift))
            gate = after(expert_at, waits)
        return ring_sum(sums, q_shift, each)

    in_chunks = []
    kept = None

    def forward(index, chunk, gate):
        nonlocal kept
        in_chunks.append(chunk)
        out, kept = moe_fwd(
            index, ring, gate, experts, capacity, chunk, weights_all, shared_all, kept
        )
        return out

    final = middle + through(jnp.concatenate([ffn_in, info], 1), forward)
    error = final - target[0].astype(f32)
    loss_part = jnp.sum(error * error)

    d_shared = []
    d_kept = None

    def backward(index, chunk, gate):
        nonlocal d_kept
        out, part, d_kept = moe_bwd(
            index,
            ring,
            gate,
            experts,
            capacity,
            chunk,
            in_chunks[index],
            weights_all,
            shared_all,
            [kept[1], kept[2], kept[4], kept[5]],
            d_kept,
        )
        d_shared.append(part)
        return out

    def half_grads(half):
        taken, scaled = kept[0], kept[3]
        d_taken, d_gates, d_ups = d_kept
        return (mm_tn(d_gates[half], taken), mm_tn(d_ups[half], taken), mm_tn(scaled[half], d_taken))

    block = error.astype(bf16)
    terms = []
    for step in range(ring):
        if step:
            block = q_shift(block)
        found = backward(step, [item for pair in gather_x(block) for item in pair], expert_at)
        pairs_of = [[found[2 * i], found[2 * i + 1]] for i in range(chips)]
        terms.append(scatter_x(pairs_of))
    d_all = ring_sum(terms, q_shift)
    for_other = [item.astype(bf16) for item in half_grads(1)]
    from_other = [both_halves(for_other[0]), both_halves(jnp.stack(for_other[1:], 0))]
    d_ffn = d_all[:, :width]
    d_info = d_all[:, width:]
    d_router = d_info[:, :experts] + d_info[:, experts : 2 * experts]
    d_router = jnp.where(chosen_any, d_router, 0.0)

    d_slices = jnp.stack([sum(item[i] for item in d_shared) for i in range(3)], 0)
    d_logits = (router * (d_router - jnp.sum(router * d_router, axis=-1, keepdims=True))).astype(
        bf16
    )
    d_router_proj = mm_tn(ffn_in, d_logits)
    d_ffn = d_ffn + mm_nt(d_logits, router_proj)
    d_middle_norm, d_gain_ffn = norm_back(middle, factor_ffn, gain_ffn, d_ffn)
    d_middle = error + d_middle_norm

    d_branch = gather_ctx_rows(d_middle.astype(bf16))
    d_out_proj = mm_tn(heads, d_branch).astype(bf16)
    d_heads = mm_nt(d_branch, out_proj).astype(bf16)
    d_heads = after(d_heads, d_out_proj, from_other[0])
    d_query, d_rope, d_pairs, d_key_rope = attend_back(
        query, query_rope, pairs, key_rope, d_heads, scale
    )
    d_latent_sum = jnp.concatenate([mm_nt(d_pairs, latent_up), d_key_rope], 1).astype(bf16)
    d_latent = sum_ctx(d_latent_sum)
    d_rope = rotate_back(d_rope, cosine, sine).astype(bf16)
    d_rope = d_rope.transpose(1, 0, 2).reshape(seq_len, rope_cols)
    d_query = after(jnp.concatenate([d_query, d_rope], 1), d_latent_sum)
    d_latent_part, _ = norm_back(
        latent_part, inverse_root(latent_part), gain_latent, d_latent[:, :LAT]
    )
    d_latent_raw = jnp.concatenate(
        [d_latent_part, rotate_back(d_latent[:, LAT:], cosine, sine)], -1
    ).astype(bf16)
    first = ctx * rows
    own_latent = lax.dynamic_slice_in_dim(latent_part, first, rows, 0)
    own_grads = lax.dynamic_slice_in_dim(d_latent, first, rows, 0)[:, :LAT]
    d_gain_latent = jnp.sum(own_grads * own_latent * inverse_root(own_latent), axis=0)
    latent_cols = (LAT + DR) // ctx_count
    d_latent_all = lax.dynamic_slice_in_dim(
        d_latent_raw, ctx * latent_cols, latent_cols, 1
    )
    d_packed = mm_tn(attn_in, d_query).astype(bf16)
    d_attn_in = scatter_ctx(
        mm_nt(after(d_query, d_packed), packed).astype(bf16)
    ) + mm_nt(lax.dynamic_slice_in_dim(d_latent_raw, first, rows, 0), latent_down)
    d_latent_up = mm_tn(latent, d_pairs)
    d_source_norm, d_gain_attn = norm_back(source, factor_attn, gain_attn, d_attn_in)
    token_grad = d_middle + d_source_norm

    def by_rows(value):
        cols = value.shape[1]
        return value.astype(bf16).reshape(ctx_count, shard_count, -1, cols).transpose(1, 0, 2, 3)

    d_latent_in = by_rows(mm_tn(attn_in, d_latent_all))
    d_latent_out = by_rows(d_latent_up)
    latent_shape = d_latent_in.shape
    d_latents = jnp.concatenate(
        [d_latent_in.reshape(latent_shape[:2] + (-1,)), d_latent_out.reshape(latent_shape[:2] + (-1,))],
        2,
    ).reshape(shard_count, ctx_count, -1, LANES)

    early = jnp.concatenate(
        [
            d_out_proj.reshape(shard_count, -1, LANES),
            by_rows(d_packed).reshape(shard_count, -1, LANES),
        ],
        1,
    )
    sum_early = ring_shard(early)
    sum_latents = ring_shard(d_latents)
    sums = [sum_early, sum_latents]
    flat = jnp.concatenate([item.astype(bf16).reshape(2, -1, LANES) for item in sums], 1)
    flat = swap_halves(flat)
    out_rows = d_out_proj.size // (shard_count * LANES)
    g_attn_out = flat[:out_rows].reshape(piece, width)
    flat = flat[out_rows:].astype(bf16)
    packed_rows = d_packed.size // (shard_count * LANES)
    flat = jnp.concatenate(
        [
            flat[:packed_rows].reshape(ctx_count, -1, LANES),
            flat[packed_rows:].reshape(ctx_count, -1, LANES),
        ],
        1,
    )
    flat = lax.all_to_all(flat, "ctx", split_axis=0, concat_axis=0, tiled=True).astype(f32)
    packed_rows = packed_rows // ctx_count
    g_packed = flat[:, :packed_rows].reshape(ctx_count, piece, -1)
    g_plain = g_packed[..., :plain_cols].reshape(ctx_count, piece, own_heads, DN)
    g_rope = g_packed[..., plain_cols:].reshape(ctx_count, piece, own_heads, DR)
    g_query = jnp.concatenate([g_plain, g_rope], -1).transpose(1, 0, 2, 3).reshape(piece, -1)
    g_latents = flat[:, packed_rows:].reshape(ctx_count, -1)
    g_latent_in = g_latents[:, : piece * latent_cols].reshape(ctx_count, piece, latent_cols)
    g_latent_in = g_latent_in.transpose(1, 0, 2).reshape(piece, -1)
    g_latent_out = g_latents[:, piece * latent_cols :].reshape(ctx_count, LAT // devices, -1)
    g_latent_out = g_latent_out.transpose(1, 0, 2).reshape(LAT // devices, -1)

    from_other = [
        lax.dynamic_index_in_dim(after(item, late), 1 - half_bit, 0, False)
        for item, late in zip(from_other, (d_packed, d_latents))
    ]
    from_other = [from_other[0], from_other[1][0], from_other[1][1]]
    d_expert = [item + other.astype(f32) for item, other in zip(half_grads(0), from_other)]
    d_expert = [d_expert[0].T, d_expert[1].T, d_expert[2]]

    moves = []
    for a in range(ctx_count):
        for b in range(shard_count):
            moves.append((a * shard_count + b, b * ctx_count + a))
    d_slices = after(d_slices, d_heads).reshape(3, 2, slice_rows, width)
    d_slices = d_slices[:, 0] + half_swap(d_slices[:, 1].astype(bf16)).astype(f32)
    d_slices = after(d_slices.astype(bf16), d_packed)
    g_down = lax.ppermute(d_slices[2], ("ctx", "shard"), moves)
    d_both = d_slices[:2].reshape(2, slice_rows, devices, piece)
    d_both = lax.all_to_all(
        d_both.transpose(2, 0, 1, 3).reshape(devices, 2 * slice_rows, piece),
        ("ctx", "shard"),
        split_axis=0,
        concat_axis=0,
        tiled=True,
    )
    g_down = after(g_down, d_latents).astype(f32)
    d_both = after(d_both, d_latents)
    d_both = d_both.reshape(ctx_count, shard_count, 2, slice_rows, piece)
    d_both = d_both.transpose(2, 4, 1, 0, 3).reshape(2, piece, -1).astype(f32)
    g_gate = d_both[0]
    g_up = d_both[1]

    small_sums = jnp.concatenate(
        [
            d_gain_ffn.reshape(devices, piece),
            d_router_proj.reshape(devices, piece * experts),
            d_gain_attn.reshape(devices, piece),
            d_gain_latent.reshape(devices, -1),
            jnp.broadcast_to(loss_part, (devices, 1)),
        ],
        1,
    )
    small_sums = all_sum(small_sums)
    g_ffn = small_sums[:piece]
    at = piece + piece * experts
    g_router = small_sums[piece:at].reshape(piece, experts)
    g_attn = small_sums[at : at + piece]
    g_latent = small_sums[at + piece : -1]
    loss = small_sums[-1] / (rows * devices * width)

    return (
        final.astype(bf16)[None],
        loss,
        token_grad[None],
        g_attn,
        g_query,
        g_latent_in,
        g_latent,
        g_latent_out,
        g_attn_out,
        g_ffn,
        g_router,
        g_gate,
        g_up,
        g_down,
        d_expert[0][None],
        d_expert[1][None],
        d_expert[2][None],
    )


def solution(mesh):
    in_specs = (
        P("shard", "ctx", None),
        P("shard", "ctx", None),
        P("shard", "ctx", None),
        P("shard"),
        P("shard", None),
        P("shard", None),
        P("shard"),
        P("shard", None),
        P("shard", None),
        P("shard"),
        P("shard", None),
        P("shard", None),
        P("shard", None),
        P("shard", None),
        P(("ctx", "shard"), None, None),
        P(("ctx", "shard"), None, None),
        P(("ctx", "shard"), None, None),
    )
    out_specs = (
        P("shard", "ctx", None),
        P(),
        P("shard", "ctx", None),
        P(("ctx", "shard")),
        P(("ctx", "shard"), None),
        P(("ctx", "shard"), None),
        P(("ctx", "shard")),
        P(("ctx", "shard"), None),
        P(("ctx", "shard"), None),
        P(("ctx", "shard")),
        P(("ctx", "shard"), None),
        P(("ctx", "shard"), None),
        P(("ctx", "shard"), None),
        P(("ctx", "shard"), None),
        P(("ctx", "shard"), None, None),
        P(("ctx", "shard"), None, None),
        P(("ctx", "shard"), None, None),
    )
    return jax.shard_map(
        on_device, mesh=mesh, in_specs=in_specs, out_specs=out_specs, check_vma=False
    )
```

time: 1830 us -> 1250 us (0.68)
  matrix products: 479 us -> 107 us
  Pallas kernels: 32.6 us -> 247 us
  waiting for transfers between devices: 620 us -> 433 us
  starting transfers between devices: 223 us -> 115 us
  local copies, waits for them, and re-layouts: 271 us -> 171 us
  blocking collectives: 40 us -> 0 us
    pallas_call x0 -> x24, Pallas kernels: none -> 215 us  [the longest x8 215 us: moe_call(): pl.pallas_call(functools.partial(kernel, dims + (len(before),)), in_specs...]
    unnamed x7 -> x3, waiting for transfers between devices: 169 us -> 0.05 us
    dot_general x41 -> x5, matrix products: 158 us -> 13 us  [mm(): return jnp.dot(left, right, preferred_element_type=f32)]
    dot_general x42 -> x5, matrix products: 156 us -> 16 us  [mm_nt(): lax.dot_general(left, right, (((1,), (1,)), ((), ())), preferred_element_...]
    ppermute x44 -> x40, starting transfers between devices: 133 us -> 8.13 us  [core_swap(): return lax.ppermute(value, 'ctx', [(i, i ^ 1) for i in range(count)])]
    all_gather x3, waiting for transfers between devices: 124 us -> 0.02 us  [both_halves(): lax.all_gather(value, 'shard', axis=0, tiled=False, axis_index_groups=gro...]
    ppermute x21 -> x27, waiting for transfers between devices: 90 us -> 150 us  [q_shift(): lax.ppermute(value, 'shard', [(i, (i + 2) % count) for i in range(count)])]
    ppermute x22, waiting for transfers between devices: 148 us -> 204 us  [x_shift(): lax.ppermute(value, 'ctx', [(i, (i + 2) % count) for i in range(count)])]
  transfers between devices with their start and end apart: 123 -> 107, of which waited for: 39 -> 33; matrix products, arithmetic and copies ran while one was open for 42% -> 31% of each run, Pallas kernels for 2% -> 20%
where the time goes in v2:
time: 1250 us; the launch traced here: 1240 us
  waiting for transfers between devices  433 us (35%)
  Pallas kernels  247 us (20%)
  local copies, waits for them, and re-layouts  171 us (14%)
  other arithmetic  152 us (12%)
  starting transfers between devices  115 us (9%)
  matrix products  107 us (9%)
  between operations  18.4 us (1%)
    pallas_call x8, Pallas kernels, moe_call(): pl.pallas_call(functools.partial(kernel, dims + (len(before),)), in_specs...  215 us
    ppermute x22, waiting for transfers between devices, x_shift(): lax.ppermute(value, 'ctx', [(i, (i + 2) % count) for i in range(count)])  204 us
    ppermute x27, waiting for transfers between devices, q_shift(): lax.ppermute(value, 'shard', [(i, (i + 2) % count) for i in range(count)])  150 us
    dot_general x11, matrix products, mm_tn(): lax.dot_general(left, right, (((0,), (0,)), ((), ())), preferred_element_...  73.3 us
    ppermute x6, waiting for transfers between devices, half_swap(): return lax.ppermute(value, 'shard', [(i, i ^ 1) for i in range(count)])  71.4 us
    unnamed x287, local copies, waits for them, and re-layouts  44 us
    convert_element_type x19, other arithmetic, ring_sum(): total = shift(total.astype(bf16)).astype(f32) + term.astype(f32)  41.8 us
    ppermute x22, starting transfers between devices, x_shift(): lax.ppermute(value, 'ctx', [(i, (i + 2) % count) for i in range(count)])  38.6 us
  transfers between devices with their start and end apart: 107, of which 33 were waited for; matrix products, arithmetic and copies ran while one was open for 31% of the time, Pallas kernels for 20%

profile of v2, /device:TPU:0, one launch (start us, length us, event | category | flops | bytes accessed | tf_op | source)
XLA Modules:
  0.0 1243.0 jit_solution(1213895999218240571)
XLA Ops:
  86.4 16.6 %collective-permute-done.5 = bf16[128,640]{1,0:T(8,128)(2,1)S(1)} collective-permute-done((bf16[128,640]{1,0:T(8,128)(2,1)S(1)}, bf16[128,640]{1,0:T(8,128)(2,1)S(1)}, u32[]{:S(2)}, u32[]{:S(2)}) %collective-permute-start.5) | collective-permute-done | bytes 163872 | tf_op jit(solution)/shard_map/ppermute | solution.py:95
  122.9 39.7 %collective-permute-done.17 = bf16[264,2048]{1,0:T(8,128)(2,1)S(1)} collective-permute-done((bf16[264,2048]{1,0:T(8,128)(2,1)S(1)}, bf16[264,2048]{1,0:T(8,128)(2,1)S(1)}, u32[]{:S(2)}, u32[]{:S(2)}) %collective-permute-start.17) | collective-permute-done | bytes 1081376 | tf_op jit(solution)/shard_map/ppermute | solution.py:84
  232.9 11.9 attend.1
  264.5 23.3 %collective-permute-done.22 = bf16[256,2048]{1,0:T(8,128)(2,1)} collective-permute-done((bf16[256,2048]{1,0:T(8,128)(2,1)S(1)}, bf16[256,2048]{1,0:T(8,128)(2,1)}, u32[]{:S(2)}, u32[]{:S(2)}) %collective-permute-start.22) | collective-permute-done | bytes 1048608 | tf_op jit(solution)/shard_map/ppermute | solution.py:79
  298.9 23.8 %collective-permute-done.25.refs_2_.refs_6_ = bf16[256,2176]{1,0:T(8,128)(2,1)} collective-permute-done((bf16[256,2176]{1,0:T(8,128)(2,1)}, bf16[256,2176]{1,0:T(8,128)(2,1)}, u32[]{:S(2)}, u32[]{:S(2)}) %collective-permute-start.25) | collective-permute-done | bytes 1114144 | tf_op jit(solution)/shard_map/ppermute | solution.py:79
  330.3 23.4 %moe_fwd.4 = (bf16[256,2048]{1,0:T(8,128)(2,1)}, bf16[256,2048]{1,0:T(8,128)(2,1)}, bf16[256,2048]{1,0:T(8,128)(2,1)}, bf16[256,2048]{1,0:T(8,128)(2,1)}, bf16[2...) custom-call(s32[2]{0:T(128)} %pad_add_fusion.expert_ref, ...), custom_call_target="tpu_custom_call" | custom-call | tf_op jit(solution)/shard_map/moe_fwd/pallas_call | solution.py:539
  362.3 23.0 %moe_fwd.5 = (bf16[256,2048]{1,0:T(8,128)(2,1)}, bf16[256,2048]{1,0:T(8,128)(2,1)}, bf16[256,2048]{1,0:T(8,128)(2,1)}, bf16[256,2048]{1,0:T(8,128)(2,1)}, bf16[2...) custom-call(s32[2]{0:T(128)} %after.18.expert_ref, ...), custom_call_target="tpu_custom_call", output_to_operand_aliasing={{4}: (12, {}), {5}: (13, {}), {6}: (14, {}), {7}: (15, {}),... | custom-call | tf_op jit(solution)/shard_map/moe_fwd/pallas_call | solution.py:539
  394.5 23.4 %moe_fwd.6 = (bf16[256,2048]{1,0:T(8,128)(2,1)}, bf16[256,2048]{1,0:T(8,128)(2,1)}, bf16[256,2048]{1,0:T(8,128)(2,1)}, bf16[256,2048]{1,0:T(8,128)(2,1)}, bf16[2...) custom-call(s32[2]{0:T(128)} %after.19.expert_ref, ...), custom_call_target="tpu_custom_call", output_to_operand_aliasing={{4}: (12, {}), {5}: (13, {}), {6}: (14, {}), {7}: (15, {}),... | custom-call | tf_op jit(solution)/shard_map/moe_fwd/pallas_call | solution.py:539
  419.0 17.6 %collective-permute-done.33 = bf16[256,2048]{1,0:T(8,128)(2,1)} collective-permute-done((bf16[256,2048]{1,0:T(8,128)(2,1)}, bf16[256,2048]{1,0:T(8,128)(2,1)}, u32[]{:S(2)}, u32[]{:S(2)}) %collective-permute-start.33) | collective-permute-done | bytes 1048608 | tf_op jit(solution)/shard_map/ppermute | solution.py:79
  445.7 23.2 %moe_fwd.7 = (bf16[256,2048]{1,0:T(8,128)(2,1)}, bf16[256,2048]{1,0:T(8,128)(2,1)}, bf16[256,2048]{1,0:T(8,128)(2,1)}, bf16[256,2048]{1,0:T(8,128)(2,1)}, bf16[2...) custom-call(s32[2]{0:T(128)} %after.21.expert_ref, ...), custom_call_target="tpu_custom_call", output_to_operand_aliasing={{4}: (12, {}), {5}: (13, {}), {6}: (14, {}), {7}: (15, {}),... | custom-call | tf_op jit(solution)/shard_map/moe_fwd/pallas_call | solution.py:539
  476.9 22.2 %collective-permute-done.43 = bf16[256,2048]{1,0:T(8,128)(2,1)S(1)} collective-permute-done((bf16[256,2048]{1,0:T(8,128)(2,1)S(1)}, bf16[256,2048]{1,0:T(8,128)(2,1)S(1)}, u32[]{:S(2)}, u32[]{:S(2)}) %collective-permute-start.43) | collective-permute-done | bytes 1048608 | tf_op jit(solution)/shard_map/ppermute | solution.py:95
  502.0 20.2 %collective-permute-done.52 = bf16[256,2048]{1,0:T(8,128)(2,1)S(1)} collective-permute-done((bf16[256,2048]{1,0:T(8,128)(2,1)S(1)}, bf16[256,2048]{1,0:T(8,128)(2,1)S(1)}, u32[]{:S(2)}, u32[]{:S(2)}) %collective-permute-start.52) | collective-permute-done | bytes 1048608 | tf_op jit(solution)/shard_map/ppermute | solution.py:79
  531.1 22.3 %collective-permute-done.54.refs_0_ = bf16[256,2048]{1,0:T(8,128)(2,1)} collective-permute-done((bf16[256,2048]{1,0:T(8,128)(2,1)S(1)}, bf16[256,2048]{1,0:T(8,128)(2,1)}, u32[]{:S(2)}, u32[]{:S(2)}) %collective-permute-start.54) | collective-permute-done | bytes 1048608 | tf_op jit(solution)/shard_map/ppermute | solution.py:95
  555.5 19.2 %collective-permute-done.56.refs_2_ = bf16[256,2048]{1,0:T(8,128)(2,1)} collective-permute-done((bf16[256,2048]{1,0:T(8,128)(2,1)}, bf16[256,2048]{1,0:T(8,128)(2,1)}, u32[]{:S(2)}, u32[]{:S(2)}) %collective-permute-start.56) | collective-permute-done | bytes 1048608 | tf_op jit(solution)/shard_map/ppermute | solution.py:79
  580.3 30.6 %moe_bwd.4 = (bf16[256,2176]{1,0:T(8,128)(2,1)}, bf16[256,2176]{1,0:T(8,128)(2,1)}, bf16[256,2176]{1,0:T(8,128)(2,1)}, bf16[256,2176]{1,0:T(8,128)(2,1)}, f32[17...) custom-call(s32[2]{0:T(128)} %pad_add_fusion.expert_ref, ...), custom_call_target="tpu_custom_call" | custom-call | tf_op jit(solution)/shard_map/moe_bwd/pallas_call | solution.py:539
  610.9 30.5 %moe_bwd.5 = (bf16[256,2176]{1,0:T(8,128)(2,1)}, bf16[256,2176]{1,0:T(8,128)(2,1)}, bf16[256,2176]{1,0:T(8,128)(2,1)}, bf16[256,2176]{1,0:T(8,128)(2,1)}, f32[17...) custom-call(s32[2]{0:T(128)} %pad_add_fusion.expert_ref, ...), custom_call_target="tpu_custom_call", output_to_operand_aliasing={{7}: (20, {}), {8}: (21, {}), {9}: (22, {})} | custom-call | tf_op jit(solution)/shard_map/moe_bwd/pallas_call | solution.py:539
  647.6 30.6 %moe_bwd.6 = (bf16[256,2176]{1,0:T(8,128)(2,1)}, bf16[256,2176]{1,0:T(8,128)(2,1)}, bf16[256,2176]{1,0:T(8,128)(2,1)}, bf16[256,2176]{1,0:T(8,128)(2,1)}, f32[17...) custom-call(s32[2]{0:T(128)} %pad_add_fusion.expert_ref, ...), custom_call_target="tpu_custom_call", output_to_operand_aliasing={{7}: (20, {}), {8}: (21, {}), {9}: (22, {})} | custom-call | tf_op jit(solution)/shard_map/moe_bwd/pallas_call | solution.py:539
  684.8 30.6 %moe_bwd.7 = (bf16[256,2176]{1,0:T(8,128)(2,1)}, bf16[256,2176]{1,0:T(8,128)(2,1)}, bf16[256,2176]{1,0:T(8,128)(2,1)}, bf16[256,2176]{1,0:T(8,128)(2,1)}, f32[17...) custom-call(s32[2]{0:T(128)} %pad_add_fusion.expert_ref, ...), custom_call_target="tpu_custom_call", output_to_operand_aliasing={{7}: (20, {}), {8}: (21, {}), {9}: (22, {})} | custom-call | tf_op jit(solution)/shard_map/moe_bwd/pallas_call | solution.py:539
  727.8 17.8 %collective-permute-done.70 = bf16[256,2176]{1,0:T(8,128)(2,1)S(1)} collective-permute-done((bf16[256,2176]{1,0:T(8,128)(2,1)S(1)}, bf16[256,2176]{1,0:T(8,128)(2,1)S(1)}, u32[]{:S(2)}, u32[]{:S(2)}) %collective-permute-start.70) | collective-permute-done | bytes 1114144 | tf_op jit(solution)/shard_map/ppermute | solution.py:79
  758.3 34.2 %collective-permute-done.78 = bf16[256,2176]{1,0:T(8,128)(2,1)} collective-permute-done((bf16[256,2176]{1,0:T(8,128)(2,1)}, bf16[256,2176]{1,0:T(8,128)(2,1)}, u32[]{:S(2)}, u32[]{:S(2)}) %collective-permute-start.78) | collective-permute-done | bytes 1114144 | tf_op jit(solution)/shard_map/ppermute | solution.py:79
  805.5 17.8 %collective-permute-done.80 = bf16[256,2176]{1,0:T(8,128)(2,1)S(1)} collective-permute-done((bf16[256,2176]{1,0:T(8,128)(2,1)S(1)}, bf16[256,2176]{1,0:T(8,128)(2,1)S(1)}, u32[]{:S(2)}, u32[]{:S(2)}) %collective-permute-start.80) | collective-permute-done | bytes 1114144 | tf_op jit(solution)/shard_map/ppermute | solution.py:95
  840.8 16.0 %collective-permute-done.84 = bf16[256,2048]{1,0:T(8,128)(2,1)S(1)} collective-permute-done((bf16[256,2048]{1,0:T(8,128)(2,1)S(1)}, bf16[256,2048]{1,0:T(8,128)(2,1)S(1)}, u32[]{:S(2)}, u32[]{:S(2)}) %collective-permute-start.84) | collective-permute-done | bytes 1048608 | tf_op jit(solution)/shard_map/ppermute | solution.py:79
  894.8 20.3 %attend_back.1 = (bf16[1024,512]{1,0:T(8,128)(2,1)S(1)}, f32[4,1024,64]{2,1,0:T(8,128)S(1)}, bf16[1024,1024]{1,0:T(8,128)(2,1)S(1)}, f32[1024,64]{1,0:T(8,128)S(1)}) custom-call(bf16[1024,512]{1,0:T(8,128)(2,1)S(1)} %copy-done.8, bf16[4,1024,64]{2,1,0:T(8,128)(2,1)S(1)} %copy-done.4, bf16[1024,1024]{1,0:T(8,128)(2,1)S(1)} %copy-done.6, ...), custom_call_target="tpu_custom_call" | custom-call | tf_op jit(solution)/shard_map/attend_back/pallas_call | solution.py:289
  960.0 11.7 fusion.4
  979.4 30.0 %collective-permute-done.98 = bf16[3,88,2048]{2,1,0:T(8,128)(2,1)S(1)} collective-permute-done((bf16[3,88,2048]{2,1,0:T(8,128)(2,1)S(1)}, bf16[3,88,2048]{2,1,0:T(8,128)(2,1)S(1)}, u32[]{:S(2)}, u32[]{:S(2)}) %collective-permute-start.98) | collective-permute-done | bytes 1081376 | tf_op jit(solution)/shard_map/ppermute | solution.py:84
  1036.8 28.1 %collective-permute-done.90 = bf16[1024,576]{0,1:T(8,128)(2,1)} collective-permute-done((bf16[1024,576]{0,1:T(8,128)(2,1)S(1)}, bf16[1024,576]{0,1:T(8,128)(2,1)}, u32[]{:S(2)}, u32[]{:S(2)}) %collective-permute-start.90) | collective-permute-done | bytes 1179680 | tf_op jit(solution)/shard_map/ppermute | solution.py:79
  1118.2 10.8 collective-permute-done.95
  1131.2 12.7 %all-to-all-start.1 = ((f32[32,1,1169]{2,1,0:T(1,128)}), f32[32,1,1169]{2,1,0:T(1,128)S(1)}, u32[]{:S(2)}, u32[]{:S(2)}) async-start(f32[32,1,1169]{2,1,0:T(1,128)} %copy.352), calls=%async_computation.1 | async-start | bytes 327680 | tf_op jit(solution)/shard_map/all_to_all | solution.py:201
  1146.4 18.6 %collective-permute-done.96 = bf16[2,4,200,128]{3,2,1,0:T(8,128)(2,1)S(1)} collective-permute-done((bf16[2,4,200,128]{3,2,1,0:T(8,128)(2,1)S(1)}, bf16[2,4,200,128]{3,2,1,0:T(8,128)(2,1)S(1)}, u32[]{:S(2)}, u32[]{:S(2)}) %collective-permute-start.96) | collective-permute-done | bytes 409632 | tf_op jit(solution)/shard_map/ppermute | solution.py:95
  1168.2 9.9 collective-permute-start.97
  1204.2 11.7 fusion.3
  1215.9 10.6 fusion.2
  (742 shorter events, 542.4 us)
Async XLA Ops:
  7.2 68.2 %collective-permute-start = (bf16[256,2048]{1,0:T(8,128)(2,1)}, bf16[256,2048]{1,0:T(8,128)(2,1)}, u32[]{:S(2)}, u32[]{:S(2)}) collective-permute-start(bf16[256,2048]{1,0:T(8,128)(2,1)} %bitcast.337), channel_id=1, source_target_pairs={{0,16},{8,24},{16,0},{24,8},{1,17},{9,25},{17,1},{25,9},{2,18},{10... | collective-permute-start | bytes 3145736 | tf_op jit(solution)/shard_map/ppermute | solution.py:79
  23.3 80.4 %all-to-all-start = ((bf16[8,176,256]{2,1,0:T(8,128)(2,1)}), bf16[8,176,256]{2,1,0:T(8,128)(2,1)}, u32[]{:S(2)}, u32[]{:S(2)}) async-start(bf16[8,176,256]{2,1,0:T(8,128)(2,1)} %bitcast.8), calls=%async_computation | async-start | bytes 1441792 | tf_op jit(solution)/shard_map/all_to_all | solution.py:721
  28.1 302.2 %all-gather.7.cloned.1.call-start = ((), (), s32[]{:S(2)}) async-start(), calls=%async_computation.4 | async-start | bytes 25952256 | tf_op jit(solution)/shard_map/all_gather | solution.py:90
  40.7 43.9 %collective-permute-start.14 = (bf16[64,2048]{1,0:T(8,128)(2,1)}, bf16[64,2048]{1,0:T(8,128)(2,1)}, u32[]{:S(2)}, u32[]{:S(2)}) collective-permute-start(bf16[64,2048]{1,0:T(8,128)(2,1)} %get-tuple-element.342), channel_id=1, source_target_pairs={{0,2},{1,6},{10,10},{11,14},{20,18},{21,22},{30,26},{31,30}} | collective-permute-start | bytes 786440 | tf_op jit(solution)/shard_map/ppermute | solution.py:709
  49.2 840.3 %all-gather.9.cloned.1.call-start = ((), (), s32[]{:S(2)}) async-start(), calls=%async_computation.5 | async-start | bytes 8650752 | tf_op jit(solution)/shard_map/all_gather | solution.py:90
  75.4 39.8 %collective-permute-start.9 = (bf16[512,1024]{1,0:T(8,128)(2,1)}, bf16[512,1024]{1,0:T(8,128)(2,1)}, u32[]{:S(2)}, u32[]{:S(2)}) collective-permute-start(bf16[512,1024]{1,0:T(8,128)(2,1)} %get-tuple-element.343), channel_id=1, source_target_pairs={{0,2},{1,3},{2,4},{3,5},{4,6},{5,7},{6,0},{7,1},{8,10},{9,11},{10,... | collective-permute-start | bytes 3145736 | tf_op jit(solution)/shard_map/ppermute | solution.py:95
  84.6 82.7 %collective-permute-start.1 = (bf16[512,2048]{1,0:T(8,128)(2,1)S(1)}, bf16[512,2048]{1,0:T(8,128)(2,1)}, u32[]{:S(2)}, u32[]{:S(2)}) collective-permute-start(bf16[512,2048]{1,0:T(8,128)(2,1)S(1)} %constant_dynamic-update-slice_fusion.16), channel_id=1, source_target_pairs={{0,8},{8,0},{16,24},{24,16},{1,9},{9,1},{17,25},{25,17},{2,10},{10... | collective-permute-start | bytes 6291464 | tf_op jit(solution)/shard_map/ppermute | solution.py:74
  115.1 47.4 %collective-permute-start.17 = (bf16[264,2048]{1,0:T(8,128)(2,1)S(1)}, bf16[264,2048]{1,0:T(8,128)(2,1)S(1)}, u32[]{:S(2)}, u32[]{:S(2)}) collective-permute-start(bf16[264,2048]{1,0:T(8,128)(2,1)S(1)} %pad_maximum_fusion.9), channel_id=1, source_target_pairs={{0,1},{1,0},{2,3},{3,2},{4,5},{5,4},{6,7},{7,6},{8,9},{9,8},{10,11... | collective-permute-start | bytes 3244040 | tf_op jit(solution)/shard_map/ppermute | solution.py:84
  115.2 49.2 %collective-permute-start.10 = (bf16[512,1024]{1,0:T(8,128)(2,1)}, bf16[512,1024]{1,0:T(8,128)(2,1)}, u32[]{:S(2)}, u32[]{:S(2)}) collective-permute-start(bf16[512,1024]{1,0:T(8,128)(2,1)} %collective-permute-done.9), channel_id=1, source_target_pairs={{0,2},{1,3},{2,4},{3,5},{4,6},{5,7},{6,0},{7,1},{8,10},{9,11},{10,... | collective-permute-start | bytes 3145736 | tf_op jit(solution)/shard_map/ppermute | solution.py:95
  122.8 51.8 %collective-permute-start.7 = (bf16[1024,640]{1,0:T(8,128)(2,1)S(1)}, bf16[1024,640]{1,0:T(8,128)(2,1)S(1)}, u32[]{:S(2)}, u32[]{:S(2)}) collective-permute-start(bf16[1024,640]{1,0:T(8,128)(2,1)S(1)} %constant_dynamic-update-slice_fusion.10), channel_id=1, source_target_pairs={{0,8},{8,0},{16,24},{24,16},{1,9},{9,1},{17,25},{25,17},{2,10},{10... | collective-permute-start | bytes 3932168 | tf_op jit(solution)/shard_map/ppermute | solution.py:74
  392.1 44.6 %collective-permute-start.33 = (bf16[256,2048]{1,0:T(8,128)(2,1)}, bf16[256,2048]{1,0:T(8,128)(2,1)}, u32[]{:S(2)}, u32[]{:S(2)}) collective-permute-start(bf16[256,2048]{1,0:T(8,128)(2,1)} %get-tuple-element.334), channel_id=1, source_target_pairs={{0,16},{8,24},{16,0},{24,8},{1,17},{9,25},{17,1},{25,9},{2,18},{10... | collective-permute-start | bytes 3145736 | tf_op jit(solution)/shard_map/ppermute | solution.py:79
  418.5 51.0 %collective-permute-start.42 = (bf16[256,2048]{1,0:T(8,128)(2,1)}, bf16[256,2048]{1,0:T(8,128)(2,1)}, u32[]{:S(2)}, u32[]{:S(2)}) collective-permute-start(bf16[256,2048]{1,0:T(8,128)(2,1)} %get-tuple-element.123), channel_id=1, source_target_pairs={{0,8},{8,0},{16,24},{24,16},{1,9},{9,1},{17,25},{25,17},{2,10},{10... | collective-permute-start | bytes 3145736 | tf_op jit(solution)/shard_map/ppermute | solution.py:74
  476.3 45.9 %collective-permute-start.52 = (bf16[256,2048]{1,0:T(8,128)(2,1)S(1)}, bf16[256,2048]{1,0:T(8,128)(2,1)S(1)}, u32[]{:S(2)}, u32[]{:S(2)}) collective-permute-start(bf16[256,2048]{1,0:T(8,128)(2,1)S(1)} %copy-done.87), channel_id=1, source_target_pairs={{0,16},{8,24},{16,0},{24,8},{1,17},{9,25},{17,1},{25,9},{2,18},{10... | collective-permute-start | bytes 3145736 | tf_op jit(solution)/shard_map/ppermute | solution.py:79
  555.4 55.5 %collective-permute-start.55 = (bf16[256,2048]{1,0:T(8,128)(2,1)}, bf16[256,2048]{1,0:T(8,128)(2,1)}, u32[]{:S(2)}, u32[]{:S(2)}) collective-permute-start(bf16[256,2048]{1,0:T(8,128)(2,1)} %collective-permute-done.54.refs_0_), channel_id=1, source_target_pairs={{0,8},{8,0},{16,24},{24,16},{1,9},{9,1},{17,25},{25,17},{2,10},{10... | collective-permute-start | bytes 3145736 | tf_op jit(solution)/shard_map/ppermute | solution.py:74
  577.7 64.3 %collective-permute-start.67 = (bf16[256,2048]{1,0:T(8,128)(2,1)}, bf16[256,2048]{1,0:T(8,128)(2,1)}, u32[]{:S(2)}, u32[]{:S(2)}) collective-permute-start(bf16[256,2048]{1,0:T(8,128)(2,1)} %collective-permute-done.65.refs_0_), channel_id=1, source_target_pairs={{0,16},{8,24},{16,0},{24,8},{1,17},{9,25},{17,1},{25,9},{2,18},{10... | collective-permute-start | bytes 3145736 | tf_op jit(solution)/shard_map/ppermute | solution.py:79
  578.3 63.8 %collective-permute-start.73 = (bf16[256,2048]{1,0:T(8,128)(2,1)}, bf16[256,2048]{1,0:T(8,128)(2,1)}, u32[]{:S(2)}, u32[]{:S(2)}) collective-permute-start(bf16[256,2048]{1,0:T(8,128)(2,1)} %collective-permute-done.65.refs_0_), channel_id=1, source_target_pairs={{0,2},{1,3},{2,4},{3,5},{4,6},{5,7},{6,0},{7,1},{8,10},{9,11},{10,... | collective-permute-start | bytes 3145736 | tf_op jit(solution)/shard_map/ppermute | solution.py:95
  644.7 72.9 %collective-permute-start.63 = (bf16[256,2176]{1,0:T(8,128)(2,1)}, bf16[256,2176]{1,0:T(8,128)(2,1)}, u32[]{:S(2)}, u32[]{:S(2)}) collective-permute-start(bf16[256,2176]{1,0:T(8,128)(2,1)} %get-tuple-element.145), channel_id=1, source_target_pairs={{0,8},{8,0},{16,24},{24,16},{1,9},{9,1},{17,25},{25,17},{2,10},{10... | collective-permute-start | bytes 3342344 | tf_op jit(solution)/shard_map/ppermute | solution.py:74
  684.3 121.2 %collective-permute-start.83 = (bf16[256,2176]{1,0:T(8,128)(2,1)}, bf16[256,2176]{1,0:T(8,128)(2,1)}, u32[]{:S(2)}, u32[]{:S(2)}) collective-permute-start(bf16[256,2176]{1,0:T(8,128)(2,1)} %get-tuple-element.163), channel_id=1, source_target_pairs={{0,8},{8,0},{16,24},{24,16},{1,9},{9,1},{17,25},{25,17},{2,10},{10... | collective-permute-start | bytes 3342344 | tf_op jit(solution)/shard_map/ppermute | solution.py:74
  723.6 81.8 %collective-permute-start.82 = (bf16[256,2176]{1,0:T(8,128)(2,1)}, bf16[256,2176]{1,0:T(8,128)(2,1)}, u32[]{:S(2)}, u32[]{:S(2)}) collective-permute-start(bf16[256,2176]{1,0:T(8,128)(2,1)} %add_convert_fusion), channel_id=1, source_target_pairs={{0,16},{8,24},{16,0},{24,8},{1,17},{9,25},{17,1},{25,9},{2,18},{10... | collective-permute-start | bytes 3342344 | tf_op jit(solution)/shard_map/ppermute | solution.py:79
  745.5 47.0 %collective-permute-start.78 = (bf16[256,2176]{1,0:T(8,128)(2,1)}, bf16[256,2176]{1,0:T(8,128)(2,1)}, u32[]{:S(2)}, u32[]{:S(2)}) collective-permute-start(bf16[256,2176]{1,0:T(8,128)(2,1)} %add_convert_fusion.2), channel_id=1, source_target_pairs={{0,16},{8,24},{16,0},{24,8},{1,17},{9,25},{17,1},{25,9},{2,18},{10... | collective-permute-start | bytes 3342344 | tf_op jit(solution)/shard_map/ppermute | solution.py:79
  750.5 42.0 %collective-permute-start.72 = (bf16[256,2176]{1,0:T(8,128)(2,1)}, bf16[256,2176]{1,0:T(8,128)(2,1)}, u32[]{:S(2)}, u32[]{:S(2)}) collective-permute-start(bf16[256,2176]{1,0:T(8,128)(2,1)} %add_convert_fusion.3), channel_id=1, source_target_pairs={{0,2},{1,3},{2,4},{3,5},{4,6},{5,7},{6,0},{7,1},{8,10},{9,11},{10,... | collective-permute-start | bytes 3342344 | tf_op jit(solution)/shard_map/ppermute | solution.py:95
  758.2 446.0 %all-gather.11.cloned.1.call-start = ((), (), s32[]{:S(2)}) async-start(), calls=%async_computation.6 | async-start | bytes 17301504 | tf_op jit(solution)/shard_map/all_gather | solution.py:90
  933.0 87.9 %collective-permute-start.89 = (bf16[1024,576]{0,1:T(8,128)(2,1)}, bf16[1024,576]{0,1:T(8,128)(2,1)}, u32[]{:S(2)}, u32[]{:S(2)}) collective-permute-start(bf16[1024,576]{0,1:T(8,128)(2,1)} %copy.348), channel_id=1, source_target_pairs={{0,8},{8,0},{16,24},{24,16},{1,9},{9,1},{17,25},{25,17},{2,10},{10... | collective-permute-start | bytes 3538952 | tf_op jit(solution)/shard_map/ppermute | solution.py:74
  943.2 162.4 %collective-permute-start.88 = (bf16[256,2048]{1,0:T(8,128)(2,1)}, bf16[256,2048]{1,0:T(8,128)(2,1)}, u32[]{:S(2)}, u32[]{:S(2)}) collective-permute-start(bf16[256,2048]{1,0:T(8,128)(2,1)} %get-tuple-element.304), channel_id=1, source_target_pairs={{0,8},{8,0},{16,24},{24,16},{1,9},{9,1},{17,25},{25,17},{2,10},{10... | collective-permute-start | bytes 3145736 | tf_op jit(solution)/shard_map/ppermute | solution.py:74
  958.1 75.6 %collective-permute-start.91 = (bf16[2,2560,128]{2,1,0:T(8,128)(2,1)}, bf16[2,2560,128]{2,1,0:T(8,128)(2,1)}, u32[]{:S(2)}, u32[]{:S(2)}) collective-permute-start(bf16[2,2560,128]{2,1,0:T(8,128)(2,1)} %dynamic-slice_bitcast_fusion.2), channel_id=1, source_target_pairs={{0,2},{1,3},{2,4},{3,5},{4,6},{5,7},{6,0},{7,1},{8,10},{9,11},{10,... | collective-permute-start | bytes 3932168 | tf_op jit(solution)/shard_map/ppermute | solution.py:95
  959.9 49.5 %collective-permute-start.98 = (bf16[3,88,2048]{2,1,0:T(8,128)(2,1)S(1)}, bf16[3,88,2048]{2,1,0:T(8,128)(2,1)S(1)}, u32[]{:S(2)}, u32[]{:S(2)}) collective-permute-start(bf16[3,88,2048]{2,1,0:T(8,128)(2,1)S(1)} %fusion.47), channel_id=1, source_target_pairs={{0,1},{1,0},{2,3},{3,2},{4,5},{5,4},{6,7},{7,6},{8,9},{9,8},{10,11... | collective-permute-start | bytes 3244040 | tf_op jit(solution)/shard_map/ppermute | solution.py:84
  979.4 126.1 %collective-permute-start.87 = (bf16[256,2048]{1,0:T(8,128)(2,1)}, bf16[256,2048]{1,0:T(8,128)(2,1)}, u32[]{:S(2)}, u32[]{:S(2)}) collective-permute-start(bf16[256,2048]{1,0:T(8,128)(2,1)} %add_convert_fusion.7), channel_id=1, source_target_pairs={{0,16},{8,24},{16,0},{24,8},{1,17},{9,25},{17,1},{25,9},{2,18},{10... | collective-permute-start | bytes 3145736 | tf_op jit(solution)/shard_map/ppermute | solution.py:79
  1016.7 114.5 %all-to-all-start.3 = ((bf16[32,176,64]{1,2,0:T(8,128)(2,1)}), bf16[32,176,64]{1,2,0:T(8,128)(2,1)}, u32[]{:S(2)}, u32[]{:S(2)}) async-start(bf16[32,176,64]{1,2,0:T(8,128)(2,1)} %reshape.633), calls=%async_computation.3 | async-start | bytes 2097152 | tf_op jit(solution)/shard_map/all_to_all | solution.py:977
  1029.2 83.5 %collective-permute-start.99 = (bf16[88,2048]{1,0:T(8,128)(2,1)}, bf16[88,2048]{1,0:T(8,128)(2,1)}, u32[]{:S(2)}, u32[]{:S(2)}) collective-permute-start(bf16[88,2048]{1,0:T(8,128)(2,1)} %slice_bitcast_fusion.1), channel_id=1, source_target_pairs={{0,0},{1,4},{2,8},{3,12},{4,16},{5,20},{6,24},{7,28},{8,1},{9,5},{... | collective-permute-start | bytes 1081352 | tf_op jit(solution)/shard_map/ppermute | solution.py:975
  1036.8 78.1 %collective-permute-start.92 = (bf16[2,2560,128]{2,1,0:T(8,128)(2,1)}, bf16[2,2560,128]{2,1,0:T(8,128)(2,1)}, u32[]{:S(2)}, u32[]{:S(2)}) collective-permute-start(bf16[2,2560,128]{2,1,0:T(8,128)(2,1)} %fusion.26), channel_id=1, source_target_pairs={{0,2},{1,3},{2,4},{3,5},{4,6},{5,7},{6,0},{7,1},{8,10},{9,11},{10,... | collective-permute-start | bytes 3932168 | tf_op jit(solution)/shard_map/ppermute | solution.py:95
  1118.2 46.9 %collective-permute-start.93 = (bf16[2,2560,128]{2,1,0:T(8,128)(2,1)}, bf16[2,2560,128]{2,1,0:T(8,128)(2,1)}, u32[]{:S(2)}, u32[]{:S(2)}) collective-permute-start(bf16[2,2560,128]{2,1,0:T(8,128)(2,1)} %fusion.25), channel_id=1, source_target_pairs={{0,2},{1,3},{2,4},{3,5},{4,6},{5,7},{6,0},{7,1},{8,10},{9,11},{10,... | collective-permute-start | bytes 3932168 | tf_op jit(solution)/shard_map/ppermute | solution.py:95
  1131.2 58.8 %all-to-all-start.1 = ((f32[32,1,1169]{2,1,0:T(1,128)}), f32[32,1,1169]{2,1,0:T(1,128)S(1)}, u32[]{:S(2)}, u32[]{:S(2)}) async-start(f32[32,1,1169]{2,1,0:T(1,128)} %copy.352), calls=%async_computation.1 | async-start | bytes 327680 | tf_op jit(solution)/shard_map/all_to_all | solution.py:201
  (211 other events, 3228.1 us)
Sparse Core Ops, SparseCore 0:
  49.3 235.9 all-gather.6
  758.4 74.8 all-gather.8
  861.0 161.3 all-gather.10

commit v3 on v2

--- a/solution.py
+++ b/solution.py
@@ -126,9 +126,12 @@
     return ((ctx // 2 - dx + chips) % chips) * 2 + (ctx % 2 + dc) % 2
 
 
-def sum_ctx(value):
-    total = value.astype(f32) + core_swap(value.astype(bf16)).astype(f32)
-    moving = total.astype(bf16)
+def sum_cores(value):
+    return (value.astype(f32) + core_swap(value.astype(bf16)).astype(f32)).astype(bf16)
+
+
+def sum_chips(moving):
+    total = moving.astype(f32)
     for _ in range(lax.axis_size("ctx") // 2 - 1):
         moving = x_shift(moving)
         total = total + moving.astype(f32)
@@ -202,7 +205,7 @@
     return jnp.sum(value, axis=0)
 
 
-def ring_shard(full, each=None):
+def ring_shard(full, each):
     ring = lax.axis_size("shard") // 2
     me = lax.axis_index("shard") // 2
     full = full.reshape((ring, 2) + full.shape[1:])
@@ -713,19 +716,20 @@
 
     slice_rows = shared_down.shape[0] // ctx_count
     down_own = lax.dynamic_slice_in_dim(shared_down, ctx * slice_rows, slice_rows, 0)
+    down_other = half_swap(down_own)
     both = jnp.stack([shared_gate, shared_up], 0).reshape(
-        2, depth, shard_count, ctx_count, slice_rows
-    )
-    both = lax.dynamic_index_in_dim(both, ctx, 3, False)
-    both = both.transpose(2, 0, 3, 1).reshape(shard_count, 2 * slice_rows, depth)
+        2, depth, ring, 2, ctx_count, slice_rows
+    )
+    both = lax.dynamic_index_in_dim(both, ctx, 4, False).transpose(2, 3, 0, 4, 1)
+    both = jnp.stack([both, both[:, ::-1]], 1)
+    both = both.reshape(shard_count, 4 * slice_rows, depth)
     both = lax.all_to_all(both, "shard", split_axis=0, concat_axis=0, tiled=True)
-    both = both.transpose(1, 0, 2).reshape(2 * slice_rows, width)
-    slices = jnp.concatenate([both, down_own], 0)
-    slices = jnp.stack([slices, half_swap(slices)], 0).reshape(2, 3, slice_rows, width)
-    shared_all = [slices[:, i].reshape(2 * slice_rows, width) for i in range(3)]
+    both = both.transpose(1, 0, 2).reshape(2, 2, slice_rows, width)
+    shared_all = [both[:, i].reshape(2 * slice_rows, width) for i in range(2)]
+    shared_all.append(jnp.concatenate([down_own, down_other], 0))
 
     small = gather_shard_from(both_of(small, half_swap(small), half_bit))
-    small = after(small, both)
+    small = after(small, both, down_other)
     small = gather_ctx_rows(small).reshape(ctx_count, shard_count, part, -1)
     latent_cols = LAT + DR
     small_gains = small[..., latent_cols : latent_cols + 3].transpose(3, 1, 0, 2)
@@ -744,7 +748,7 @@
     rope_proj = gathered[:, plain_cols : plain_cols + rope_cols]
     packed = gathered[:, : plain_cols + rope_cols]
     latent_up = gathered[:, plain_cols + rope_cols :].reshape(LAT, own_pairs)
-    out_proj = gather_shard_from(after(out_pair, gathered, slices))
+    out_proj = gather_shard_from(after(out_pair, gathered))
 
     source = tokens[0].astype(f32)
     factor_attn = inverse_root(source)
@@ -861,13 +865,20 @@
         terms.append(scatter_x(pairs_of))
     d_all = ring_sum(terms, q_shift)
     for_other = [item.astype(bf16) for item in half_grads(1)]
-    from_other = [both_halves(for_other[0]), both_halves(jnp.stack(for_other[1:], 0))]
+    d_slices = jnp.stack([sum(item[i] for item in d_shared) for i in range(3)], 0)
+    d_slices = d_slices.reshape(3, 2, slice_rows, width)
+    found = half_swap(d_slices[:, 1].astype(bf16))
+    d_slices = (d_slices[:, 0] + found.astype(f32)).astype(bf16)
+    from_other = [
+        both_halves(for_other[0]),
+        both_halves(after(jnp.stack(for_other[1:], 0), found)),
+    ]
+
     d_ffn = d_all[:, :width]
     d_info = d_all[:, width:]
     d_router = d_info[:, :experts] + d_info[:, experts : 2 * experts]
     d_router = jnp.where(chosen_any, d_router, 0.0)
 
-    d_slices = jnp.stack([sum(item[i] for item in d_shared) for i in range(3)], 0)
     d_logits = (router * (d_router - jnp.sum(router * d_router, axis=-1, keepdims=True))).astype(
         bf16
     )
@@ -884,7 +895,8 @@
         query, query_rope, pairs, key_rope, d_heads, scale
     )
     d_latent_sum = jnp.concatenate([mm_nt(d_pairs, latent_up), d_key_rope], 1).astype(bf16)
-    d_latent = sum_ctx(d_latent_sum)
+    d_latent_cores = sum_cores(d_latent_sum)
+    d_latent = sum_chips(d_latent_cores)
     d_rope = rotate_back(d_rope, cosine, sine).astype(bf16)
     d_rope = d_rope.transpose(1, 0, 2).reshape(seq_len, rope_cols)
     d_query = after(jnp.concatenate([d_query, d_rope], 1), d_latent_sum)
@@ -904,7 +916,7 @@
     )
     d_packed = mm_tn(attn_in, d_query).astype(bf16)
     d_attn_in = scatter_ctx(
-        mm_nt(after(d_query, d_packed), packed).astype(bf16)
+        mm_nt(after(d_query, d_packed, d_latent_cores), packed).astype(bf16)
     ) + mm_nt(lax.dynamic_slice_in_dim(d_latent_raw, first, rows, 0), latent_down)
     d_latent_up = mm_tn(latent, d_pairs)
     d_source_norm, d_gain_attn = norm_back(source, factor_attn, gain_attn, d_attn_in)
@@ -914,65 +926,21 @@
         cols = value.shape[1]
         return value.astype(bf16).reshape(ctx_count, shard_count, -1, cols).transpose(1, 0, 2, 3)
 
-    d_latent_in = by_rows(mm_tn(attn_in, d_latent_all))
-    d_latent_out = by_rows(d_latent_up)
-    latent_shape = d_latent_in.shape
-    d_latents = jnp.concatenate(
-        [d_latent_in.reshape(latent_shape[:2] + (-1,)), d_latent_out.reshape(latent_shape[:2] + (-1,))],
-        2,
-    ).reshape(shard_count, ctx_count, -1, LANES)
-
     early = jnp.concatenate(
         [
             d_out_proj.reshape(shard_count, -1, LANES),
             by_rows(d_packed).reshape(shard_count, -1, LANES),
+            by_rows(d_latent_up).reshape(shard_count, -1, LANES),
         ],
         1,
     )
-    sum_early = ring_shard(early)
-    sum_latents = ring_shard(d_latents)
-    sums = [sum_early, sum_latents]
-    flat = jnp.concatenate([item.astype(bf16).reshape(2, -1, LANES) for item in sums], 1)
-    flat = swap_halves(flat)
-    out_rows = d_out_proj.size // (shard_count * LANES)
-    g_attn_out = flat[:out_rows].reshape(piece, width)
-    flat = flat[out_rows:].astype(bf16)
-    packed_rows = d_packed.size // (shard_count * LANES)
-    flat = jnp.concatenate(
-        [
-            flat[:packed_rows].reshape(ctx_count, -1, LANES),
-            flat[packed_rows:].reshape(ctx_count, -1, LANES),
-        ],
-        1,
-    )
-    flat = lax.all_to_all(flat, "ctx", split_axis=0, concat_axis=0, tiled=True).astype(f32)
-    packed_rows = packed_rows // ctx_count
-    g_packed = flat[:, :packed_rows].reshape(ctx_count, piece, -1)
-    g_plain = g_packed[..., :plain_cols].reshape(ctx_count, piece, own_heads, DN)
-    g_rope = g_packed[..., plain_cols:].reshape(ctx_count, piece, own_heads, DR)
-    g_query = jnp.concatenate([g_plain, g_rope], -1).transpose(1, 0, 2, 3).reshape(piece, -1)
-    g_latents = flat[:, packed_rows:].reshape(ctx_count, -1)
-    g_latent_in = g_latents[:, : piece * latent_cols].reshape(ctx_count, piece, latent_cols)
-    g_latent_in = g_latent_in.transpose(1, 0, 2).reshape(piece, -1)
-    g_latent_out = g_latents[:, piece * latent_cols :].reshape(ctx_count, LAT // devices, -1)
-    g_latent_out = g_latent_out.transpose(1, 0, 2).reshape(LAT // devices, -1)
-
     from_other = [
         lax.dynamic_index_in_dim(after(item, late), 1 - half_bit, 0, False)
-        for item, late in zip(from_other, (d_packed, d_latents))
+        for item, late in zip(from_other, (d_packed, d_packed))
     ]
     from_other = [from_other[0], from_other[1][0], from_other[1][1]]
     d_expert = [item + other.astype(f32) for item, other in zip(half_grads(0), from_other)]
-    d_expert = [d_expert[0].T, d_expert[1].T, d_expert[2]]
-
-    moves = []
-    for a in range(ctx_count):
-        for b in range(shard_count):
-            moves.append((a * shard_count + b, b * ctx_count + a))
-    d_slices = after(d_slices, d_heads).reshape(3, 2, slice_rows, width)
-    d_slices = d_slices[:, 0] + half_swap(d_slices[:, 1].astype(bf16)).astype(f32)
-    d_slices = after(d_slices.astype(bf16), d_packed)
-    g_down = lax.ppermute(d_slices[2], ("ctx", "shard"), moves)
+
     d_both = d_slices[:2].reshape(2, slice_rows, devices, piece)
     d_both = lax.all_to_all(
         d_both.transpose(2, 0, 1, 3).reshape(devices, 2 * slice_rows, piece),
@@ -981,9 +949,53 @@
         concat_axis=0,
         tiled=True,
     )
-    g_down = after(g_down, d_latents).astype(f32)
-    d_both = after(d_both, d_latents)
-    d_both = d_both.reshape(ctx_count, shard_count, 2, slice_rows, piece)
+    sum_early = ring_shard(
+        early, lambda place, total: total if place else after(total, d_both)
+    )
+    d_latent_in = mm_tn(attn_in, d_latent_all).astype(bf16)
+    latent_terms = d_latent_in.reshape(ctx_count, ring, 2, piece, latent_cols)
+    sum_latents = ring_sum(
+        [
+            lax.dynamic_index_in_dim(latent_terms, (shard // 2 - dq + ring) % ring, 1, False)
+            for dq in range(ring)
+        ],
+        q_shift,
+    )
+    sum_latents = swap_halves(sum_latents.transpose(1, 0, 2, 3)).astype(bf16)
+    flat = swap_halves(sum_early).astype(bf16)
+    out_rows = d_out_proj.size // (shard_count * LANES)
+    packed_rows = d_packed.size // (shard_count * LANES)
+    g_attn_out = flat[:out_rows].astype(f32).reshape(piece, width)
+    flat = jnp.concatenate(
+        [
+            flat[out_rows : out_rows + packed_rows].reshape(ctx_count, -1, LANES),
+            flat[out_rows + packed_rows :].reshape(ctx_count, -1, LANES),
+            sum_latents.reshape(ctx_count, -1, LANES),
+        ],
+        1,
+    )
+    packed_rows = packed_rows // ctx_count
+    up_rows = d_latent_up.size // (shard_count * ctx_count * LANES)
+    flat = lax.all_to_all(flat, "ctx", split_axis=0, concat_axis=0, tiled=True).astype(f32)
+    g_packed = flat[:, :packed_rows].reshape(ctx_count, piece, -1)
+    g_plain = g_packed[..., :plain_cols].reshape(ctx_count, piece, own_heads, DN)
+    g_rope = g_packed[..., plain_cols:].reshape(ctx_count, piece, own_heads, DR)
+    g_query = jnp.concatenate([g_plain, g_rope], -1).transpose(1, 0, 2, 3).reshape(piece, -1)
+    g_latent_out = flat[:, packed_rows : packed_rows + up_rows]
+    g_latent_out = g_latent_out.reshape(ctx_count, LAT // devices, -1)
+    g_latent_out = g_latent_out.transpose(1, 0, 2).reshape(LAT // devices, -1)
+    g_latent_in = flat[:, packed_rows + up_rows :].reshape(ctx_count, piece, latent_cols)
+    g_latent_in = g_latent_in.transpose(1, 0, 2).reshape(piece, -1)
+
+    d_expert = [d_expert[0].T, d_expert[1].T, d_expert[2]]
+
+    moves = []
+    for a in range(ctx_count):
+        for b in range(shard_count):
+            moves.append((a * shard_count + b, b * ctx_count + a))
+    g_down = lax.ppermute(after(d_slices[2], d_packed), ("ctx", "shard"), moves)
+    g_down = after(g_down, sum_early).astype(f32)
+    d_both = after(d_both, d_attn_in).reshape(ctx_count, shard_count, 2, slice_rows, piece)
     d_both = d_both.transpose(2, 4, 1, 0, 3).reshape(2, piece, -1).astype(f32)
     g_gate = d_both[0]
     g_up = d_both[1]

time: 1250 us -> 1190 us (0.952)
  waiting for transfers between devices: 433 us -> 344 us
  starting transfers between devices: 115 us -> 142 us
    ppermute x22, waiting for transfers between devices: 204 us -> 155 us  [x_shift(): lax.ppermute(value, 'ctx', [(i, (i + 2) % count) for i in range(count)])]
    ppermute x6 -> x7, waiting for transfers between devices: 71.4 us -> 26 us  [half_swap(): return lax.ppermute(value, 'shard', [(i, i ^ 1) for i in range(count)])]
    ppermute x6 -> x7, starting transfers between devices: 13.6 us -> 37.8 us  [half_swap(): return lax.ppermute(value, 'shard', [(i, i ^ 1) for i in range(count)])]
    ppermute x27, starting transfers between devices: 12.6 us -> 27.6 us  [q_shift(): lax.ppermute(value, 'shard', [(i, (i + 2) % count) for i in range(count)])]
    ppermute x22, starting transfers between devices: 38.6 us -> 25.5 us  [x_shift(): lax.ppermute(value, 'ctx', [(i, (i + 2) % count) for i in range(count)])]
    unnamed x287 -> x290, local copies, waits for them, and re-layouts: 44 us -> 43.8 us
  transfers between devices with their start and end apart: 107 -> 108, of which waited for: 33 -> 33; matrix products, arithmetic and copies ran while one was open for 31% -> 32% of each run, Pallas kernels for 20% -> 21%
where the time goes in v3:
time: 1190 us; the launch traced here: 1180 us
  waiting for transfers between devices  344 us (29%)
  Pallas kernels  247 us (21%)
  local copies, waits for them, and re-layouts  170 us (14%)
  other arithmetic  152 us (13%)
  starting transfers between devices  142 us (12%)
  matrix products  105 us (9%)
  between operations  18.4 us (2%)
    pallas_call x8, Pallas kernels, moe_call(): pl.pallas_call(functools.partial(kernel, dims + (len(before),)), in_specs...  215 us
    ppermute x22, waiting for transfers between devices, x_shift(): lax.ppermute(value, 'ctx', [(i, (i + 2) % count) for i in range(count)])  155 us
    ppermute x27, waiting for transfers between devices, q_shift(): lax.ppermute(value, 'shard', [(i, (i + 2) % count) for i in range(count)])  140 us
    dot_general x11, matrix products, mm_tn(): lax.dot_general(left, right, (((0,), (0,)), ((), ())), preferred_element_...  73.7 us
    convert_element_type x19, other arithmetic, ring_sum(): total = shift(total.astype(bf16)).astype(f32) + term.astype(f32)  45.8 us
    unnamed x290, local copies, waits for them, and re-layouts  43.8 us
    ppermute x7, starting transfers between devices, half_swap(): return lax.ppermute(value, 'shard', [(i, i ^ 1) for i in range(count)])  37.8 us
    ppermute x27, starting transfers between devices, q_shift(): lax.ppermute(value, 'shard', [(i, (i + 2) % count) for i in range(count)])  27.6 us
  transfers between devices with their start and end apart: 108, of which 33 were waited for; matrix products, arithmetic and copies ran while one was open for 32% of the time, Pallas kernels for 21%

profile of v3, /device:TPU:0, one launch (start us, length us, event | category | flops | bytes accessed | tf_op | source)
XLA Modules:
  0.0 1179.1 jit_solution(11668468617962463076)
XLA Ops:
  72.8 21.4 %collective-permute-start.6 = (bf16[88,2048]{1,0:T(8,128)(2,1)}, bf16[88,2048]{1,0:T(8,128)(2,1)S(1)}, u32[]{:S(2)}, u32[]{:S(2)}) collective-permute-start(bf16[88,2048]{1,0:T(8,128)(2,1)} %constant_dynamic-slice_fusion.10), channel_id=1, source_target_pairs={{0,1},{1,0},{2,3},{3,2},{4,5},{5,4},{6,7},{7,6},{8,9},{9,8},{10,11... | collective-permute-start | bytes 1081352 | tf_op jit(solution)/shard_map/ppermute | solution.py:84
  103.8 18.7 %collective-permute-done.17 = bf16[64,2048]{1,0:T(8,128)(2,1)} collective-permute-done((bf16[64,2048]{1,0:T(8,128)(2,1)}, bf16[64,2048]{1,0:T(8,128)(2,1)}, u32[]{:S(2)}, u32[]{:S(2)}) %collective-permute-start.17) | collective-permute-done | bytes 262176 | tf_op jit(solution)/shard_map/ppermute | solution.py:84
  142.8 10.3 collective-permute-start.12
  163.7 9.2 collective-permute-done.12
  225.0 11.9 %attend.1 = bf16[1024,512]{1,0:T(8,128)(2,1)S(1)} custom-call(bf16[1024,512]{1,0:T(8,128)(2,1)S(1)} %fusion.42.q_ref, bf16[4,1024,64]{2,1,0:T(8,128)(2,1)S(1)} %pad_maximum_fusion.10.r_ref, bf16[1024,1024]{1,0:T(8,128)(2,1)S(1)} %convolution_convert_fusion.8.p_ref, bf16[1024,64]{1,0:T(8,128)(2,1)S(1)} %pad_maximum_fusion.15.k_ref), custom_call_target="tpu_custom_call" | custom-call | tf_op jit(solution)/shard_map/attend/pallas_call | solution.py:278
  247.9 25.0 %collective-permute-done.22 = bf16[256,2048]{1,0:T(8,128)(2,1)} collective-permute-done((bf16[256,2048]{1,0:T(8,128)(2,1)S(1)}, bf16[256,2048]{1,0:T(8,128)(2,1)}, u32[]{:S(2)}, u32[]{:S(2)}) %collective-permute-start.22) | collective-permute-done | bytes 1048608 | tf_op jit(solution)/shard_map/ppermute | solution.py:79
  281.7 25.8 %collective-permute-done.25.refs_2_.refs_6_ = bf16[256,2176]{1,0:T(8,128)(2,1)} collective-permute-done((bf16[256,2176]{1,0:T(8,128)(2,1)}, bf16[256,2176]{1,0:T(8,128)(2,1)}, u32[]{:S(2)}, u32[]{:S(2)}) %collective-permute-start.25) | collective-permute-done | bytes 1114144 | tf_op jit(solution)/shard_map/ppermute | solution.py:79
  314.8 23.3 %moe_fwd.4 = (bf16[256,2048]{1,0:T(8,128)(2,1)}, bf16[256,2048]{1,0:T(8,128)(2,1)}, bf16[256,2048]{1,0:T(8,128)(2,1)}, bf16[256,2048]{1,0:T(8,128)(2,1)}, bf16[2...) custom-call(s32[2]{0:T(128)} %pad_add_fusion.expert_ref, ...), custom_call_target="tpu_custom_call" | custom-call | tf_op jit(solution)/shard_map/moe_fwd/pallas_call | solution.py:542
  345.1 23.1 %moe_fwd.5 = (bf16[256,2048]{1,0:T(8,128)(2,1)}, bf16[256,2048]{1,0:T(8,128)(2,1)}, bf16[256,2048]{1,0:T(8,128)(2,1)}, bf16[256,2048]{1,0:T(8,128)(2,1)}, bf16[2...) custom-call(s32[2]{0:T(128)} %after.19.expert_ref, ...), custom_call_target="tpu_custom_call", output_to_operand_aliasing={{4}: (12, {}), {5}: (13, {}), {6}: (14, {}), {7}: (15, {}),... | custom-call | tf_op jit(solution)/shard_map/moe_fwd/pallas_call | solution.py:542
  377.4 23.3 %moe_fwd.6 = (bf16[256,2048]{1,0:T(8,128)(2,1)}, bf16[256,2048]{1,0:T(8,128)(2,1)}, bf16[256,2048]{1,0:T(8,128)(2,1)}, bf16[256,2048]{1,0:T(8,128)(2,1)}, bf16[2...) custom-call(s32[2]{0:T(128)} %after.20.expert_ref, ...), custom_call_target="tpu_custom_call", output_to_operand_aliasing={{4}: (12, {}), {5}: (13, {}), {6}: (14, {}), {7}: (15, {}),... | custom-call | tf_op jit(solution)/shard_map/moe_fwd/pallas_call | solution.py:542
  401.8 17.6 %collective-permute-done.33 = bf16[256,2048]{1,0:T(8,128)(2,1)} collective-permute-done((bf16[256,2048]{1,0:T(8,128)(2,1)}, bf16[256,2048]{1,0:T(8,128)(2,1)}, u32[]{:S(2)}, u32[]{:S(2)}) %collective-permute-start.33) | collective-permute-done | bytes 1048608 | tf_op jit(solution)/shard_map/ppermute | solution.py:79
  429.3 23.2 %moe_fwd.7 = (bf16[256,2048]{1,0:T(8,128)(2,1)}, bf16[256,2048]{1,0:T(8,128)(2,1)}, bf16[256,2048]{1,0:T(8,128)(2,1)}, bf16[256,2048]{1,0:T(8,128)(2,1)}, bf16[2...) custom-call(s32[2]{0:T(128)} %after.22.expert_ref, ...), custom_call_target="tpu_custom_call", output_to_operand_aliasing={{4}: (12, {}), {5}: (13, {}), {6}: (14, {}), {7}: (15, {}),... | custom-call | tf_op jit(solution)/shard_map/moe_fwd/pallas_call | solution.py:542
  460.5 22.3 %collective-permute-done.43 = bf16[256,2048]{1,0:T(8,128)(2,1)S(1)} collective-permute-done((bf16[256,2048]{1,0:T(8,128)(2,1)S(1)}, bf16[256,2048]{1,0:T(8,128)(2,1)S(1)}, u32[]{:S(2)}, u32[]{:S(2)}) %collective-permute-start.43) | collective-permute-done | bytes 1048608 | tf_op jit(solution)/shard_map/ppermute | solution.py:95
  486.2 19.5 %collective-permute-done.52 = bf16[256,2048]{1,0:T(8,128)(2,1)S(1)} collective-permute-done((bf16[256,2048]{1,0:T(8,128)(2,1)S(1)}, bf16[256,2048]{1,0:T(8,128)(2,1)S(1)}, u32[]{:S(2)}, u32[]{:S(2)}) %collective-permute-start.52) | collective-permute-done | bytes 1048608 | tf_op jit(solution)/shard_map/ppermute | solution.py:79
  513.9 23.1 %collective-permute-done.54.refs_0_ = bf16[256,2048]{1,0:T(8,128)(2,1)} collective-permute-done((bf16[256,2048]{1,0:T(8,128)(2,1)S(1)}, bf16[256,2048]{1,0:T(8,128)(2,1)}, u32[]{:S(2)}, u32[]{:S(2)}) %collective-permute-start.54) | collective-permute-done | bytes 1048608 | tf_op jit(solution)/shard_map/ppermute | solution.py:95
  538.3 19.9 %collective-permute-done.56.refs_2_ = bf16[256,2048]{1,0:T(8,128)(2,1)} collective-permute-done((bf16[256,2048]{1,0:T(8,128)(2,1)}, bf16[256,2048]{1,0:T(8,128)(2,1)}, u32[]{:S(2)}, u32[]{:S(2)}) %collective-permute-start.56) | collective-permute-done | bytes 1048608 | tf_op jit(solution)/shard_map/ppermute | solution.py:79
  563.7 30.6 %moe_bwd.4 = (bf16[256,2176]{1,0:T(8,128)(2,1)}, bf16[256,2176]{1,0:T(8,128)(2,1)}, bf16[256,2176]{1,0:T(8,128)(2,1)}, bf16[256,2176]{1,0:T(8,128)(2,1)}, f32[17...) custom-call(s32[2]{0:T(128)} %pad_add_fusion.expert_ref, ...), custom_call_target="tpu_custom_call" | custom-call | tf_op jit(solution)/shard_map/moe_bwd/pallas_call | solution.py:542
  594.3 30.4 %moe_bwd.5 = (bf16[256,2176]{1,0:T(8,128)(2,1)}, bf16[256,2176]{1,0:T(8,128)(2,1)}, bf16[256,2176]{1,0:T(8,128)(2,1)}, bf16[256,2176]{1,0:T(8,128)(2,1)}, f32[17...) custom-call(s32[2]{0:T(128)} %pad_add_fusion.expert_ref, ...), custom_call_target="tpu_custom_call", output_to_operand_aliasing={{7}: (20, {}), {8}: (21, {}), {9}: (22, {})} | custom-call | tf_op jit(solution)/shard_map/moe_bwd/pallas_call | solution.py:542
  630.9 30.6 %moe_bwd.6 = (bf16[256,2176]{1,0:T(8,128)(2,1)}, bf16[256,2176]{1,0:T(8,128)(2,1)}, bf16[256,2176]{1,0:T(8,128)(2,1)}, bf16[256,2176]{1,0:T(8,128)(2,1)}, f32[17...) custom-call(s32[2]{0:T(128)} %pad_add_fusion.expert_ref, ...), custom_call_target="tpu_custom_call", output_to_operand_aliasing={{7}: (20, {}), {8}: (21, {}), {9}: (22, {})} | custom-call | tf_op jit(solution)/shard_map/moe_bwd/pallas_call | solution.py:542
  667.5 30.6 %moe_bwd.7 = (bf16[256,2176]{1,0:T(8,128)(2,1)}, bf16[256,2176]{1,0:T(8,128)(2,1)}, bf16[256,2176]{1,0:T(8,128)(2,1)}, bf16[256,2176]{1,0:T(8,128)(2,1)}, f32[17...) custom-call(s32[2]{0:T(128)} %pad_add_fusion.expert_ref, ...), custom_call_target="tpu_custom_call", output_to_operand_aliasing={{7}: (20, {}), {8}: (21, {}), {9}: (22, {})} | custom-call | tf_op jit(solution)/shard_map/moe_bwd/pallas_call | solution.py:542
  710.5 17.7 %collective-permute-done.70 = bf16[256,2176]{1,0:T(8,128)(2,1)S(1)} collective-permute-done((bf16[256,2176]{1,0:T(8,128)(2,1)S(1)}, bf16[256,2176]{1,0:T(8,128)(2,1)S(1)}, u32[]{:S(2)}, u32[]{:S(2)}) %collective-permute-start.70) | collective-permute-done | bytes 1114144 | tf_op jit(solution)/shard_map/ppermute | solution.py:79
  747.2 28.0 %collective-permute-done.78 = bf16[256,2176]{1,0:T(8,128)(2,1)} collective-permute-done((bf16[256,2176]{1,0:T(8,128)(2,1)}, bf16[256,2176]{1,0:T(8,128)(2,1)}, u32[]{:S(2)}, u32[]{:S(2)}) %collective-permute-start.78) | collective-permute-done | bytes 1114144 | tf_op jit(solution)/shard_map/ppermute | solution.py:79
  782.4 23.5 %collective-permute-done.80 = bf16[256,2176]{1,0:T(8,128)(2,1)S(1)} collective-permute-done((bf16[256,2176]{1,0:T(8,128)(2,1)S(1)}, bf16[256,2176]{1,0:T(8,128)(2,1)S(1)}, u32[]{:S(2)}, u32[]{:S(2)}) %collective-permute-start.80) | collective-permute-done | bytes 1114144 | tf_op jit(solution)/shard_map/ppermute | solution.py:95
  843.4 9.7 fusion.22
  856.9 12.2 %all-to-all-done.2 = bf16[32,176,64]{1,2,0:T(8,128)(2,1)} async-done(((bf16[32,176,64]{1,2,0:T(8,128)(2,1)}), bf16[32,176,64]{1,2,0:T(8,128)(2,1)}, u32[]{:S(2)}, u32[]{:S(2)}) %all-to-all-start.2) | async-done | bytes 720928 | tf_op jit(solution)/shard_map/all_to_all | solution.py:945
  889.5 20.3 %attend_back.1 = (bf16[1024,512]{1,0:T(8,128)(2,1)S(1)}, f32[4,1024,64]{2,1,0:T(8,128)S(1)}, bf16[1024,1024]{1,0:T(8,128)(2,1)S(1)}, f32[1024,64]{1,0:T(8,128)S(1)}) custom-call(bf16[1024,512]{1,0:T(8,128)(2,1)S(1)} %copy-done.8, bf16[4,1024,64]{2,1,0:T(8,128)(2,1)S(1)} %copy-done.3, bf16[1024,1024]{1,0:T(8,128)(2,1)S(1)} %copy-done.5, ...), custom_call_target="tpu_custom_call" | custom-call | tf_op jit(solution)/shard_map/attend_back/pallas_call | solution.py:292
  969.8 18.2 %collective-permute-done.91 = bf16[2,3072,128]{2,1,0:T(8,128)(2,1)} collective-permute-done((bf16[2,3072,128]{2,1,0:T(8,128)(2,1)}, bf16[2,3072,128]{2,1,0:T(8,128)(2,1)}, u32[]{:S(2)}, u32[]{:S(2)}) %collective-permute-start.91) | collective-permute-done | bytes 1572896 | tf_op jit(solution)/shard_map/ppermute | solution.py:95
  1015.5 11.7 fusion.4
  1028.1 10.3 collective-permute-done.96
  1076.8 10.2 all-to-all-start.1
  1148.0 11.6 fusion.3
  1159.6 11.7 fusion.2
  (750 shorter events, 535.9 us)
Async XLA Ops:
  7.2 63.9 %collective-permute-start = (bf16[256,2048]{1,0:T(8,128)(2,1)}, bf16[256,2048]{1,0:T(8,128)(2,1)}, u32[]{:S(2)}, u32[]{:S(2)}) collective-permute-start(bf16[256,2048]{1,0:T(8,128)(2,1)} %bitcast.312), channel_id=1, source_target_pairs={{0,16},{8,24},{16,0},{24,8},{1,17},{9,25},{17,1},{25,9},{2,18},{10... | collective-permute-start | bytes 3145736 | tf_op jit(solution)/shard_map/ppermute | solution.py:79
  15.5 39.4 %collective-permute-start.2 = (bf16[64,640]{1,0:T(8,128)(2,1)}, bf16[64,640]{1,0:T(8,128)(2,1)S(1)}, u32[]{:S(2)}, u32[]{:S(2)}) collective-permute-start(bf16[64,640]{1,0:T(8,128)(2,1)} %pad_dynamic-slice_fusion.2), channel_id=1, source_target_pairs={{0,1},{1,0},{2,3},{3,2},{4,5},{5,4},{6,7},{7,6},{8,9},{9,8},{10,11... | collective-permute-start | bytes 245768 | tf_op jit(solution)/shard_map/ppermute | solution.py:84
  23.7 103.6 %all-to-all-start = ((bf16[8,352,256]{2,1,0:T(8,128)(2,1)}), bf16[8,352,256]{2,1,0:T(8,128)(2,1)}, u32[]{:S(2)}, u32[]{:S(2)}) async-start(bf16[8,352,256]{2,1,0:T(8,128)(2,1)} %bitcast.11), calls=%async_computation | async-start | bytes 2883584 | tf_op jit(solution)/shard_map/all_to_all | solution.py:726
  28.6 286.2 %all-gather.7.cloned.1.call-start = ((), (), s32[]{:S(2)}) async-start(), calls=%async_computation.4 | async-start | bytes 25952256 | tf_op jit(solution)/shard_map/all_gather | solution.py:90
  51.8 832.3 %all-gather.9.cloned.1.call-start = ((), (), s32[]{:S(2)}) async-start(), calls=%async_computation.5 | async-start | bytes 8650752 | tf_op jit(solution)/shard_map/all_gather | solution.py:90
  54.9 39.2 %collective-permute-start.13 = (bf16[64,2048]{1,0:T(8,128)(2,1)}, bf16[64,2048]{1,0:T(8,128)(2,1)S(1)}, u32[]{:S(2)}, u32[]{:S(2)}) collective-permute-start(bf16[64,2048]{1,0:T(8,128)(2,1)} %get-tuple-element.341), channel_id=1, source_target_pairs={{0,0},{1,4},{10,8},{11,12},{20,16},{21,20},{30,24},{31,28}} | collective-permute-start | bytes 786440 | tf_op jit(solution)/shard_map/ppermute | solution.py:712
  72.7 82.8 %collective-permute-start.1 = (bf16[512,2048]{1,0:T(8,128)(2,1)S(1)}, bf16[512,2048]{1,0:T(8,128)(2,1)}, u32[]{:S(2)}, u32[]{:S(2)}) collective-permute-start(bf16[512,2048]{1,0:T(8,128)(2,1)S(1)} %constant_dynamic-update-slice_fusion.16), channel_id=1, source_target_pairs={{0,8},{8,0},{16,24},{24,16},{1,9},{9,1},{17,25},{25,17},{2,10},{10... | collective-permute-start | bytes 6291464 | tf_op jit(solution)/shard_map/ppermute | solution.py:74
  72.8 61.3 %collective-permute-start.6 = (bf16[88,2048]{1,0:T(8,128)(2,1)}, bf16[88,2048]{1,0:T(8,128)(2,1)S(1)}, u32[]{:S(2)}, u32[]{:S(2)}) collective-permute-start(bf16[88,2048]{1,0:T(8,128)(2,1)} %constant_dynamic-slice_fusion.10), channel_id=1, source_target_pairs={{0,1},{1,0},{2,3},{3,2},{4,5},{5,4},{6,7},{7,6},{8,9},{9,8},{10,11... | collective-permute-start | bytes 1081352 | tf_op jit(solution)/shard_map/ppermute | solution.py:84
  103.8 39.0 %collective-permute-start.11 = (bf16[512,1024]{1,0:T(8,128)(2,1)}, bf16[512,1024]{1,0:T(8,128)(2,1)}, u32[]{:S(2)}, u32[]{:S(2)}) collective-permute-start(bf16[512,1024]{1,0:T(8,128)(2,1)} %collective-permute-done.10), channel_id=1, source_target_pairs={{0,2},{1,3},{2,4},{3,5},{4,6},{5,7},{6,0},{7,1},{8,10},{9,11},{10,... | collective-permute-start | bytes 3145736 | tf_op jit(solution)/shard_map/ppermute | solution.py:95
  375.0 44.5 %collective-permute-start.33 = (bf16[256,2048]{1,0:T(8,128)(2,1)}, bf16[256,2048]{1,0:T(8,128)(2,1)}, u32[]{:S(2)}, u32[]{:S(2)}) collective-permute-start(bf16[256,2048]{1,0:T(8,128)(2,1)} %get-tuple-element.329), channel_id=1, source_target_pairs={{0,16},{8,24},{16,0},{24,8},{1,17},{9,25},{17,1},{25,9},{2,18},{10... | collective-permute-start | bytes 3145736 | tf_op jit(solution)/shard_map/ppermute | solution.py:79
  401.3 51.7 %collective-permute-start.42 = (bf16[256,2048]{1,0:T(8,128)(2,1)}, bf16[256,2048]{1,0:T(8,128)(2,1)}, u32[]{:S(2)}, u32[]{:S(2)}) collective-permute-start(bf16[256,2048]{1,0:T(8,128)(2,1)} %get-tuple-element.123), channel_id=1, source_target_pairs={{0,8},{8,0},{16,24},{24,16},{1,9},{9,1},{17,25},{25,17},{2,10},{10... | collective-permute-start | bytes 3145736 | tf_op jit(solution)/shard_map/ppermute | solution.py:74
  459.0 46.7 %collective-permute-start.52 = (bf16[256,2048]{1,0:T(8,128)(2,1)S(1)}, bf16[256,2048]{1,0:T(8,128)(2,1)S(1)}, u32[]{:S(2)}, u32[]{:S(2)}) collective-permute-start(bf16[256,2048]{1,0:T(8,128)(2,1)S(1)} %copy-done.80), channel_id=1, source_target_pairs={{0,16},{8,24},{16,0},{24,8},{1,17},{9,25},{17,1},{25,9},{2,18},{10... | collective-permute-start | bytes 3145736 | tf_op jit(solution)/shard_map/ppermute | solution.py:79
  538.3 56.1 %collective-permute-start.55 = (bf16[256,2048]{1,0:T(8,128)(2,1)}, bf16[256,2048]{1,0:T(8,128)(2,1)}, u32[]{:S(2)}, u32[]{:S(2)}) collective-permute-start(bf16[256,2048]{1,0:T(8,128)(2,1)} %collective-permute-done.54.refs_0_), channel_id=1, source_target_pairs={{0,8},{8,0},{16,24},{24,16},{1,9},{9,1},{17,25},{25,17},{2,10},{10... | collective-permute-start | bytes 3145736 | tf_op jit(solution)/shard_map/ppermute | solution.py:74
  560.6 64.7 %collective-permute-start.67 = (bf16[256,2048]{1,0:T(8,128)(2,1)}, bf16[256,2048]{1,0:T(8,128)(2,1)}, u32[]{:S(2)}, u32[]{:S(2)}) collective-permute-start(bf16[256,2048]{1,0:T(8,128)(2,1)} %collective-permute-done.65.refs_0_), channel_id=1, source_target_pairs={{0,16},{8,24},{16,0},{24,8},{1,17},{9,25},{17,1},{25,9},{2,18},{10... | collective-permute-start | bytes 3145736 | tf_op jit(solution)/shard_map/ppermute | solution.py:79
  561.8 63.7 %collective-permute-start.73 = (bf16[256,2048]{1,0:T(8,128)(2,1)}, bf16[256,2048]{1,0:T(8,128)(2,1)}, u32[]{:S(2)}, u32[]{:S(2)}) collective-permute-start(bf16[256,2048]{1,0:T(8,128)(2,1)} %collective-permute-done.65.refs_0_), channel_id=1, source_target_pairs={{0,2},{1,3},{2,4},{3,5},{4,6},{5,7},{6,0},{7,1},{8,10},{9,11},{10,... | collective-permute-start | bytes 3145736 | tf_op jit(solution)/shard_map/ppermute | solution.py:95
  624.8 37.4 %collective-permute-start.61 = (bf16[256,2176]{1,0:T(8,128)(2,1)}, bf16[256,2176]{1,0:T(8,128)(2,1)}, u32[]{:S(2)}, u32[]{:S(2)}) collective-permute-start(bf16[256,2176]{1,0:T(8,128)(2,1)} %get-tuple-element.143), channel_id=1, source_target_pairs={{0,8},{8,0},{16,24},{24,16},{1,9},{9,1},{17,25},{25,17},{2,10},{10... | collective-permute-start | bytes 3342344 | tf_op jit(solution)/shard_map/ppermute | solution.py:74
  627.5 72.8 %collective-permute-start.63 = (bf16[256,2176]{1,0:T(8,128)(2,1)}, bf16[256,2176]{1,0:T(8,128)(2,1)}, u32[]{:S(2)}, u32[]{:S(2)}) collective-permute-start(bf16[256,2176]{1,0:T(8,128)(2,1)} %get-tuple-element.145), channel_id=1, source_target_pairs={{0,8},{8,0},{16,24},{24,16},{1,9},{9,1},{17,25},{25,17},{2,10},{10... | collective-permute-start | bytes 3342344 | tf_op jit(solution)/shard_map/ppermute | solution.py:74
  629.4 37.6 %collective-permute-start.74 = (bf16[256,2048]{1,0:T(8,128)(2,1)}, bf16[256,2048]{1,0:T(8,128)(2,1)}, u32[]{:S(2)}, u32[]{:S(2)}) collective-permute-start(bf16[256,2048]{1,0:T(8,128)(2,1)} %collective-permute-done.73.refs_0_), channel_id=1, source_target_pairs={{0,8},{8,0},{16,24},{24,16},{1,9},{9,1},{17,25},{25,17},{2,10},{10... | collective-permute-start | bytes 3145736 | tf_op jit(solution)/shard_map/ppermute | solution.py:74
  667.0 115.4 %collective-permute-start.83 = (bf16[256,2176]{1,0:T(8,128)(2,1)}, bf16[256,2176]{1,0:T(8,128)(2,1)}, u32[]{:S(2)}, u32[]{:S(2)}) collective-permute-start(bf16[256,2176]{1,0:T(8,128)(2,1)} %get-tuple-element.163), channel_id=1, source_target_pairs={{0,8},{8,0},{16,24},{24,16},{1,9},{9,1},{17,25},{25,17},{2,10},{10... | collective-permute-start | bytes 3342344 | tf_op jit(solution)/shard_map/ppermute | solution.py:74
  706.9 75.5 %collective-permute-start.82 = (bf16[256,2176]{1,0:T(8,128)(2,1)}, bf16[256,2176]{1,0:T(8,128)(2,1)}, u32[]{:S(2)}, u32[]{:S(2)}) collective-permute-start(bf16[256,2176]{1,0:T(8,128)(2,1)} %add_convert_fusion.1), channel_id=1, source_target_pairs={{0,16},{8,24},{16,0},{24,8},{1,17},{9,25},{17,1},{25,9},{2,18},{10... | collective-permute-start | bytes 3342344 | tf_op jit(solution)/shard_map/ppermute | solution.py:79
  728.3 47.0 %collective-permute-start.78 = (bf16[256,2176]{1,0:T(8,128)(2,1)}, bf16[256,2176]{1,0:T(8,128)(2,1)}, u32[]{:S(2)}, u32[]{:S(2)}) collective-permute-start(bf16[256,2176]{1,0:T(8,128)(2,1)} %add_convert_fusion.3), channel_id=1, source_target_pairs={{0,16},{8,24},{16,0},{24,8},{1,17},{9,25},{17,1},{25,9},{2,18},{10... | collective-permute-start | bytes 3342344 | tf_op jit(solution)/shard_map/ppermute | solution.py:79
  733.8 41.4 %collective-permute-start.72 = (bf16[256,2176]{1,0:T(8,128)(2,1)}, bf16[256,2176]{1,0:T(8,128)(2,1)}, u32[]{:S(2)}, u32[]{:S(2)}) collective-permute-start(bf16[256,2176]{1,0:T(8,128)(2,1)} %add_convert_fusion.4), channel_id=1, source_target_pairs={{0,2},{1,3},{2,4},{3,5},{4,6},{5,7},{6,0},{7,1},{8,10},{9,11},{10,... | collective-permute-start | bytes 3342344 | tf_op jit(solution)/shard_map/ppermute | solution.py:95
  779.6 50.1 %collective-permute-start.92 = (bf16[3,88,2048]{2,1,0:T(8,128)(2,1)S(1)}, bf16[3,88,2048]{2,1,0:T(8,128)(2,1)S(1)}, u32[]{:S(2)}, u32[]{:S(2)}) collective-permute-start(bf16[3,88,2048]{2,1,0:T(8,128)(2,1)S(1)} %fusion.45), channel_id=1, source_target_pairs={{0,1},{1,0},{2,3},{3,2},{4,5},{5,4},{6,7},{7,6},{8,9},{9,8},{10,11... | collective-permute-start | bytes 3244040 | tf_op jit(solution)/shard_map/ppermute | solution.py:84
  841.6 306.4 %all-gather.11.cloned.1.call-start = ((), (), s32[]{:S(2)}) async-start(), calls=%async_computation.6 | async-start | bytes 17301504 | tf_op jit(solution)/shard_map/all_gather | solution.py:90
  918.2 38.3 %collective-permute-start.86 = (bf16[1024,576]{0,1:T(8,128)(2,1)}, bf16[1024,576]{0,1:T(8,128)(2,1)}, u32[]{:S(2)}, u32[]{:S(2)}) collective-permute-start(bf16[1024,576]{0,1:T(8,128)(2,1)} %copy.372), channel_id=1, source_target_pairs={{0,8},{8,0},{16,24},{24,16},{1,9},{9,1},{17,25},{25,17},{2,10},{10... | collective-permute-start | bytes 3538952 | tf_op jit(solution)/shard_map/ppermute | solution.py:74
  948.5 39.5 %collective-permute-start.91 = (bf16[2,3072,128]{2,1,0:T(8,128)(2,1)}, bf16[2,3072,128]{2,1,0:T(8,128)(2,1)}, u32[]{:S(2)}, u32[]{:S(2)}) collective-permute-start(bf16[2,3072,128]{2,1,0:T(8,128)(2,1)} %dynamic-slice_bitcast_fusion.2), channel_id=1, source_target_pairs={{0,2},{1,3},{2,4},{3,5},{4,6},{5,7},{6,0},{7,1},{8,10},{9,11},{10,... | collective-permute-start | bytes 4718600 | tf_op jit(solution)/shard_map/ppermute | solution.py:95
  952.2 181.3 %collective-permute-start.100 = (bf16[88,2048]{1,0:T(8,128)(2,1)}, bf16[88,2048]{1,0:T(8,128)(2,1)}, u32[]{:S(2)}, u32[]{:S(2)}) collective-permute-start(bf16[88,2048]{1,0:T(8,128)(2,1)} %after.29), channel_id=1, source_target_pairs={{0,0},{1,4},{2,8},{3,12},{4,16},{5,20},{6,24},{7,28},{8,1},{9,5},{... | collective-permute-start | bytes 1081352 | tf_op jit(solution)/shard_map/ppermute | solution.py:996
  969.8 70.5 %collective-permute-start.87 = (bf16[256,2048]{1,0:T(8,128)(2,1)}, bf16[256,2048]{1,0:T(8,128)(2,1)}, u32[]{:S(2)}, u32[]{:S(2)}) collective-permute-start(bf16[256,2048]{1,0:T(8,128)(2,1)} %get-tuple-element.301), channel_id=1, source_target_pairs={{0,8},{8,0},{16,24},{24,16},{1,9},{9,1},{17,25},{25,17},{2,10},{10... | collective-permute-start | bytes 3145736 | tf_op jit(solution)/shard_map/ppermute | solution.py:74
  995.1 55.5 %collective-permute-start.93 = (bf16[2,3072,128]{2,1,0:T(8,128)(2,1)}, bf16[2,3072,128]{2,1,0:T(8,128)(2,1)}, u32[]{:S(2)}, u32[]{:S(2)}) collective-permute-start(bf16[2,3072,128]{2,1,0:T(8,128)(2,1)} %convert_element_type.661), channel_id=1, source_target_pairs={{0,2},{1,3},{2,4},{3,5},{4,6},{5,7},{6,0},{7,1},{8,10},{9,11},{10,... | collective-permute-start | bytes 4718600 | tf_op jit(solution)/shard_map/ppermute | solution.py:95
  1027.2 42.9 %collective-permute-start.89 = (bf16[256,2048]{1,0:T(8,128)(2,1)}, bf16[256,2048]{1,0:T(8,128)(2,1)}, u32[]{:S(2)}, u32[]{:S(2)}) collective-permute-start(bf16[256,2048]{1,0:T(8,128)(2,1)} %get-tuple-element.302), channel_id=1, source_target_pairs={{0,8},{8,0},{16,24},{24,16},{1,9},{9,1},{17,25},{25,17},{2,10},{10... | collective-permute-start | bytes 3145736 | tf_op jit(solution)/shard_map/ppermute | solution.py:74
  1054.2 38.7 %collective-permute-start.94 = (bf16[2,3072,128]{2,1,0:T(8,128)(2,1)}, bf16[2,3072,128]{2,1,0:T(8,128)(2,1)}, u32[]{:S(2)}, u32[]{:S(2)}) collective-permute-start(bf16[2,3072,128]{2,1,0:T(8,128)(2,1)} %fusion.6), channel_id=1, source_target_pairs={{0,2},{1,3},{2,4},{3,5},{4,6},{5,7},{6,0},{7,1},{8,10},{9,11},{10,... | collective-permute-start | bytes 4718600 | tf_op jit(solution)/shard_map/ppermute | solution.py:95
  1076.8 42.3 %all-to-all-start.1 = ((f32[32,1,1169]{2,1,0:T(1,128)}), f32[32,1,1169]{2,1,0:T(1,128)S(1)}, u32[]{:S(2)}, u32[]{:S(2)}) async-start(f32[32,1,1169]{2,1,0:T(1,128)} %copy.376), calls=%async_computation.1 | async-start | bytes 327680 | tf_op jit(solution)/shard_map/all_to_all | solution.py:204
  (212 other events, 3125.5 us)
Sparse Core Ops, SparseCore 0:
  51.9 222.1 all-gather.6
  741.6 99.6 all-gather.8
  856.3 143.8 all-gather.10
